TPU v7x, 32 devices: a whole 2x2x4 slice. The times are simulated.
32 devices in a mesh: groups: 2 (over x), band: 16 (over z, y, core).
Axes of the slice: x: 2, y: 2, z: 4, core: 2. Of those that a mesh axis runs over, the one named last changes fastest.
Arguments:
- orbitals: float32 [32, 96, 9216], P(('groups', 'band')), parts along dimension 0, may hold values from -6 to 6
Outputs:
- exchange_term: float32 [32, 96, 9216], P(('groups', 'band')), parts along dimension 0
There are 2 independent parts, one for each index of `groups`. A program takes and returns all parts, laid end to end along the dimension named above; each array names one. Nothing has to cross between parts.
All inputs are finite; a program needn't handle non-finite values.
Results may differ from a plain program's by a relative error of at most 0.0003.
Values sent between devices are 32-bit elements; how exact they have to be, the bound alone decides.
No kernel may reach another device: no remote copies, remote signals or barrier semaphores. Data moves between devices by JAX's collectives and lax.ppermute only.
A program may use at most 128 MiB of HBM per device.

v0:
```python
import functools
import math

import jax
import jax.numpy as jnp
import numpy as np
from jax import lax
from jax.experimental import pallas as pl
from jax.experimental.pallas import tpu as pltpu
from jax.sharding import PartitionSpec as P

OFFSET = 5
screening = 5.44
LANES = 128
X_STEPS = 3
PLANE_STEPS = 2
SETTLE_STEPS = 6
FAR_ROWS = 40


def from_behind(value, axis, by):
    count = lax.axis_size(axis)
    return lax.ppermute(value, axis, [(i, (i + by) % count) for i in range(count)])


def screened_kernel(points):
    signed = jnp.arange(LANES, dtype=jnp.int32)
    inside = signed < points
    signed = jnp.where(signed >= points // 2, signed - points, signed)
    wavenumber = signed.astype(jnp.float32) * (2.0 * math.pi / points)
    squared = (
        wavenumber[:points, None, None] ** 2
        + wavenumber[None, :points, None] ** 2
        + wavenumber[None, None, :] ** 2
    )
    screen_rate = screening / points
    finite = jnp.where(squared > 0.0, squared, 1.0)
    screened = 4.0 * math.pi / finite * -jnp.expm1(-finite / (4.0 * screen_rate * screen_rate))
    kernel = jnp.where(squared > 0.0, screened, math.pi / (screen_rate * screen_rate))
    return jnp.where(inside, kernel / float(points * points * points), 0.0)


def hartley_tables(points):
    counter = np.arange(points)
    angles = 2.0 * np.pi * (counter[:, None] * counter[None, :] % points) / points
    table = np.cos(angles) + np.sin(angles)
    high = table.astype(jnp.bfloat16)
    low = (table - high.astype(np.float64)).astype(jnp.bfloat16)
    left = np.zeros((2 * points, 2 * points), jnp.bfloat16)
    left[:points, :points] = high
    left[:points, points:] = high
    left[points:, :points] = low
    right = np.zeros((2 * LANES, 2 * LANES), jnp.bfloat16)
    right[:points, :points] = high
    right[:points, LANES:LANES + points] = low
    right[LANES:LANES + points, :points] = high
    return jnp.asarray(left), jnp.asarray(right)


def two_terms(value):
    high = value.astype(jnp.bfloat16)
    low = (value - high.astype(jnp.float32)).astype(jnp.bfloat16)
    return high, low


def from_left(left, value):
    half = value.shape[0]
    terms = jnp.concatenate(two_terms(value), 0)
    out = jnp.dot(left, terms, preferred_element_type=jnp.float32)
    return out[:half] + out[half:]


def from_right(value, right):
    out = jnp.dot(jnp.concatenate(two_terms(value), 1), right, preferred_element_type=jnp.float32)
    return out[:, :LANES] + out[:, LANES:]


def pair_body(points, slot, has, *refs):
    refs = list(refs)
    flags_ref = refs.pop(0)
    names = ["a", "b"] + [name for name in ("sum_a", "sum_b") if name in has]
    far = {name: refs.pop(0) for name in names}
    if "then" in has:
        refs.pop(0)
    kernel_ref, left_ref, right_ref = refs.pop(0), refs.pop(0), refs.pop(0)
    out_refs = {"for_a": refs.pop(0)}
    if "halves" in has:
        out_refs["low_a"] = refs.pop(0)
    if "for_b" in has:
        out_refs["for_b"] = refs.pop(0)
    if "hand_on" in has:
        refs.pop(0)
    held, near, near_kernel, near_out, sems, kernel_sems, out_sems = refs
    outs = list(out_refs)
    step = pl.program_id(0)
    active = flags_ref[2 * slot] == 1
    with_sum = flags_ref[2 * slot + 1] == 1
    columns = near.shape[2] // X_STEPS
    ys = columns // points
    per_step = points // PLANE_STEPS
    late = X_STEPS + PLANE_STEPS

    def span_of(chunk):
        start = chunk * columns
        return pl.ds(start if isinstance(chunk, int) else pl.multiple_of(start, columns), columns)

    def fetch(name, chunk):
        place, span = names.index(name), span_of(chunk)
        return pltpu.make_async_copy(
            far[name].at[:, span], near.at[place, :, span], sems.at[place, chunk]
        )

    def fetch_kernel(part):
        span = pl.ds(part * per_step, per_step)
        return pltpu.make_async_copy(
            kernel_ref.at[span], near_kernel.at[span], kernel_sems.at[part]
        )

    def give(name, chunk):
        span = span_of(chunk)
        source = near_out.at[0 if name != "for_b" else 1]
        if "halves" in has and name != "for_b":
            rows = pl.ds(points - FAR_ROWS, FAR_ROWS) if name == "low_a" else pl.ds(0, points - FAR_ROWS)
            source = source.at[rows, span]
        else:
            source = source.at[:, span]
        return pltpu.make_async_copy(
            source, out_refs[name].at[:, span], out_sems.at[outs.index(name), chunk]
        )

    def here(name, chunk):
        return near[names.index(name), :, span_of(chunk)]

    sums = [name for name in names if name.startswith("sum")]

    @pl.when(active & (step == 0))
    def start_first():
        for chunk in range(2):
            for name in ("a", "b"):
                fetch(name, chunk).start()

    @pl.when(active & (step + 2 < X_STEPS))
    def start_next():
        for name in ("a", "b"):
            fetch(name, step + 2).start()

    @pl.when(active & (step == X_STEPS - 2))
    def start_kernel():
        for part in range(PLANE_STEPS):
            fetch_kernel(part).start()

    if sums:
        @pl.when(active & (step == X_STEPS))
        def start_sums():
            for chunk in range(X_STEPS):
                for name in sums:
                    fetch(name, chunk).start()

    def lanes_apart(block):
        gap = jnp.zeros((points, LANES - points), jnp.float32)
        rows = [
            jnp.concatenate([block[:, q * points:(q + 1) * points], gap], 1) for q in range(ys)
        ]
        return jnp.swapaxes(jnp.stack(rows, 0), 0, 1)

    def lanes_together(block):
        block = jnp.swapaxes(block, 0, 1)
        return jnp.concatenate([block[q][:, :points] for q in range(ys)], 1)

    def side_by_side(block):
        return jnp.concatenate([block[i] for i in range(per_step)], 1)

    @pl.when(active & (step < X_STEPS))
    def forward_x():
        for name in ("a", "b"):
            fetch(name, step).wait()
        spectrum = from_left(left_ref[...], here("a", step) * here("b", step))
        start = pl.multiple_of(step * ys, ys)
        held[:, pl.ds(start, ys), :] = lanes_apart(spectrum)

    @pl.when(active & (step >= X_STEPS) & (step < late))
    def planes():
        left = left_ref[...]
        right = right_ref[...]
        part = step - X_STEPS
        first = part * per_step
        block = held[pl.ds(first, per_step)].reshape(per_step * points, LANES)
        block = from_right(block, right).reshape(per_step, points, LANES)
        wide = from_left(left, side_by_side(block))
        fetch_kernel(part).wait()
        wide = from_left(left, wide * side_by_side(near_kernel[pl.ds(first, per_step)]))
        block = jnp.concatenate(
            [wide[:, i * LANES:(i + 1) * LANES] for i in range(per_step)], 0
        )
        block = from_right(block, right)
        held[pl.ds(first, per_step)] = block.reshape(per_step, points, LANES)

    @pl.when(active & (step >= late))
    def inverse_x():
        chunk = step - late
        start = pl.multiple_of(chunk * ys, ys)
        for name in sums:
            fetch(name, chunk).wait()
        block = lanes_together(held[:, pl.ds(start, ys), :])
        potential = from_left(left_ref[...], block)
        for_a = -(here("b", chunk) * potential)
        if "sum_a" in has:
            for_a = for_a + jnp.where(with_sum, here("sum_a", chunk), 0.0)
        near_out[0, :, span_of(chunk)] = for_a
        if "for_b" in has:
            for_b = -(here("a", chunk) * potential)
            if "sum_b" in has:
                for_b = for_b + here("sum_b", chunk)
            near_out[1, :, span_of(chunk)] = for_b
        for name in outs:
            give(name, chunk).start()

    @pl.when(active & (step == late + X_STEPS - 1))
    def wait_outs():
        for chunk in range(X_STEPS):
            for name in outs:
                give(name, chunk).wait()


def pair_terms(
    flags, slot, a, b, constants, sum_a=None, sum_b=None, for_b=False, halves=False, in_place=False, then=None, hand_on=False
):
    points, plane = a.shape
    kernel, left, right = constants
    optional = {"sum_a": sum_a, "sum_b": sum_b}
    optional = {name: value for name, value in optional.items() if value is not None}
    blocks = [a, b, *optional.values()]
    waited = [] if then is None else [then]
    has = list(optional) + ["for_b"] * for_b + ["halves"] * halves + ["then"] * len(waited)
    has += ["hand_on"] * hand_on
    rows = ([points - FAR_ROWS, FAR_ROWS] if halves else [points]) + [points] * for_b
    aliases = {3: 0} if in_place else {}
    if hand_on:
        aliases[1] = len(rows)
    anywhere = pl.BlockSpec(memory_space=pl.ANY)
    out = pl.pallas_call(
        functools.partial(pair_body, points, slot, has),
        grid=(2 * X_STEPS + PLANE_STEPS,),
        in_specs=[pl.BlockSpec(memory_space=pltpu.SMEM)]
        + [anywhere] * (len(blocks) + len(waited) + 1)
        + [pl.BlockSpec(table.shape, lambda i: (0, 0)) for table in (left, right)],
        out_specs=[anywhere] * (len(rows) + hand_on),
        out_shape=[
            jax.ShapeDtypeStruct((n, plane), jnp.float32) for n in rows + [points] * hand_on
        ],
        input_output_aliases=aliases,
        scratch_shapes=[
            pltpu.VMEM((points, points, LANES), jnp.float32),
            pltpu.VMEM((len(blocks), points, plane), jnp.float32),
            pltpu.VMEM((points, points, LANES), jnp.float32),
            pltpu.VMEM((2 if for_b else 1, points, plane), jnp.float32),
            pltpu.SemaphoreType.DMA((len(blocks), X_STEPS)),
            pltpu.SemaphoreType.DMA((PLANE_STEPS,)),
            pltpu.SemaphoreType.DMA((len(rows), X_STEPS)),
        ],
        compiler_params=pltpu.CompilerParams(vmem_limit_bytes=62 * 2**20),
        cost_estimate=pl.CostEstimate(
            flops=100_000_000, bytes_accessed=1_000_000, transcendentals=0
        ),
        name="pair_terms",
    )(flags, *blocks, *waited, kernel, left, right)
    return out if len(out) > 1 else out[0]


def copy_body(flags_ref, block_ref, new_block_ref):
    new_block_ref[...] = block_ref[...]


def copied(flags, block):
    points, plane = block.shape
    part = pl.BlockSpec((points, plane // X_STEPS), lambda i: (0, i))
    return pl.pallas_call(
        copy_body,
        grid=(X_STEPS,),
        in_specs=[pl.BlockSpec(memory_space=pltpu.SMEM), part],
        out_specs=part,
        out_shape=jax.ShapeDtypeStruct(block.shape, block.dtype),
        compiler_params=pltpu.CompilerParams(vmem_limit_bytes=62 * 2**20),
        name="copied",
    )(flags, block)


def gate_body(token_ref, left_ref, partner_ref, block_ref, new_left_ref, new_block_ref):
    del token_ref, partner_ref, block_ref, new_block_ref
    new_left_ref[...] = left_ref[...]


def gate(token, left, partner, block):
    in_vmem = pl.BlockSpec(memory_space=pltpu.VMEM)
    anywhere = pl.BlockSpec(memory_space=pl.ANY)
    return pl.pallas_call(
        gate_body,
        in_specs=[in_vmem, in_vmem, anywhere, anywhere],
        out_specs=[in_vmem, anywhere],
        out_shape=[
            jax.ShapeDtypeStruct(left.shape, left.dtype),
            jax.ShapeDtypeStruct(block.shape, block.dtype),
        ],
        input_output_aliases={3: 1},
        compiler_params=pltpu.CompilerParams(vmem_limit_bytes=62 * 2**20),
        name="gate",
    )(token, left, partner, block)


def hold_body(*refs):
    del refs


def hold(block, *then):
    anywhere = pl.BlockSpec(memory_space=pl.ANY)
    return pl.pallas_call(
        hold_body,
        in_specs=[anywhere] * (1 + len(then)),
        out_specs=anywhere,
        out_shape=jax.ShapeDtypeStruct(block.shape, block.dtype),
        input_output_aliases={0: 0},
        compiler_params=pltpu.CompilerParams(vmem_limit_bytes=62 * 2**20),
        name="hold",
    )(block, *then)


def settle_body(flags_ref, home_ref, top_ref, bottom_ref, own_ref, out_ref, near, sems):
    del own_ref
    columns = out_ref.shape[1] // SETTLE_STEPS
    split = top_ref.shape[0]

    def move(parts):
        copies = []
        for i in range(SETTLE_STEPS):
            span = pl.ds(i * columns, columns)
            for j, (source_ref, start) in enumerate(parts):
                rows = pl.ds(start, source_ref.shape[0])
                copies.append((
                    pltpu.make_async_copy(
                        source_ref.at[:, span], near.at[rows, span], sems.at[0, j, i]
                    ),
                    pltpu.make_async_copy(
                        near.at[rows, span], out_ref.at[rows, span], sems.at[1, j, i]
                    ),
                ))
        for inward, outward in copies:
            inward.start()
        for inward, outward in copies:
            inward.wait()
            outward.start()
        for inward, outward in copies:
            outward.wait()

    @pl.when(flags_ref[RESULT] == 1)
    def from_home():
        move([(home_ref, 0)])

    @pl.when(flags_ref[RESULT] == 2)
    def from_far():
        move([(top_ref, 0), (bottom_ref, split)])


def settle(flags, home, top, bottom, own_sum):
    anywhere = pl.BlockSpec(memory_space=pl.ANY)
    return pl.pallas_call(
        settle_body,
        in_specs=[pl.BlockSpec(memory_space=pltpu.SMEM)] + [anywhere] * 4,
        out_specs=anywhere,
        out_shape=jax.ShapeDtypeStruct(own_sum.shape, own_sum.dtype),
        input_output_aliases={4: 0},
        scratch_shapes=[
            pltpu.VMEM(own_sum.shape, own_sum.dtype),
            pltpu.SemaphoreType.DMA((2, 2, SETTLE_STEPS)),
        ],
        compiler_params=pltpu.CompilerParams(vmem_limit_bytes=62 * 2**20),
        name="settle",
    )(flags, home, top, bottom, own_sum)


def both_halves(*pairs):
    return list(pairs) + [(15 - source, 15 - target) for source, target in pairs]


CROSSING = both_halves((3, 14), (4, 9))
PARTNERS = both_halves((8, 14), (15, 9), (9, 11), (14, 12))
ARRIVED = both_halves((14, 2), (9, 5))
SINGLES = both_halves((5, 10), (2, 13))
BESIDE = both_halves((13, 14), (10, 9))
DIRECT = both_halves((15, 10), (8, 13))
TURNED = both_halves((11, 14), (12, 9))
HOME_ACROSS = both_halves((9, 4), (14, 3))
HOME_FAR = both_halves((9, 15), (14, 8))
HOME_TURN = both_halves((9, 11), (14, 12))
HOME_TURNED = both_halves((11, 15), (12, 8))
RESULT = 12
FLAGS = {i: (1, 0, 1, 0, 1, 1, 0, 0, 0, 0, 1, 1, 0) for i in (9, 14, 6, 1)}
FLAGS.update({i: (0, 0, 0, 0, 0, 0, 1, 0, 1, 1, 0, 0, 0) for i in (10, 13, 5, 2)})
FLAGS.update({i: (0,) * RESULT + (1,) for i in (3, 4, 11, 12)})
FLAGS.update({i: (0,) * RESULT + (2,) for i in (15, 8, 0, 7)})


def sixteen_bands(orbitals, constants):
    def send(value, pairs):
        return lax.ppermute(value[None], "band", pairs)[0]

    kernel, left, right = constants
    own = orbitals[0]
    flags = jnp.asarray([FLAGS[i] for i in range(16)], jnp.int32)
    flags = flags[lax.axis_index("band")]
    pair = functools.partial(pair_terms, flags)
    crossed = send(own, CROSSING)
    partner = send(own, PARTNERS)
    own_copy = copied(flags, own)
    token = crossed[:8, :LANES] + kernel[0, :8] + own_copy[:8, :LANES]
    left, held_back = gate(send(token, ARRIVED), left, partner, own_copy)
    constants = (kernel, left, right)
    beside = send(held_back, BESIDE)
    single = send(held_back, SINGLES)
    direct = send(held_back, DIRECT)

    partner_sum, crossed_sum = pair(0, partner, crossed, constants, for_b=True)
    own_sum, crossed_sum = pair(1, own, crossed, constants, sum_b=crossed_sum, for_b=True)
    home = send(crossed_sum, HOME_ACROSS)
    partner = hold(partner, own_sum, beside)
    turned = send(partner, TURNED)
    top, bottom = pair(2, partner, beside, constants, sum_a=partner_sum, halves=True)
    bottom = send(bottom, HOME_TURN)
    top = send(top, HOME_FAR)
    bottom = send(bottom, HOME_TURNED)
    own_sum = pair(3, own, single, constants, sum_a=own_sum, in_place=True)
    own_sum = pair(4, own, direct, constants, sum_a=own_sum, in_place=True, then=home)
    own_sum = pair(5, own, turned, constants, sum_a=own_sum, in_place=True)
    return settle(flags, home, top, bottom, own_sum)[None]


def any_bands(orbitals, constants):
    own = orbitals[0]
    flags = jnp.ones((4,), jnp.int32)
    lower = from_behind(orbitals, "band", OFFSET)[0]
    upper = from_behind(orbitals, "band", -OFFSET)[0]
    total = pair_terms(flags, 0, own, lower, constants)
    return pair_terms(flags, 1, own, upper, constants, sum_a=total)[None]


def local(bands, orbitals):
    points = orbitals.shape[1]
    constants = (screened_kernel(points), *hartley_tables(points))
    if bands == 16:
        return sixteen_bands(orbitals, constants)
    return any_bands(orbitals, constants)


def solution(mesh):
    return jax.shard_map(
        functools.partial(local, mesh.shape["band"]),
        mesh=mesh,
        in_specs=(P(("groups", "band"), None, None),),
        out_specs=P(("groups", "band"), None, None),
        check_vma=False,
    )
```

profile of v0, /device:TPU:0, one launch (start us, length us, event | category | flops | bytes accessed | tf_op | source)
XLA Modules:
  0.0 177.1 jit_solution(6793140776483314323)
XLA Ops:
  0.0 2.4 %collective-permute-start = (f32[1,96,9216]{2,1,0:T(8,128)}, f32[1,96,9216]{2,1,0:T(8,128)}, u32[]{:S(2)}, u32[]{:S(2)}) collective-permute-start(f32[1,96,9216]{2,1,0:T(8,128)} %param.4), channel_id=1, source_target_pairs={{3,14},{4,9},{12,1},{11,6},{19,30},{20,25},{28,17},{27,22}} | collective-permute-start | bytes 10616840 | tf_op jit(solution)/shard_map/ppermute | solution.py:404
  2.4 6.6 %collective-permute-start.1 = (f32[1,96,9216]{2,1,0:T(8,128)}, f32[1,96,9216]{2,1,0:T(8,128)}, u32[]{:S(2)}, u32[]{:S(2)}) collective-permute-start(f32[1,96,9216]{2,1,0:T(8,128)} %param.4), channel_id=1, source_target_pairs={{8,14},{15,9},{9,11},{14,12},{7,1},{0,6},{6,4},{1,3},{24,30},{31,2... | collective-permute-start | bytes 10616840 | tf_op jit(solution)/shard_map/ppermute | solution.py:404
  9.0 1.3 dynamic-slice_bitcast_fusion.flags_ref.refs_0_
  10.3 4.7 %copied.1.block_ref = f32[96,9216]{1,0:T(8,128)} custom-call(s32[13]{0:T(128)} %dynamic-slice_bitcast_fusion.flags_ref.refs_0_, f32[96,9216]{1,0:T(8,128)} %bitcast.27), custom_call_target="tpu_custom_call" | custom-call | tf_op jit(solution)/shard_map/copied/pallas_call | solution.py:277
  15.0 0.1 broadcast_add_fusion
  15.1 3.1 %fusion.5.refs_3_.refs_4_.refs_5_ = f32[96,96,128]{2,1,0:T(8,128)S(1)} fusion(f32[128]{0:T(128)S(1)} %fusion.13, f32[96,96]{1,0:T(8,128)S(1)} %broadcast_add_fusion, pred[128]{0:T(512)(128)(4,1)S(1)} %iota_compare_fusion), kind=kLoop, calls=%fused_computation.7 | loop fusion | flops 12976128 | bytes 4756096 | tf_op jit(solution)/shard_map/jit(_where)/select_n | solution.py:40
  18.2 0.0 copy-start
  18.2 0.0 collective-permute-done
  18.2 2.1 %copy-done = f32[96,96,128]{2,1,0:T(8,128)} copy-done((f32[96,96,128]{2,1,0:T(8,128)}, f32[96,96,128]{2,1,0:T(8,128)S(1)}, u32[]{:S(2)}) %copy-start) | copy-done | bytes 4718616
  20.3 0.7 fusion.9
  21.0 0.6 collective-permute-start.2
  21.6 24.8 %collective-permute-done.1 = f32[1,96,9216]{2,1,0:T(8,128)} collective-permute-done((f32[1,96,9216]{2,1,0:T(8,128)}, f32[1,96,9216]{2,1,0:T(8,128)}, u32[]{:S(2)}, u32[]{:S(2)}) %collective-permute-start.1) | collective-permute-done | bytes 3538976 | tf_op jit(solution)/shard_map/ppermute | solution.py:404
  46.5 0.0 collective-permute-done.2
  46.5 0.0 copy-start.2
  46.5 0.6 copy-done.2
  47.1 1.6 gate.1
  48.6 2.5 %collective-permute-start.4 = (f32[1,96,9216]{2,1,0:T(8,128)}, f32[1,96,9216]{2,1,0:T(8,128)}, u32[]{:S(2)}, u32[]{:S(2)}) collective-permute-start(f32[1,96,9216]{2,1,0:T(8,128)} %bitcast.32), channel_id=1, source_target_pairs={{13,14},{10,9},{2,1},{5,6},{29,30},{26,25},{18,17},{21,22}} | collective-permute-start | bytes 10616840 | tf_op jit(solution)/shard_map/ppermute | solution.py:404
  51.1 2.5 %collective-permute-start.10 = (f32[1,96,9216]{2,1,0:T(8,128)}, f32[1,96,9216]{2,1,0:T(8,128)}, u32[]{:S(2)}, u32[]{:S(2)}) collective-permute-start(f32[1,96,9216]{2,1,0:T(8,128)} %bitcast.33), channel_id=1, source_target_pairs={{5,10},{2,13},{10,5},{13,2},{21,26},{18,29},{26,21},{29,18}} | collective-permute-start | bytes 10616840 | tf_op jit(solution)/shard_map/ppermute | solution.py:404
  53.6 1.5 pair_terms.6
  55.1 1.6 pair_terms.7
  56.7 2.5 %collective-permute-start.3 = (f32[1,96,9216]{2,1,0:T(8,128)}, f32[1,96,9216]{2,1,0:T(8,128)}, u32[]{:S(2)}, u32[]{:S(2)}) collective-permute-start(f32[1,96,9216]{2,1,0:T(8,128)} %bitcast.37), channel_id=1, source_target_pairs={{9,4},{14,3},{6,11},{1,12},{25,20},{30,19},{22,27},{17,28}} | collective-permute-start | bytes 10616840 | tf_op jit(solution)/shard_map/ppermute | solution.py:404
  59.2 9.7 %collective-permute-start.9 = (f32[1,96,9216]{2,1,0:T(8,128)}, f32[1,96,9216]{2,1,0:T(8,128)}, u32[]{:S(2)}, u32[]{:S(2)}) collective-permute-start(f32[1,96,9216]{2,1,0:T(8,128)} %bitcast.34), channel_id=1, source_target_pairs={{15,10},{8,13},{0,5},{7,2},{31,26},{24,29},{16,21},{23,18}} | collective-permute-start | bytes 10616840 | tf_op jit(solution)/shard_map/ppermute | solution.py:404
  68.8 0.0 collective-permute-done.4
  68.8 2.5 %collective-permute-start.8 = (f32[1,96,9216]{2,1,0:T(8,128)}, f32[1,96,9216]{2,1,0:T(8,128)}, u32[]{:S(2)}, u32[]{:S(2)}) collective-permute-start(f32[1,96,9216]{2,1,0:T(8,128)} %bitcast.15), channel_id=1, source_target_pairs={{11,14},{12,9},{4,1},{3,6},{27,30},{28,25},{20,17},{19,22}} | collective-permute-start | bytes 10616840 | tf_op jit(solution)/shard_map/ppermute | solution.py:404
  71.3 1.6 pair_terms.8
  72.9 1.9 %collective-permute-start.6 = (f32[1,40,9216]{2,1,0:T(8,128)}, f32[1,40,9216]{2,1,0:T(8,128)}, u32[]{:S(2)}, u32[]{:S(2)}) collective-permute-start(f32[1,40,9216]{2,1,0:T(8,128)} %bitcast.39), channel_id=1, source_target_pairs={{9,11},{14,12},{6,4},{1,3},{25,27},{30,28},{22,20},{17,19}} | collective-permute-start | bytes 4423688 | tf_op jit(solution)/shard_map/ppermute | solution.py:404
  74.8 0.0 collective-permute-done.10
  74.8 1.3 collective-permute-start.5
  76.1 0.0 collective-permute-done.6
  76.1 1.3 collective-permute-start.7
  77.4 1.6 pair_terms.9.refs_3_
  78.9 0.0 collective-permute-done.3
  79.0 43.5 %collective-permute-done.9 = f32[1,96,9216]{2,1,0:T(8,128)} collective-permute-done((f32[1,96,9216]{2,1,0:T(8,128)}, f32[1,96,9216]{2,1,0:T(8,128)}, u32[]{:S(2)}, u32[]{:S(2)}) %collective-permute-start.9) | collective-permute-done | bytes 3538976 | tf_op jit(solution)/shard_map/ppermute | solution.py:404
  122.4 1.5 pair_terms.10.refs_3_
  124.0 0.0 collective-permute-done.8
  124.0 1.8 %pair_terms.11.own_ref = f32[96,9216]{1,0:T(8,128)} custom-call(s32[13]{0:T(128)} %dynamic-slice_bitcast_fusion.flags_ref.refs_0_, f32[96,9216]{1,0:T(8,128)} %bitcast.31, f32[96,9216]{1,0:T(8,128)} %bitcast.16.refs_2_, f32[96,9216]{1,0:T(8,128)} %pair_terms.10.refs_3_, f32[96,96,128]{2,1,0:T(8,128)} %copy-done, ...), custom_call_target="tpu_custom_call", output_to_operand_aliasing={{}: (3, {})} | custom-call | flops 100000000 | bytes 1000000 | tf_op jit(solution)/shard_map/pair_terms/pallas_call | solution.py:241
  125.7 46.2 %collective-permute-done.5 = f32[1,56,9216]{2,1,0:T(8,128)} collective-permute-done((f32[1,56,9216]{2,1,0:T(8,128)}, f32[1,56,9216]{2,1,0:T(8,128)}, u32[]{:S(2)}, u32[]{:S(2)}) %collective-permute-start.5) | collective-permute-done | bytes 2064416 | tf_op jit(solution)/shard_map/ppermute | solution.py:404
  171.9 0.0 collective-permute-done.7
  171.9 0.0 copy-start.1
  171.9 1.1 copy-done.1
  173.0 3.9 %settle.1 = f32[96,9216]{1,0:T(8,128)} custom-call(s32[13]{0:T(128)} %dynamic-slice_bitcast_fusion.flags_ref.refs_0_, f32[96,9216]{1,0:T(8,128)} %bitcast.8.refs_4_.home_ref, f32[56,9216]{1,0:T(8,128)} %bitcast.12.top_ref, f32[40,9216]{1,0:T(8,128)} %bitcast.35, f32[96,9216]{1,0:T(8,128)} %pair_terms.11.own_ref), custom_call_target="tpu_custom_call", output_to_operand_aliasing={{}: (4, {})} | custom-call | tf_op jit(solution)/shard_map/settle/pallas_call | solution.py:365
  (5 shorter events, 0.0 us)
Async XLA Ops:
  0.0 18.2 %collective-permute-start = (f32[1,96,9216]{2,1,0:T(8,128)}, f32[1,96,9216]{2,1,0:T(8,128)}, u32[]{:S(2)}, u32[]{:S(2)}) collective-permute-start(f32[1,96,9216]{2,1,0:T(8,128)} %param.4), channel_id=1, source_target_pairs={{3,14},{4,9},{12,1},{11,6},{19,30},{20,25},{28,17},{27,22}} | collective-permute-start | bytes 10616840 | tf_op jit(solution)/shard_map/ppermute | solution.py:404
  2.4 44.0 %collective-permute-start.1 = (f32[1,96,9216]{2,1,0:T(8,128)}, f32[1,96,9216]{2,1,0:T(8,128)}, u32[]{:S(2)}, u32[]{:S(2)}) collective-permute-start(f32[1,96,9216]{2,1,0:T(8,128)} %param.4), channel_id=1, source_target_pairs={{8,14},{15,9},{9,11},{14,12},{7,1},{0,6},{6,4},{1,3},{24,30},{31,2... | collective-permute-start | bytes 10616840 | tf_op jit(solution)/shard_map/ppermute | solution.py:404
  18.2 2.1 %copy-start = (f32[96,96,128]{2,1,0:T(8,128)}, f32[96,96,128]{2,1,0:T(8,128)S(1)}, u32[]{:S(2)}) copy-start(f32[96,96,128]{2,1,0:T(8,128)S(1)} %fusion.5.refs_3_.refs_4_.refs_5_) | copy-start | bytes 14155780
  21.0 25.5 %collective-permute-start.2 = (f32[1,8,128]{2,1,0:T(8,128)S(1)}, f32[1,8,128]{2,1,0:T(8,128)S(1)}, u32[]{:S(2)}, u32[]{:S(2)}) collective-permute-start(f32[1,8,128]{2,1,0:T(8,128)S(1)} %fusion.9), channel_id=1, source_target_pairs={{14,2},{9,5},{1,13},{6,10},{30,18},{25,21},{17,29},{22,26}} | collective-permute-start | bytes 12296 | tf_op jit(solution)/shard_map/ppermute | solution.py:404
  46.5 0.6 copy-start.2
  48.6 20.2 %collective-permute-start.4 = (f32[1,96,9216]{2,1,0:T(8,128)}, f32[1,96,9216]{2,1,0:T(8,128)}, u32[]{:S(2)}, u32[]{:S(2)}) collective-permute-start(f32[1,96,9216]{2,1,0:T(8,128)} %bitcast.32), channel_id=1, source_target_pairs={{13,14},{10,9},{2,1},{5,6},{29,30},{26,25},{18,17},{21,22}} | collective-permute-start | bytes 10616840 | tf_op jit(solution)/shard_map/ppermute | solution.py:404
  51.1 23.7 %collective-permute-start.10 = (f32[1,96,9216]{2,1,0:T(8,128)}, f32[1,96,9216]{2,1,0:T(8,128)}, u32[]{:S(2)}, u32[]{:S(2)}) collective-permute-start(f32[1,96,9216]{2,1,0:T(8,128)} %bitcast.33), channel_id=1, source_target_pairs={{5,10},{2,13},{10,5},{13,2},{21,26},{18,29},{26,21},{29,18}} | collective-permute-start | bytes 10616840 | tf_op jit(solution)/shard_map/ppermute | solution.py:404
  56.7 22.2 %collective-permute-start.3 = (f32[1,96,9216]{2,1,0:T(8,128)}, f32[1,96,9216]{2,1,0:T(8,128)}, u32[]{:S(2)}, u32[]{:S(2)}) collective-permute-start(f32[1,96,9216]{2,1,0:T(8,128)} %bitcast.37), channel_id=1, source_target_pairs={{9,4},{14,3},{6,11},{1,12},{25,20},{30,19},{22,27},{17,28}} | collective-permute-start | bytes 10616840 | tf_op jit(solution)/shard_map/ppermute | solution.py:404
  59.2 63.2 %collective-permute-start.9 = (f32[1,96,9216]{2,1,0:T(8,128)}, f32[1,96,9216]{2,1,0:T(8,128)}, u32[]{:S(2)}, u32[]{:S(2)}) collective-permute-start(f32[1,96,9216]{2,1,0:T(8,128)} %bitcast.34), channel_id=1, source_target_pairs={{15,10},{8,13},{0,5},{7,2},{31,26},{24,29},{16,21},{23,18}} | collective-permute-start | bytes 10616840 | tf_op jit(solution)/shard_map/ppermute | solution.py:404
  68.8 55.1 %collective-permute-start.8 = (f32[1,96,9216]{2,1,0:T(8,128)}, f32[1,96,9216]{2,1,0:T(8,128)}, u32[]{:S(2)}, u32[]{:S(2)}) collective-permute-start(f32[1,96,9216]{2,1,0:T(8,128)} %bitcast.15), channel_id=1, source_target_pairs={{11,14},{12,9},{4,1},{3,6},{27,30},{28,25},{20,17},{19,22}} | collective-permute-start | bytes 10616840 | tf_op jit(solution)/shard_map/ppermute | solution.py:404
  72.9 3.2 %collective-permute-start.6 = (f32[1,40,9216]{2,1,0:T(8,128)}, f32[1,40,9216]{2,1,0:T(8,128)}, u32[]{:S(2)}, u32[]{:S(2)}) collective-permute-start(f32[1,40,9216]{2,1,0:T(8,128)} %bitcast.39), channel_id=1, source_target_pairs={{9,11},{14,12},{6,4},{1,3},{25,27},{30,28},{22,20},{17,19}} | collective-permute-start | bytes 4423688 | tf_op jit(solution)/shard_map/ppermute | solution.py:404
  74.8 97.1 %collective-permute-start.5 = (f32[1,56,9216]{2,1,0:T(8,128)}, f32[1,56,9216]{2,1,0:T(8,128)}, u32[]{:S(2)}, u32[]{:S(2)}) collective-permute-start(f32[1,56,9216]{2,1,0:T(8,128)} %bitcast.38), channel_id=1, source_target_pairs={{9,15},{14,8},{6,0},{1,7},{25,31},{30,24},{22,16},{17,23}} | collective-permute-start | bytes 6193160 | tf_op jit(solution)/shard_map/ppermute | solution.py:404
  76.1 95.8 %collective-permute-start.7 = (f32[1,40,9216]{2,1,0:T(8,128)}, f32[1,40,9216]{2,1,0:T(8,128)S(1)}, u32[]{:S(2)}, u32[]{:S(2)}) collective-permute-start(f32[1,40,9216]{2,1,0:T(8,128)} %collective-permute-done.6), channel_id=1, source_target_pairs={{11,15},{12,8},{4,0},{3,7},{27,31},{28,24},{20,16},{19,23}} | collective-permute-start | bytes 4423688 | tf_op jit(solution)/shard_map/ppermute | solution.py:404
  171.9 1.1 copy-start.1
where the time goes:
time: 178 us; the launch traced here: 177 us
  waiting for transfers between devices  114 us (64%)
  starting transfers between devices  33.6 us (19%)
  Pallas kernels  19.7 us (11%)
  local copies, waits for them, and re-layouts  5.1 us (3%)
  other arithmetic  3.86 us (2%)
    ppermute x11, waiting for transfers between devices, send(): return lax.ppermute(value[None], 'band', pairs)[0]  114 us
    ppermute x11, starting transfers between devices, send(): return lax.ppermute(value[None], 'band', pairs)[0]  33.6 us
    pallas_call x6, Pallas kernels, pair_terms(): pl.pallas_call(functools.partial(pair_body, points, slot, has), grid=(2 *...  9.61 us
    pallas_call x1, Pallas kernels, copied(): pl.pallas_call(copy_body, grid=(X_STEPS,), in_specs=[pl.BlockSpec(memory_...  4.69 us
    pallas_call x1, Pallas kernels, settle(): pl.pallas_call(settle_body, in_specs=[pl.BlockSpec(memory_space=pltpu.SME...  3.85 us
    unnamed x6, local copies, waits for them, and re-layouts  3.82 us
  transfers between devices with their start and end apart: 11, of which 3 were waited for; matrix products, arithmetic and copies ran while one was open for 3% of the time, Pallas kernels for 8%

commit v1 on v0

--- a/solution.py
+++ b/solution.py
@@ -267,8 +267,10 @@
     return out if len(out) > 1 else out[0]
 
 
-def copy_body(flags_ref, block_ref, new_block_ref):
-    new_block_ref[...] = block_ref[...]
+def copy_body(flags_ref, block_ref, first_ref, second_ref):
+    del flags_ref
+    first_ref[...] = block_ref[...]
+    second_ref[...] = block_ref[...]
 
 
 def copied(flags, block):
@@ -278,8 +280,8 @@
         copy_body,
         grid=(X_STEPS,),
         in_specs=[pl.BlockSpec(memory_space=pltpu.SMEM), part],
-        out_specs=part,
-        out_shape=jax.ShapeDtypeStruct(block.shape, block.dtype),
+        out_specs=[part, part],
+        out_shape=[jax.ShapeDtypeStruct(block.shape, block.dtype)] * 2,
         compiler_params=pltpu.CompilerParams(vmem_limit_bytes=62 * 2**20),
         name="copied",
     )(flags, block)
@@ -410,16 +412,17 @@
     pair = functools.partial(pair_terms, flags)
     crossed = send(own, CROSSING)
     partner = send(own, PARTNERS)
-    own_copy = copied(flags, own)
+    own_copy, direct_copy = copied(flags, own)
     token = crossed[:8, :LANES] + kernel[0, :8] + own_copy[:8, :LANES]
-    left, held_back = gate(send(token, ARRIVED), left, partner, own_copy)
+    direct_copy = hold(direct_copy, partner)
+    direct = send(direct_copy, DIRECT)
+    left, held_back = gate(send(token, ARRIVED), left, direct_copy, own_copy)
     constants = (kernel, left, right)
     beside = send(held_back, BESIDE)
     single = send(held_back, SINGLES)
-    direct = send(held_back, DIRECT)
 
     partner_sum, crossed_sum = pair(0, partner, crossed, constants, for_b=True)
-    own_sum, crossed_sum = pair(1, own, crossed, constants, sum_b=crossed_sum, for_b=True)
+    own_sum, crossed_sum = pair(1, own, crossed, constants, sum_b=crossed_sum, for_b=True, then=direct)
     home = send(crossed_sum, HOME_ACROSS)
     partner = hold(partner, own_sum, beside)
     turned = send(partner, TURNED)
@@ -427,8 +430,8 @@
     bottom = send(bottom, HOME_TURN)
     top = send(top, HOME_FAR)
     bottom = send(bottom, HOME_TURNED)
-    own_sum = pair(3, own, single, constants, sum_a=own_sum, in_place=True)
-    own_sum = pair(4, own, direct, constants, sum_a=own_sum, in_place=True, then=home)
+    own_sum = pair(3, own, direct, constants, sum_a=own_sum, in_place=True)
+    own_sum = pair(4, own, single, constants, sum_a=own_sum, in_place=True, then=home)
     own_sum = pair(5, own, turned, constants, sum_a=own_sum, in_place=True)
     return settle(flags, home, top, bottom, own_sum)[None]
 

time: 178 us -> 167 us (0.938)
  starting transfers between devices: 33.6 us -> 28.1 us
  waiting for transfers between devices: 114 us -> 110 us
  local copies, waits for them, and re-layouts: 5.1 us -> 2.98 us
    ppermute x11, starting transfers between devices: 33.6 us -> 28.1 us  [send(): return lax.ppermute(value[None], 'band', pairs)[0]]
    ppermute x11, waiting for transfers between devices: 114 us -> 110 us  [send(): return lax.ppermute(value[None], 'band', pairs)[0]]
    unnamed x6 -> x4, local copies, waits for them, and re-layouts: 3.82 us -> 1.69 us
  transfers between devices with their start and end apart: 11 -> 11, of which waited for: 3 -> 4; matrix products, arithmetic and copies ran while one was open for 3% -> 4% of each run, Pallas kernels for 8% -> 10%
where the time goes in v1:
time: 167 us
  waiting for transfers between devices  110 us (66%)
  starting transfers between devices  28.1 us (17%)
  Pallas kernels  20.2 us (12%)
  other arithmetic  5.28 us (3%)
  local copies, waits for them, and re-layouts  2.98 us (2%)
    ppermute x11, waiting for transfers between devices, send(): return lax.ppermute(value[None], 'band', pairs)[0]  110 us
    ppermute x11, starting transfers between devices, send(): return lax.ppermute(value[None], 'band', pairs)[0]  28.1 us
    pallas_call x6, Pallas kernels, pair_terms(): pl.pallas_call(functools.partial(pair_body, points, slot, has), grid=(2 *...  9.61 us
    pallas_call x1, Pallas kernels, copied(): pl.pallas_call(copy_body, grid=(X_STEPS,), in_specs=[pl.BlockSpec(memory_...  5.23 us
    select_n x1, other arithmetic, screened_kernel(): return jnp.where(inside, kernel / float(points * points * points), 0.0)  4.49 us
    pallas_call x1, Pallas kernels, settle(): pl.pallas_call(settle_body, in_specs=[pl.BlockSpec(memory_space=pltpu.SME...  3.85 us
  transfers between devices with their start and end apart: 11, of which 4 were waited for; matrix products, arithmetic and copies ran while one was open for 4% of the time, Pallas kernels for 10%

profile of v1, /device:TPU:0, one launch (start us, length us, event | category | flops | bytes accessed | tf_op | source)
XLA Modules:
  0.0 166.6 jit_solution(11021407352266249859)
XLA Ops:
  0.0 7.7 %collective-permute-start.1 = (f32[1,96,9216]{2,1,0:T(8,128)}, f32[1,96,9216]{2,1,0:T(8,128)}, u32[]{:S(2)}, u32[]{:S(2)}) collective-permute-start(f32[1,96,9216]{2,1,0:T(8,128)} %param.4), channel_id=1, source_target_pairs={{8,14},{15,9},{9,11},{14,12},{7,1},{0,6},{6,4},{1,3},{24,30},{31,2... | collective-permute-start | bytes 10616840 | tf_op jit(solution)/shard_map/ppermute | solution.py:406
  7.7 2.5 %collective-permute-start = (f32[1,96,9216]{2,1,0:T(8,128)}, f32[1,96,9216]{2,1,0:T(8,128)}, u32[]{:S(2)}, u32[]{:S(2)}) collective-permute-start(f32[1,96,9216]{2,1,0:T(8,128)} %param.4), channel_id=1, source_target_pairs={{3,14},{4,9},{12,1},{11,6},{19,30},{20,25},{28,17},{27,22}} | collective-permute-start | bytes 10616840 | tf_op jit(solution)/shard_map/ppermute | solution.py:406
  10.2 1.3 dynamic-slice_bitcast_fusion.flags_ref.refs_0_
  11.4 5.2 %copied.1 = (f32[96,9216]{1,0:T(8,128)}, f32[96,9216]{1,0:T(8,128)}) custom-call(s32[13]{0:T(128)} %dynamic-slice_bitcast_fusion.flags_ref.refs_0_, f32[96,9216]{1,0:T(8,128)} %bitcast.30), custom_call_target="tpu_custom_call" | custom-call | tf_op jit(solution)/shard_map/copied/pallas_call | solution.py:279
  16.7 0.1 broadcast_add_fusion
  16.8 4.5 %fusion.5.refs_3_.refs_5_.refs_4_ = f32[96,96,128]{2,1,0:T(8,128)} fusion(f32[128]{0:T(128)S(1)} %fusion.14, f32[96,96]{1,0:T(8,128)S(1)} %broadcast_add_fusion, pred[128]{0:T(512)(128)(4,1)S(1)} %iota_compare_fusion), kind=kLoop, calls=%fused_computation.7 | loop fusion | flops 12976128 | bytes 4756096 | tf_op jit(solution)/shard_map/jit(_where)/select_n | solution.py:40
  21.3 23.9 %collective-permute-done.1 = f32[1,96,9216]{2,1,0:T(8,128)} collective-permute-done((f32[1,96,9216]{2,1,0:T(8,128)}, f32[1,96,9216]{2,1,0:T(8,128)}, u32[]{:S(2)}, u32[]{:S(2)}) %collective-permute-start.1) | collective-permute-done | bytes 3538976 | tf_op jit(solution)/shard_map/ppermute | solution.py:406
  45.2 3.1 %collective-permute-start.3 = (f32[1,96,9216]{2,1,0:T(8,128)}, f32[1,96,9216]{2,1,0:T(8,128)}, u32[]{:S(2)}, u32[]{:S(2)}) collective-permute-start(f32[1,96,9216]{2,1,0:T(8,128)} %bitcast.35), channel_id=1, source_target_pairs={{15,10},{8,13},{0,5},{7,2},{31,26},{24,29},{16,21},{23,18}} | collective-permute-start | bytes 10616840 | tf_op jit(solution)/shard_map/ppermute | solution.py:406
  48.3 0.0 collective-permute-done
  48.3 0.7 fusion.11
  49.0 0.6 collective-permute-start.2
  49.6 0.0 collective-permute-done.2
  49.6 0.0 copy-start.1
  49.6 0.6 copy-done.1
  50.2 1.5 gate.1
  51.7 2.4 %collective-permute-start.5 = (f32[1,96,9216]{2,1,0:T(8,128)}, f32[1,96,9216]{2,1,0:T(8,128)}, u32[]{:S(2)}, u32[]{:S(2)}) collective-permute-start(f32[1,96,9216]{2,1,0:T(8,128)} %bitcast.36), channel_id=1, source_target_pairs={{13,14},{10,9},{2,1},{5,6},{29,30},{26,25},{18,17},{21,22}} | collective-permute-start | bytes 10616840 | tf_op jit(solution)/shard_map/ppermute | solution.py:406
  54.2 2.4 %collective-permute-start.10 = (f32[1,96,9216]{2,1,0:T(8,128)}, f32[1,96,9216]{2,1,0:T(8,128)}, u32[]{:S(2)}, u32[]{:S(2)}) collective-permute-start(f32[1,96,9216]{2,1,0:T(8,128)} %bitcast.37), channel_id=1, source_target_pairs={{5,10},{2,13},{10,5},{13,2},{21,26},{18,29},{26,21},{29,18}} | collective-permute-start | bytes 10616840 | tf_op jit(solution)/shard_map/ppermute | solution.py:406
  56.6 1.5 pair_terms.6
  58.2 27.6 %collective-permute-done.3 = f32[1,96,9216]{2,1,0:T(8,128)} collective-permute-done((f32[1,96,9216]{2,1,0:T(8,128)}, f32[1,96,9216]{2,1,0:T(8,128)}, u32[]{:S(2)}, u32[]{:S(2)}) %collective-permute-start.3) | collective-permute-done | bytes 3538976 | tf_op jit(solution)/shard_map/ppermute | solution.py:406
  85.8 1.6 pair_terms.7
  87.4 2.5 %collective-permute-start.4 = (f32[1,96,9216]{2,1,0:T(8,128)}, f32[1,96,9216]{2,1,0:T(8,128)}, u32[]{:S(2)}, u32[]{:S(2)}) collective-permute-start(f32[1,96,9216]{2,1,0:T(8,128)} %bitcast.40), channel_id=1, source_target_pairs={{9,4},{14,3},{6,11},{1,12},{25,20},{30,19},{22,27},{17,28}} | collective-permute-start | bytes 10616840 | tf_op jit(solution)/shard_map/ppermute | solution.py:406
  89.9 0.0 collective-permute-done.5
  89.9 2.5 %collective-permute-start.9 = (f32[1,96,9216]{2,1,0:T(8,128)}, f32[1,96,9216]{2,1,0:T(8,128)}, u32[]{:S(2)}, u32[]{:S(2)}) collective-permute-start(f32[1,96,9216]{2,1,0:T(8,128)} %bitcast.17), channel_id=1, source_target_pairs={{11,14},{12,9},{4,1},{3,6},{27,30},{28,25},{20,17},{19,22}} | collective-permute-start | bytes 10616840 | tf_op jit(solution)/shard_map/ppermute | solution.py:406
  92.3 1.6 pair_terms.8
  93.9 1.8 %collective-permute-start.7 = (f32[1,40,9216]{2,1,0:T(8,128)}, f32[1,40,9216]{2,1,0:T(8,128)}, u32[]{:S(2)}, u32[]{:S(2)}) collective-permute-start(f32[1,40,9216]{2,1,0:T(8,128)} %bitcast.42), channel_id=1, source_target_pairs={{9,11},{14,12},{6,4},{1,3},{25,27},{30,28},{22,20},{17,19}} | collective-permute-start | bytes 4423688 | tf_op jit(solution)/shard_map/ppermute | solution.py:406
  95.8 1.3 collective-permute-start.6
  97.1 0.0 collective-permute-done.7
  97.1 1.3 collective-permute-start.8
  98.4 1.6 pair_terms.9.refs_3_
  99.9 0.0 collective-permute-done.10
  99.9 0.0 collective-permute-done.4
  100.0 1.6 pair_terms.10.refs_3_
  101.5 0.0 collective-permute-done.9
  101.5 1.8 %pair_terms.11.own_ref = f32[96,9216]{1,0:T(8,128)} custom-call(s32[13]{0:T(128)} %dynamic-slice_bitcast_fusion.flags_ref.refs_0_, f32[96,9216]{1,0:T(8,128)} %bitcast.34, f32[96,9216]{1,0:T(8,128)} %bitcast.18.refs_2_, f32[96,9216]{1,0:T(8,128)} %pair_terms.10.refs_3_, ...), custom_call_target="tpu_custom_call", output_to_operand_aliasing={{}: (3, {})} | custom-call | flops 100000000 | bytes 1000000 | tf_op jit(solution)/shard_map/pair_terms/pallas_call | solution.py:241
  103.3 54.1 %collective-permute-done.6 = f32[1,56,9216]{2,1,0:T(8,128)} collective-permute-done((f32[1,56,9216]{2,1,0:T(8,128)}, f32[1,56,9216]{2,1,0:T(8,128)}, u32[]{:S(2)}, u32[]{:S(2)}) %collective-permute-start.6) | collective-permute-done | bytes 2064416 | tf_op jit(solution)/shard_map/ppermute | solution.py:406
  157.4 4.1 %collective-permute-done.8 = f32[1,40,9216]{2,1,0:T(8,128)S(1)} collective-permute-done((f32[1,40,9216]{2,1,0:T(8,128)}, f32[1,40,9216]{2,1,0:T(8,128)S(1)}, u32[]{:S(2)}, u32[]{:S(2)}) %collective-permute-start.8) | collective-permute-done | bytes 1474592 | tf_op jit(solution)/shard_map/ppermute | solution.py:406
  161.5 0.0 copy-start
  161.5 1.1 copy-done
  162.6 3.9 %settle.1 = f32[96,9216]{1,0:T(8,128)} custom-call(s32[13]{0:T(128)} %dynamic-slice_bitcast_fusion.flags_ref.refs_0_, f32[96,9216]{1,0:T(8,128)} %bitcast.10.refs_4_.home_ref, f32[56,9216]{1,0:T(8,128)} %bitcast.14.top_ref, f32[40,9216]{1,0:T(8,128)} %bitcast.38, f32[96,9216]{1,0:T(8,128)} %pair_terms.11.own_ref), custom_call_target="tpu_custom_call", output_to_operand_aliasing={{}: (4, {})} | custom-call | tf_op jit(solution)/shard_map/settle/pallas_call | solution.py:367
  (6 shorter events, 0.0 us)
Async XLA Ops:
  0.0 45.2 %collective-permute-start.1 = (f32[1,96,9216]{2,1,0:T(8,128)}, f32[1,96,9216]{2,1,0:T(8,128)}, u32[]{:S(2)}, u32[]{:S(2)}) collective-permute-start(f32[1,96,9216]{2,1,0:T(8,128)} %param.4), channel_id=1, source_target_pairs={{8,14},{15,9},{9,11},{14,12},{7,1},{0,6},{6,4},{1,3},{24,30},{31,2... | collective-permute-start | bytes 10616840 | tf_op jit(solution)/shard_map/ppermute | solution.py:406
  7.7 40.6 %collective-permute-start = (f32[1,96,9216]{2,1,0:T(8,128)}, f32[1,96,9216]{2,1,0:T(8,128)}, u32[]{:S(2)}, u32[]{:S(2)}) collective-permute-start(f32[1,96,9216]{2,1,0:T(8,128)} %param.4), channel_id=1, source_target_pairs={{3,14},{4,9},{12,1},{11,6},{19,30},{20,25},{28,17},{27,22}} | collective-permute-start | bytes 10616840 | tf_op jit(solution)/shard_map/ppermute | solution.py:406
  45.2 40.6 %collective-permute-start.3 = (f32[1,96,9216]{2,1,0:T(8,128)}, f32[1,96,9216]{2,1,0:T(8,128)}, u32[]{:S(2)}, u32[]{:S(2)}) collective-permute-start(f32[1,96,9216]{2,1,0:T(8,128)} %bitcast.35), channel_id=1, source_target_pairs={{15,10},{8,13},{0,5},{7,2},{31,26},{24,29},{16,21},{23,18}} | collective-permute-start | bytes 10616840 | tf_op jit(solution)/shard_map/ppermute | solution.py:406
  49.0 0.7 collective-permute-start.2
  49.6 0.6 copy-start.1
  51.7 38.1 %collective-permute-start.5 = (f32[1,96,9216]{2,1,0:T(8,128)}, f32[1,96,9216]{2,1,0:T(8,128)}, u32[]{:S(2)}, u32[]{:S(2)}) collective-permute-start(f32[1,96,9216]{2,1,0:T(8,128)} %bitcast.36), channel_id=1, source_target_pairs={{13,14},{10,9},{2,1},{5,6},{29,30},{26,25},{18,17},{21,22}} | collective-permute-start | bytes 10616840 | tf_op jit(solution)/shard_map/ppermute | solution.py:406
  54.2 45.7 %collective-permute-start.10 = (f32[1,96,9216]{2,1,0:T(8,128)}, f32[1,96,9216]{2,1,0:T(8,128)}, u32[]{:S(2)}, u32[]{:S(2)}) collective-permute-start(f32[1,96,9216]{2,1,0:T(8,128)} %bitcast.37), channel_id=1, source_target_pairs={{5,10},{2,13},{10,5},{13,2},{21,26},{18,29},{26,21},{29,18}} | collective-permute-start | bytes 10616840 | tf_op jit(solution)/shard_map/ppermute | solution.py:406
  87.4 12.5 %collective-permute-start.4 = (f32[1,96,9216]{2,1,0:T(8,128)}, f32[1,96,9216]{2,1,0:T(8,128)}, u32[]{:S(2)}, u32[]{:S(2)}) collective-permute-start(f32[1,96,9216]{2,1,0:T(8,128)} %bitcast.40), channel_id=1, source_target_pairs={{9,4},{14,3},{6,11},{1,12},{25,20},{30,19},{22,27},{17,28}} | collective-permute-start | bytes 10616840 | tf_op jit(solution)/shard_map/ppermute | solution.py:406
  89.9 11.6 %collective-permute-start.9 = (f32[1,96,9216]{2,1,0:T(8,128)}, f32[1,96,9216]{2,1,0:T(8,128)}, u32[]{:S(2)}, u32[]{:S(2)}) collective-permute-start(f32[1,96,9216]{2,1,0:T(8,128)} %bitcast.17), channel_id=1, source_target_pairs={{11,14},{12,9},{4,1},{3,6},{27,30},{28,25},{20,17},{19,22}} | collective-permute-start | bytes 10616840 | tf_op jit(solution)/shard_map/ppermute | solution.py:406
  93.9 3.1 %collective-permute-start.7 = (f32[1,40,9216]{2,1,0:T(8,128)}, f32[1,40,9216]{2,1,0:T(8,128)}, u32[]{:S(2)}, u32[]{:S(2)}) collective-permute-start(f32[1,40,9216]{2,1,0:T(8,128)} %bitcast.42), channel_id=1, source_target_pairs={{9,11},{14,12},{6,4},{1,3},{25,27},{30,28},{22,20},{17,19}} | collective-permute-start | bytes 4423688 | tf_op jit(solution)/shard_map/ppermute | solution.py:406
  95.8 61.6 %collective-permute-start.6 = (f32[1,56,9216]{2,1,0:T(8,128)}, f32[1,56,9216]{2,1,0:T(8,128)}, u32[]{:S(2)}, u32[]{:S(2)}) collective-permute-start(f32[1,56,9216]{2,1,0:T(8,128)} %bitcast.41), channel_id=1, source_target_pairs={{9,15},{14,8},{6,0},{1,7},{25,31},{30,24},{22,16},{17,23}} | collective-permute-start | bytes 6193160 | tf_op jit(solution)/shard_map/ppermute | solution.py:406
  97.1 64.4 %collective-permute-start.8 = (f32[1,40,9216]{2,1,0:T(8,128)}, f32[1,40,9216]{2,1,0:T(8,128)S(1)}, u32[]{:S(2)}, u32[]{:S(2)}) collective-permute-start(f32[1,40,9216]{2,1,0:T(8,128)} %collective-permute-done.7), channel_id=1, source_target_pairs={{11,15},{12,8},{4,0},{3,7},{27,31},{28,24},{20,16},{19,23}} | collective-permute-start | bytes 4423688 | tf_op jit(solution)/shard_map/ppermute | solution.py:406
  161.5 1.1 copy-start

commit v2 on v1

--- a/solution.py
+++ b/solution.py
@@ -37,7 +37,7 @@
     finite = jnp.where(squared > 0.0, squared, 1.0)
     screened = 4.0 * math.pi / finite * -jnp.expm1(-finite / (4.0 * screen_rate * screen_rate))
     kernel = jnp.where(squared > 0.0, screened, math.pi / (screen_rate * screen_rate))
-    return jnp.where(inside, kernel / float(points * points * points), 0.0)
+    return jnp.where(inside, kernel / -float(points * points * points), 0.0)
 
 
 def hartley_tables(points):
@@ -157,10 +157,9 @@
                     fetch(name, chunk).start()
 
     def lanes_apart(block):
-        gap = jnp.zeros((points, LANES - points), jnp.float32)
-        rows = [
-            jnp.concatenate([block[:, q * points:(q + 1) * points], gap], 1) for q in range(ys)
-        ]
+        tail = jnp.zeros((points, LANES), jnp.float32)
+        wide = jnp.concatenate([block, tail], 1)
+        rows = [wide[:, q * points:q * points + LANES] for q in range(ys)]
         return jnp.swapaxes(jnp.stack(rows, 0), 0, 1)
 
     def lanes_together(block):
@@ -203,12 +202,12 @@
             fetch(name, chunk).wait()
         block = lanes_together(held[:, pl.ds(start, ys), :])
         potential = from_left(left_ref[...], block)
-        for_a = -(here("b", chunk) * potential)
+        for_a = here("b", chunk) * potential
         if "sum_a" in has:
             for_a = for_a + jnp.where(with_sum, here("sum_a", chunk), 0.0)
         near_out[0, :, span_of(chunk)] = for_a
         if "for_b" in has:
-            for_b = -(here("a", chunk) * potential)
+            for_b = here("a", chunk) * potential
             if "sum_b" in has:
                 for_b = for_b + here("sum_b", chunk)
             near_out[1, :, span_of(chunk)] = for_b
@@ -258,7 +257,7 @@
             pltpu.SemaphoreType.DMA((PLANE_STEPS,)),
             pltpu.SemaphoreType.DMA((len(rows), X_STEPS)),
         ],
-        compiler_params=pltpu.CompilerParams(vmem_limit_bytes=62 * 2**20),
+        compiler_params=pltpu.CompilerParams(vmem_limit_bytes=63 * 2**20),
         cost_estimate=pl.CostEstimate(
             flops=100_000_000, bytes_accessed=1_000_000, transcendentals=0
         ),
@@ -282,7 +281,7 @@
         in_specs=[pl.BlockSpec(memory_space=pltpu.SMEM), part],
         out_specs=[part, part],
         out_shape=[jax.ShapeDtypeStruct(block.shape, block.dtype)] * 2,
-        compiler_params=pltpu.CompilerParams(vmem_limit_bytes=62 * 2**20),
+        compiler_params=pltpu.CompilerParams(vmem_limit_bytes=63 * 2**20),
         name="copied",
     )(flags, block)
 
@@ -304,7 +303,7 @@
             jax.ShapeDtypeStruct(block.shape, block.dtype),
         ],
         input_output_aliases={3: 1},
-        compiler_params=pltpu.CompilerParams(vmem_limit_bytes=62 * 2**20),
+        compiler_params=pltpu.CompilerParams(vmem_limit_bytes=63 * 2**20),
         name="gate",
     )(token, left, partner, block)
 
@@ -321,7 +320,7 @@
         out_specs=anywhere,
         out_shape=jax.ShapeDtypeStruct(block.shape, block.dtype),
         input_output_aliases={0: 0},
-        compiler_params=pltpu.CompilerParams(vmem_limit_bytes=62 * 2**20),
+        compiler_params=pltpu.CompilerParams(vmem_limit_bytes=63 * 2**20),
         name="hold",
     )(block, *then)
 
@@ -374,7 +373,7 @@
             pltpu.VMEM(own_sum.shape, own_sum.dtype),
             pltpu.SemaphoreType.DMA((2, 2, SETTLE_STEPS)),
         ],
-        compiler_params=pltpu.CompilerParams(vmem_limit_bytes=62 * 2**20),
+        compiler_params=pltpu.CompilerParams(vmem_limit_bytes=63 * 2**20),
         name="settle",
     )(flags, home, top, bottom, own_sum)
 
@@ -424,7 +423,7 @@
     partner_sum, crossed_sum = pair(0, partner, crossed, constants, for_b=True)
     own_sum, crossed_sum = pair(1, own, crossed, constants, sum_b=crossed_sum, for_b=True, then=direct)
     home = send(crossed_sum, HOME_ACROSS)
-    partner = hold(partner, own_sum, beside)
+    partner = hold(partner, own_sum)
     turned = send(partner, TURNED)
     top, bottom = pair(2, partner, beside, constants, sum_a=partner_sum, halves=True)
     bottom = send(bottom, HOME_TURN)

time: 167 us -> 170 us (1.018)
  waiting for transfers between devices: 110 us -> 113 us
    ppermute x11, waiting for transfers between devices: 110 us -> 113 us  [send(): return lax.ppermute(value[None], 'band', pairs)[0]]
  transfers between devices with their start and end apart: 11 -> 11, of which waited for: 4 -> 4; matrix products, arithmetic and copies ran while one was open for 4% -> 3% of each run, Pallas kernels for 10% -> 10%
where the time goes in v2:
time: 170 us
  waiting for transfers between devices  113 us (66%)
  starting transfers between devices  28.1 us (17%)
  Pallas kernels  20.2 us (12%)
  local copies, waits for them, and re-layouts  3.98 us (2%)
  other arithmetic  3.84 us (2%)
    ppermute x11, waiting for transfers between devices, send(): return lax.ppermute(value[None], 'band', pairs)[0]  113 us
    ppermute x11, starting transfers between devices, send(): return lax.ppermute(value[None], 'band', pairs)[0]  28.1 us
    pallas_call x6, Pallas kernels, pair_terms(): pl.pallas_call(functools.partial(pair_body, points, slot, has), grid=(2 *...  9.61 us
    pallas_call x1, Pallas kernels, copied(): pl.pallas_call(copy_body, grid=(X_STEPS,), in_specs=[pl.BlockSpec(memory_...  5.23 us
    pallas_call x1, Pallas kernels, settle(): pl.pallas_call(settle_body, in_specs=[pl.BlockSpec(memory_space=pltpu.SME...  3.86 us
  transfers between devices with their start and end apart: 11, of which 4 were waited for; matrix products, arithmetic and copies ran while one was open for 3% of the time, Pallas kernels for 10%

profile of v2, /device:TPU:0, one launch (start us, length us, event | category | flops | bytes accessed | tf_op | source)
XLA Modules:
  0.0 169.8 jit_solution(5677742366954161564)
XLA Ops:
  0.0 7.7 %collective-permute-start.1 = (f32[1,96,9216]{2,1,0:T(8,128)}, f32[1,96,9216]{2,1,0:T(8,128)}, u32[]{:S(2)}, u32[]{:S(2)}) collective-permute-start(f32[1,96,9216]{2,1,0:T(8,128)} %param.4), channel_id=1, source_target_pairs={{8,14},{15,9},{9,11},{14,12},{7,1},{0,6},{6,4},{1,3},{24,30},{31,2... | collective-permute-start | bytes 10616840 | tf_op jit(solution)/shard_map/ppermute | solution.py:405
  7.7 2.5 %collective-permute-start = (f32[1,96,9216]{2,1,0:T(8,128)}, f32[1,96,9216]{2,1,0:T(8,128)}, u32[]{:S(2)}, u32[]{:S(2)}) collective-permute-start(f32[1,96,9216]{2,1,0:T(8,128)} %param.4), channel_id=1, source_target_pairs={{3,14},{4,9},{12,1},{11,6},{19,30},{20,25},{28,17},{27,22}} | collective-permute-start | bytes 10616840 | tf_op jit(solution)/shard_map/ppermute | solution.py:405
  10.1 1.3 dynamic-slice_bitcast_fusion.flags_ref.refs_0_
  11.4 5.2 %copied.1 = (f32[96,9216]{1,0:T(8,128)}, f32[96,9216]{1,0:T(8,128)}) custom-call(s32[13]{0:T(128)} %dynamic-slice_bitcast_fusion.flags_ref.refs_0_, f32[96,9216]{1,0:T(8,128)} %bitcast.30), custom_call_target="tpu_custom_call" | custom-call | tf_op jit(solution)/shard_map/copied/pallas_call | solution.py:278
  16.7 0.1 broadcast_add_fusion
  16.7 28.4 %collective-permute-done.1 = f32[1,96,9216]{2,1,0:T(8,128)} collective-permute-done((f32[1,96,9216]{2,1,0:T(8,128)}, f32[1,96,9216]{2,1,0:T(8,128)}, u32[]{:S(2)}, u32[]{:S(2)}) %collective-permute-start.1) | collective-permute-done | bytes 3538976 | tf_op jit(solution)/shard_map/ppermute | solution.py:405
  45.2 3.1 %collective-permute-start.3 = (f32[1,96,9216]{2,1,0:T(8,128)}, f32[1,96,9216]{2,1,0:T(8,128)}, u32[]{:S(2)}, u32[]{:S(2)}) collective-permute-start(f32[1,96,9216]{2,1,0:T(8,128)} %bitcast.35), channel_id=1, source_target_pairs={{15,10},{8,13},{0,5},{7,2},{31,26},{24,29},{16,21},{23,18}} | collective-permute-start | bytes 10616840 | tf_op jit(solution)/shard_map/ppermute | solution.py:405
  48.3 3.1 %fusion.5.refs_3_.refs_5_.refs_4_ = f32[96,96,128]{2,1,0:T(8,128)S(1)} fusion(f32[128]{0:T(128)S(1)} %fusion.14, f32[96,96]{1,0:T(8,128)S(1)} %broadcast_add_fusion, pred[128]{0:T(512)(128)(4,1)S(1)} %iota_compare_fusion), kind=kLoop, calls=%fused_computation.7 | loop fusion | flops 12976128 | bytes 4756096 | tf_op jit(solution)/shard_map/jit(_where)/select_n | solution.py:40
  51.3 0.0 copy-start
  51.3 0.0 collective-permute-done
  51.3 2.1 %copy-done = f32[96,96,128]{2,1,0:T(8,128)} copy-done((f32[96,96,128]{2,1,0:T(8,128)}, f32[96,96,128]{2,1,0:T(8,128)S(1)}, u32[]{:S(2)}) %copy-start) | copy-done | bytes 4718616
  53.4 0.7 fusion.11
  54.1 0.6 collective-permute-start.2
  54.8 0.0 collective-permute-done.2
  54.8 0.0 copy-start.1
  54.8 0.6 copy-done.1
  55.4 1.5 gate.1
  56.9 2.4 %collective-permute-start.5 = (f32[1,96,9216]{2,1,0:T(8,128)}, f32[1,96,9216]{2,1,0:T(8,128)}, u32[]{:S(2)}, u32[]{:S(2)}) collective-permute-start(f32[1,96,9216]{2,1,0:T(8,128)} %bitcast.36), channel_id=1, source_target_pairs={{13,14},{10,9},{2,1},{5,6},{29,30},{26,25},{18,17},{21,22}} | collective-permute-start | bytes 10616840 | tf_op jit(solution)/shard_map/ppermute | solution.py:405
  59.4 2.5 %collective-permute-start.10 = (f32[1,96,9216]{2,1,0:T(8,128)}, f32[1,96,9216]{2,1,0:T(8,128)}, u32[]{:S(2)}, u32[]{:S(2)}) collective-permute-start(f32[1,96,9216]{2,1,0:T(8,128)} %bitcast.37), channel_id=1, source_target_pairs={{5,10},{2,13},{10,5},{13,2},{21,26},{18,29},{26,21},{29,18}} | collective-permute-start | bytes 10616840 | tf_op jit(solution)/shard_map/ppermute | solution.py:405
  61.9 1.5 pair_terms.6
  63.4 22.4 %collective-permute-done.3 = f32[1,96,9216]{2,1,0:T(8,128)} collective-permute-done((f32[1,96,9216]{2,1,0:T(8,128)}, f32[1,96,9216]{2,1,0:T(8,128)}, u32[]{:S(2)}, u32[]{:S(2)}) %collective-permute-start.3) | collective-permute-done | bytes 3538976 | tf_op jit(solution)/shard_map/ppermute | solution.py:405
  85.8 1.6 pair_terms.7
  87.4 2.5 %collective-permute-start.4 = (f32[1,96,9216]{2,1,0:T(8,128)}, f32[1,96,9216]{2,1,0:T(8,128)}, u32[]{:S(2)}, u32[]{:S(2)}) collective-permute-start(f32[1,96,9216]{2,1,0:T(8,128)} %bitcast.39), channel_id=1, source_target_pairs={{9,4},{14,3},{6,11},{1,12},{25,20},{30,19},{22,27},{17,28}} | collective-permute-start | bytes 10616840 | tf_op jit(solution)/shard_map/ppermute | solution.py:405
  89.9 2.5 %collective-permute-start.9 = (f32[1,96,9216]{2,1,0:T(8,128)}, f32[1,96,9216]{2,1,0:T(8,128)}, u32[]{:S(2)}, u32[]{:S(2)}) collective-permute-start(f32[1,96,9216]{2,1,0:T(8,128)} %bitcast.17), channel_id=1, source_target_pairs={{11,14},{12,9},{4,1},{3,6},{27,30},{28,25},{20,17},{19,22}} | collective-permute-start | bytes 10616840 | tf_op jit(solution)/shard_map/ppermute | solution.py:405
  92.3 0.0 collective-permute-done.5
  92.3 1.6 pair_terms.8
  93.9 1.8 %collective-permute-start.7 = (f32[1,40,9216]{2,1,0:T(8,128)}, f32[1,40,9216]{2,1,0:T(8,128)}, u32[]{:S(2)}, u32[]{:S(2)}) collective-permute-start(f32[1,40,9216]{2,1,0:T(8,128)} %bitcast.41), channel_id=1, source_target_pairs={{9,11},{14,12},{6,4},{1,3},{25,27},{30,28},{22,20},{17,19}} | collective-permute-start | bytes 4423688 | tf_op jit(solution)/shard_map/ppermute | solution.py:405
  95.8 1.3 collective-permute-start.6
  97.1 0.0 collective-permute-done.7
  97.1 1.3 collective-permute-start.8
  98.4 1.6 pair_terms.9.refs_3_
  99.9 0.0 collective-permute-done.10
  99.9 0.0 collective-permute-done.4
  100.0 1.6 pair_terms.10.refs_3_
  101.5 0.0 collective-permute-done.9
  101.5 1.8 %pair_terms.11.own_ref = f32[96,9216]{1,0:T(8,128)} custom-call(s32[13]{0:T(128)} %dynamic-slice_bitcast_fusion.flags_ref.refs_0_, f32[96,9216]{1,0:T(8,128)} %bitcast.34, f32[96,9216]{1,0:T(8,128)} %bitcast.18.refs_2_, f32[96,9216]{1,0:T(8,128)} %pair_terms.10.refs_3_, f32[96,96,128]{2,1,0:T(8,128)} %copy-done, ...), custom_call_target="tpu_custom_call", output_to_operand_aliasing={{}: (3, {})} | custom-call | flops 100000000 | bytes 1000000 | tf_op jit(solution)/shard_map/pair_terms/pallas_call | solution.py:240
  103.3 59.5 %collective-permute-done.6 = f32[1,56,9216]{2,1,0:T(8,128)} collective-permute-done((f32[1,56,9216]{2,1,0:T(8,128)}, f32[1,56,9216]{2,1,0:T(8,128)}, u32[]{:S(2)}, u32[]{:S(2)}) %collective-permute-start.6) | collective-permute-done | bytes 2064416 | tf_op jit(solution)/shard_map/ppermute | solution.py:405
  162.8 3.0 %collective-permute-done.8 = f32[1,40,9216]{2,1,0:T(8,128)} collective-permute-done((f32[1,40,9216]{2,1,0:T(8,128)}, f32[1,40,9216]{2,1,0:T(8,128)}, u32[]{:S(2)}, u32[]{:S(2)}) %collective-permute-start.8) | collective-permute-done | bytes 1474592 | tf_op jit(solution)/shard_map/ppermute | solution.py:405
  165.8 3.9 %settle.1 = f32[96,9216]{1,0:T(8,128)} custom-call(s32[13]{0:T(128)} %dynamic-slice_bitcast_fusion.flags_ref.refs_0_, f32[96,9216]{1,0:T(8,128)} %bitcast.10.refs_4_.home_ref, f32[56,9216]{1,0:T(8,128)} %bitcast.14.top_ref, f32[40,9216]{1,0:T(8,128)} %bitcast.16.bottom_ref, f32[96,9216]{1,0:T(8,128)} %pair_terms.11.own_ref), custom_call_target="tpu_custom_call", output_to_operand_aliasing={{}: (4, {})} | custom-call | tf_op jit(solution)/shard_map/settle/pallas_call | solution.py:366
  (6 shorter events, 0.0 us)
Async XLA Ops:
  0.0 45.2 %collective-permute-start.1 = (f32[1,96,9216]{2,1,0:T(8,128)}, f32[1,96,9216]{2,1,0:T(8,128)}, u32[]{:S(2)}, u32[]{:S(2)}) collective-permute-start(f32[1,96,9216]{2,1,0:T(8,128)} %param.4), channel_id=1, source_target_pairs={{8,14},{15,9},{9,11},{14,12},{7,1},{0,6},{6,4},{1,3},{24,30},{31,2... | collective-permute-start | bytes 10616840 | tf_op jit(solution)/shard_map/ppermute | solution.py:405
  7.7 43.7 %collective-permute-start = (f32[1,96,9216]{2,1,0:T(8,128)}, f32[1,96,9216]{2,1,0:T(8,128)}, u32[]{:S(2)}, u32[]{:S(2)}) collective-permute-start(f32[1,96,9216]{2,1,0:T(8,128)} %param.4), channel_id=1, source_target_pairs={{3,14},{4,9},{12,1},{11,6},{19,30},{20,25},{28,17},{27,22}} | collective-permute-start | bytes 10616840 | tf_op jit(solution)/shard_map/ppermute | solution.py:405
  45.2 40.6 %collective-permute-start.3 = (f32[1,96,9216]{2,1,0:T(8,128)}, f32[1,96,9216]{2,1,0:T(8,128)}, u32[]{:S(2)}, u32[]{:S(2)}) collective-permute-start(f32[1,96,9216]{2,1,0:T(8,128)} %bitcast.35), channel_id=1, source_target_pairs={{15,10},{8,13},{0,5},{7,2},{31,26},{24,29},{16,21},{23,18}} | collective-permute-start | bytes 10616840 | tf_op jit(solution)/shard_map/ppermute | solution.py:405
  51.3 2.1 %copy-start = (f32[96,96,128]{2,1,0:T(8,128)}, f32[96,96,128]{2,1,0:T(8,128)S(1)}, u32[]{:S(2)}) copy-start(f32[96,96,128]{2,1,0:T(8,128)S(1)} %fusion.5.refs_3_.refs_5_.refs_4_) | copy-start | bytes 14155780
  54.1 0.7 collective-permute-start.2
  54.8 0.6 copy-start.1
  56.9 35.4 %collective-permute-start.5 = (f32[1,96,9216]{2,1,0:T(8,128)}, f32[1,96,9216]{2,1,0:T(8,128)}, u32[]{:S(2)}, u32[]{:S(2)}) collective-permute-start(f32[1,96,9216]{2,1,0:T(8,128)} %bitcast.36), channel_id=1, source_target_pairs={{13,14},{10,9},{2,1},{5,6},{29,30},{26,25},{18,17},{21,22}} | collective-permute-start | bytes 10616840 | tf_op jit(solution)/shard_map/ppermute | solution.py:405
  59.4 40.6 %collective-permute-start.10 = (f32[1,96,9216]{2,1,0:T(8,128)}, f32[1,96,9216]{2,1,0:T(8,128)}, u32[]{:S(2)}, u32[]{:S(2)}) collective-permute-start(f32[1,96,9216]{2,1,0:T(8,128)} %bitcast.37), channel_id=1, source_target_pairs={{5,10},{2,13},{10,5},{13,2},{21,26},{18,29},{26,21},{29,18}} | collective-permute-start | bytes 10616840 | tf_op jit(solution)/shard_map/ppermute | solution.py:405
  87.4 12.5 %collective-permute-start.4 = (f32[1,96,9216]{2,1,0:T(8,128)}, f32[1,96,9216]{2,1,0:T(8,128)}, u32[]{:S(2)}, u32[]{:S(2)}) collective-permute-start(f32[1,96,9216]{2,1,0:T(8,128)} %bitcast.39), channel_id=1, source_target_pairs={{9,4},{14,3},{6,11},{1,12},{25,20},{30,19},{22,27},{17,28}} | collective-permute-start | bytes 10616840 | tf_op jit(solution)/shard_map/ppermute | solution.py:405
  89.9 11.6 %collective-permute-start.9 = (f32[1,96,9216]{2,1,0:T(8,128)}, f32[1,96,9216]{2,1,0:T(8,128)}, u32[]{:S(2)}, u32[]{:S(2)}) collective-permute-start(f32[1,96,9216]{2,1,0:T(8,128)} %bitcast.17), channel_id=1, source_target_pairs={{11,14},{12,9},{4,1},{3,6},{27,30},{28,25},{20,17},{19,22}} | collective-permute-start | bytes 10616840 | tf_op jit(solution)/shard_map/ppermute | solution.py:405
  93.9 3.1 %collective-permute-start.7 = (f32[1,40,9216]{2,1,0:T(8,128)}, f32[1,40,9216]{2,1,0:T(8,128)}, u32[]{:S(2)}, u32[]{:S(2)}) collective-permute-start(f32[1,40,9216]{2,1,0:T(8,128)} %bitcast.41), channel_id=1, source_target_pairs={{9,11},{14,12},{6,4},{1,3},{25,27},{30,28},{22,20},{17,19}} | collective-permute-start | bytes 4423688 | tf_op jit(solution)/shard_map/ppermute | solution.py:405
  95.8 67.0 %collective-permute-start.6 = (f32[1,56,9216]{2,1,0:T(8,128)}, f32[1,56,9216]{2,1,0:T(8,128)}, u32[]{:S(2)}, u32[]{:S(2)}) collective-permute-start(f32[1,56,9216]{2,1,0:T(8,128)} %bitcast.40), channel_id=1, source_target_pairs={{9,15},{14,8},{6,0},{1,7},{25,31},{30,24},{22,16},{17,23}} | collective-permute-start | bytes 6193160 | tf_op jit(solution)/shard_map/ppermute | solution.py:405
  97.1 68.7 %collective-permute-start.8 = (f32[1,40,9216]{2,1,0:T(8,128)}, f32[1,40,9216]{2,1,0:T(8,128)}, u32[]{:S(2)}, u32[]{:S(2)}) collective-permute-start(f32[1,40,9216]{2,1,0:T(8,128)} %collective-permute-done.7), channel_id=1, source_target_pairs={{11,15},{12,8},{4,0},{3,7},{27,31},{28,24},{20,16},{19,23}} | collective-permute-start | bytes 4423688 | tf_op jit(solution)/shard_map/ppermute | solution.py:405

commit v3 on v2

--- a/solution.py
+++ b/solution.py
@@ -266,24 +266,28 @@
     return out if len(out) > 1 else out[0]
 
 
-def copy_body(flags_ref, block_ref, first_ref, second_ref):
-    del flags_ref
+def copy_body(flags_ref, kernel_ref, block_ref, first_ref, second_ref):
+    del flags_ref, kernel_ref
     first_ref[...] = block_ref[...]
     second_ref[...] = block_ref[...]
 
 
-def copied(flags, block):
+def copied(flags, kernel, block):
     points, plane = block.shape
     part = pl.BlockSpec((points, plane // X_STEPS), lambda i: (0, i))
     return pl.pallas_call(
         copy_body,
         grid=(X_STEPS,),
-        in_specs=[pl.BlockSpec(memory_space=pltpu.SMEM), part],
+        in_specs=[
+            pl.BlockSpec(memory_space=pltpu.SMEM),
+            pl.BlockSpec(memory_space=pl.ANY),
+            part,
+        ],
         out_specs=[part, part],
         out_shape=[jax.ShapeDtypeStruct(block.shape, block.dtype)] * 2,
         compiler_params=pltpu.CompilerParams(vmem_limit_bytes=63 * 2**20),
         name="copied",
-    )(flags, block)
+    )(flags, kernel, block)
 
 
 def gate_body(token_ref, left_ref, partner_ref, block_ref, new_left_ref, new_block_ref):
@@ -411,8 +415,8 @@
     pair = functools.partial(pair_terms, flags)
     crossed = send(own, CROSSING)
     partner = send(own, PARTNERS)
-    own_copy, direct_copy = copied(flags, own)
-    token = crossed[:8, :LANES] + kernel[0, :8] + own_copy[:8, :LANES]
+    own_copy, direct_copy = copied(flags, kernel, own)
+    token = crossed[:8, :LANES] + own_copy[:8, :LANES]
     direct_copy = hold(direct_copy, partner)
     direct = send(direct_copy, DIRECT)
     left, held_back = gate(send(token, ARRIVED), left, direct_copy, own_copy)

time: 170 us -> 166 us (0.976)
  waiting for transfers between devices: 113 us -> 109 us
  local copies, waits for them, and re-layouts: 3.98 us -> 1.82 us
    ppermute x11, waiting for transfers between devices: 113 us -> 109 us  [send(): return lax.ppermute(value[None], 'band', pairs)[0]]
    unnamed x4 -> x2, local copies, waits for them, and re-layouts: 2.69 us -> 0.59 us
  transfers between devices with their start and end apart: 11 -> 11, of which waited for: 4 -> 4; matrix products, arithmetic and copies ran while one was open for 3% -> 4% of each run, Pallas kernels for 10% -> 10%
where the time goes in v3:
time: 166 us; the launch traced here: 165 us
  waiting for transfers between devices  109 us (66%)
  starting transfers between devices  28.1 us (17%)
  Pallas kernels  20.2 us (12%)
  other arithmetic  5.28 us (3%)
  local copies, waits for them, and re-layouts  1.82 us (1%)
    ppermute x11, waiting for transfers between devices, send(): return lax.ppermute(value[None], 'band', pairs)[0]  109 us
    ppermute x11, starting transfers between devices, send(): return lax.ppermute(value[None], 'band', pairs)[0]  28.1 us
    pallas_call x6, Pallas kernels, pair_terms(): pl.pallas_call(functools.partial(pair_body, points, slot, has), grid=(2 *...  9.61 us
    pallas_call x1, Pallas kernels, copied(): pl.pallas_call(copy_body, grid=(X_STEPS,), in_specs=[pl.BlockSpec(memory_...  5.23 us
    select_n x1, other arithmetic, screened_kernel(): return jnp.where(inside, kernel / -float(points * points * points), 0.0)  4.48 us
    pallas_call x1, Pallas kernels, settle(): pl.pallas_call(settle_body, in_specs=[pl.BlockSpec(memory_space=pltpu.SME...  3.86 us
  transfers between devices with their start and end apart: 11, of which 4 were waited for; matrix products, arithmetic and copies ran while one was open for 4% of the time, Pallas kernels for 10%

profile of v3, /device:TPU:0, one launch (start us, length us, event | category | flops | bytes accessed | tf_op | source)
XLA Modules:
  0.0 165.0 jit_solution(2301176637956434091)
XLA Ops:
  0.0 7.6 %collective-permute-start.1 = (f32[1,96,9216]{2,1,0:T(8,128)}, f32[1,96,9216]{2,1,0:T(8,128)}, u32[]{:S(2)}, u32[]{:S(2)}) collective-permute-start(f32[1,96,9216]{2,1,0:T(8,128)} %param.4), channel_id=1, source_target_pairs={{8,14},{15,9},{9,11},{14,12},{7,1},{0,6},{6,4},{1,3},{24,30},{31,2... | collective-permute-start | bytes 10616840 | tf_op jit(solution)/shard_map/ppermute | solution.py:409
  7.6 2.5 %collective-permute-start = (f32[1,96,9216]{2,1,0:T(8,128)}, f32[1,96,9216]{2,1,0:T(8,128)}, u32[]{:S(2)}, u32[]{:S(2)}) collective-permute-start(f32[1,96,9216]{2,1,0:T(8,128)} %param.4), channel_id=1, source_target_pairs={{3,14},{4,9},{12,1},{11,6},{19,30},{20,25},{28,17},{27,22}} | collective-permute-start | bytes 10616840 | tf_op jit(solution)/shard_map/ppermute | solution.py:409
  10.1 1.2 dynamic-slice_bitcast_fusion.flags_ref.refs_0_
  11.4 0.1 broadcast_add_fusion
  11.4 4.5 %fusion.5.kernel_ref.refs_3_.refs_5_.refs_4_ = f32[96,96,128]{2,1,0:T(8,128)} fusion(f32[128]{0:T(128)S(1)} %fusion.12, f32[96,96]{1,0:T(8,128)S(1)} %broadcast_add_fusion, pred[128]{0:T(512)(128)(4,1)S(1)} %iota_compare_fusion), kind=kLoop, calls=%fused_computation.7 | loop fusion | flops 12976128 | bytes 4756096 | tf_op jit(solution)/shard_map/jit(_where)/select_n | solution.py:40
  15.9 5.2 %copied.1 = (f32[96,9216]{1,0:T(8,128)}, f32[96,9216]{1,0:T(8,128)}) custom-call(s32[13]{0:T(128)} %dynamic-slice_bitcast_fusion.flags_ref.refs_0_, f32[96,96,128]{2,1,0:T(8,128)} %fusion.5.kernel_ref.refs_3_.refs_5_.refs_4_, f32[96,9216]{1,0:T(8,128)} %bitcast.22), custom_call_target="tpu_custom_call" | custom-call | tf_op jit(solution)/shard_map/copied/pallas_call | solution.py:278
  21.2 24.0 %collective-permute-done.1 = f32[1,96,9216]{2,1,0:T(8,128)} collective-permute-done((f32[1,96,9216]{2,1,0:T(8,128)}, f32[1,96,9216]{2,1,0:T(8,128)}, u32[]{:S(2)}, u32[]{:S(2)}) %collective-permute-start.1) | collective-permute-done | bytes 3538976 | tf_op jit(solution)/shard_map/ppermute | solution.py:409
  45.2 3.1 %collective-permute-start.3 = (f32[1,96,9216]{2,1,0:T(8,128)}, f32[1,96,9216]{2,1,0:T(8,128)}, u32[]{:S(2)}, u32[]{:S(2)}) collective-permute-start(f32[1,96,9216]{2,1,0:T(8,128)} %bitcast.27), channel_id=1, source_target_pairs={{15,10},{8,13},{0,5},{7,2},{31,26},{24,29},{16,21},{23,18}} | collective-permute-start | bytes 10616840 | tf_op jit(solution)/shard_map/ppermute | solution.py:409
  48.3 0.0 collective-permute-done
  48.3 0.7 fusion.9
  49.0 0.6 collective-permute-start.2
  49.6 0.0 collective-permute-done.2
  49.6 0.0 copy-start
  49.6 0.6 copy-done
  50.2 1.5 gate.1
  51.8 2.5 %collective-permute-start.5 = (f32[1,96,9216]{2,1,0:T(8,128)}, f32[1,96,9216]{2,1,0:T(8,128)}, u32[]{:S(2)}, u32[]{:S(2)}) collective-permute-start(f32[1,96,9216]{2,1,0:T(8,128)} %bitcast.28), channel_id=1, source_target_pairs={{13,14},{10,9},{2,1},{5,6},{29,30},{26,25},{18,17},{21,22}} | collective-permute-start | bytes 10616840 | tf_op jit(solution)/shard_map/ppermute | solution.py:409
  54.2 2.5 %collective-permute-start.10 = (f32[1,96,9216]{2,1,0:T(8,128)}, f32[1,96,9216]{2,1,0:T(8,128)}, u32[]{:S(2)}, u32[]{:S(2)}) collective-permute-start(f32[1,96,9216]{2,1,0:T(8,128)} %bitcast.29), channel_id=1, source_target_pairs={{5,10},{2,13},{10,5},{13,2},{21,26},{18,29},{26,21},{29,18}} | collective-permute-start | bytes 10616840 | tf_op jit(solution)/shard_map/ppermute | solution.py:409
  56.7 1.5 pair_terms.6
  58.2 27.6 %collective-permute-done.3 = f32[1,96,9216]{2,1,0:T(8,128)} collective-permute-done((f32[1,96,9216]{2,1,0:T(8,128)}, f32[1,96,9216]{2,1,0:T(8,128)}, u32[]{:S(2)}, u32[]{:S(2)}) %collective-permute-start.3) | collective-permute-done | bytes 3538976 | tf_op jit(solution)/shard_map/ppermute | solution.py:409
  85.8 1.6 pair_terms.7
  87.4 2.5 %collective-permute-start.4 = (f32[1,96,9216]{2,1,0:T(8,128)}, f32[1,96,9216]{2,1,0:T(8,128)}, u32[]{:S(2)}, u32[]{:S(2)}) collective-permute-start(f32[1,96,9216]{2,1,0:T(8,128)} %bitcast.31), channel_id=1, source_target_pairs={{9,4},{14,3},{6,11},{1,12},{25,20},{30,19},{22,27},{17,28}} | collective-permute-start | bytes 10616840 | tf_op jit(solution)/shard_map/ppermute | solution.py:409
  89.9 2.5 %collective-permute-start.9 = (f32[1,96,9216]{2,1,0:T(8,128)}, f32[1,96,9216]{2,1,0:T(8,128)}, u32[]{:S(2)}, u32[]{:S(2)}) collective-permute-start(f32[1,96,9216]{2,1,0:T(8,128)} %bitcast.16), channel_id=1, source_target_pairs={{11,14},{12,9},{4,1},{3,6},{27,30},{28,25},{20,17},{19,22}} | collective-permute-start | bytes 10616840 | tf_op jit(solution)/shard_map/ppermute | solution.py:409
  92.4 0.0 collective-permute-done.5
  92.4 1.6 pair_terms.8
  94.0 1.8 %collective-permute-start.7 = (f32[1,40,9216]{2,1,0:T(8,128)}, f32[1,40,9216]{2,1,0:T(8,128)}, u32[]{:S(2)}, u32[]{:S(2)}) collective-permute-start(f32[1,40,9216]{2,1,0:T(8,128)} %bitcast.33), channel_id=1, source_target_pairs={{9,11},{14,12},{6,4},{1,3},{25,27},{30,28},{22,20},{17,19}} | collective-permute-start | bytes 4423688 | tf_op jit(solution)/shard_map/ppermute | solution.py:409
  95.8 1.3 collective-permute-start.6
  97.1 0.0 collective-permute-done.7
  97.1 1.3 collective-permute-start.8
  98.4 1.6 pair_terms.9.refs_3_
  99.9 0.0 collective-permute-done.10
  99.9 0.0 collective-permute-done.4
  100.0 1.6 pair_terms.10.refs_3_
  101.5 0.0 collective-permute-done.9
  101.5 1.8 %pair_terms.11.own_ref = f32[96,9216]{1,0:T(8,128)} custom-call(s32[13]{0:T(128)} %dynamic-slice_bitcast_fusion.flags_ref.refs_0_, f32[96,9216]{1,0:T(8,128)} %bitcast.26, f32[96,9216]{1,0:T(8,128)} %bitcast.17.refs_2_, f32[96,9216]{1,0:T(8,128)} %pair_terms.10.refs_3_, ...), custom_call_target="tpu_custom_call", output_to_operand_aliasing={{}: (3, {})} | custom-call | flops 100000000 | bytes 1000000 | tf_op jit(solution)/shard_map/pair_terms/pallas_call | solution.py:240
  103.3 54.6 %collective-permute-done.6 = f32[1,56,9216]{2,1,0:T(8,128)} collective-permute-done((f32[1,56,9216]{2,1,0:T(8,128)}, f32[1,56,9216]{2,1,0:T(8,128)}, u32[]{:S(2)}, u32[]{:S(2)}) %collective-permute-start.6) | collective-permute-done | bytes 2064416 | tf_op jit(solution)/shard_map/ppermute | solution.py:409
  157.9 3.0 %collective-permute-done.8 = f32[1,40,9216]{2,1,0:T(8,128)} collective-permute-done((f32[1,40,9216]{2,1,0:T(8,128)}, f32[1,40,9216]{2,1,0:T(8,128)}, u32[]{:S(2)}, u32[]{:S(2)}) %collective-permute-start.8) | collective-permute-done | bytes 1474592 | tf_op jit(solution)/shard_map/ppermute | solution.py:409
  160.9 3.9 %settle.1 = f32[96,9216]{1,0:T(8,128)} custom-call(s32[13]{0:T(128)} %dynamic-slice_bitcast_fusion.flags_ref.refs_0_, f32[96,9216]{1,0:T(8,128)} %bitcast.9.refs_4_.home_ref, f32[56,9216]{1,0:T(8,128)} %bitcast.13.top_ref, f32[40,9216]{1,0:T(8,128)} %bitcast.15.bottom_ref, f32[96,9216]{1,0:T(8,128)} %pair_terms.11.own_ref), custom_call_target="tpu_custom_call", output_to_operand_aliasing={{}: (4, {})} | custom-call | tf_op jit(solution)/shard_map/settle/pallas_call | solution.py:370
  (6 shorter events, 0.0 us)
Async XLA Ops:
  0.0 45.2 %collective-permute-start.1 = (f32[1,96,9216]{2,1,0:T(8,128)}, f32[1,96,9216]{2,1,0:T(8,128)}, u32[]{:S(2)}, u32[]{:S(2)}) collective-permute-start(f32[1,96,9216]{2,1,0:T(8,128)} %param.4), channel_id=1, source_target_pairs={{8,14},{15,9},{9,11},{14,12},{7,1},{0,6},{6,4},{1,3},{24,30},{31,2... | collective-permute-start | bytes 10616840 | tf_op jit(solution)/shard_map/ppermute | solution.py:409
  7.6 40.6 %collective-permute-start = (f32[1,96,9216]{2,1,0:T(8,128)}, f32[1,96,9216]{2,1,0:T(8,128)}, u32[]{:S(2)}, u32[]{:S(2)}) collective-permute-start(f32[1,96,9216]{2,1,0:T(8,128)} %param.4), channel_id=1, source_target_pairs={{3,14},{4,9},{12,1},{11,6},{19,30},{20,25},{28,17},{27,22}} | collective-permute-start | bytes 10616840 | tf_op jit(solution)/shard_map/ppermute | solution.py:409
  45.2 40.6 %collective-permute-start.3 = (f32[1,96,9216]{2,1,0:T(8,128)}, f32[1,96,9216]{2,1,0:T(8,128)}, u32[]{:S(2)}, u32[]{:S(2)}) collective-permute-start(f32[1,96,9216]{2,1,0:T(8,128)} %bitcast.27), channel_id=1, source_target_pairs={{15,10},{8,13},{0,5},{7,2},{31,26},{24,29},{16,21},{23,18}} | collective-permute-start | bytes 10616840 | tf_op jit(solution)/shard_map/ppermute | solution.py:409
  49.0 0.7 collective-permute-start.2
  49.6 0.6 copy-start
  51.8 40.6 %collective-permute-start.5 = (f32[1,96,9216]{2,1,0:T(8,128)}, f32[1,96,9216]{2,1,0:T(8,128)}, u32[]{:S(2)}, u32[]{:S(2)}) collective-permute-start(f32[1,96,9216]{2,1,0:T(8,128)} %bitcast.28), channel_id=1, source_target_pairs={{13,14},{10,9},{2,1},{5,6},{29,30},{26,25},{18,17},{21,22}} | collective-permute-start | bytes 10616840 | tf_op jit(solution)/shard_map/ppermute | solution.py:409
  54.2 45.7 %collective-permute-start.10 = (f32[1,96,9216]{2,1,0:T(8,128)}, f32[1,96,9216]{2,1,0:T(8,128)}, u32[]{:S(2)}, u32[]{:S(2)}) collective-permute-start(f32[1,96,9216]{2,1,0:T(8,128)} %bitcast.29), channel_id=1, source_target_pairs={{5,10},{2,13},{10,5},{13,2},{21,26},{18,29},{26,21},{29,18}} | collective-permute-start | bytes 10616840 | tf_op jit(solution)/shard_map/ppermute | solution.py:409
  87.4 12.5 %collective-permute-start.4 = (f32[1,96,9216]{2,1,0:T(8,128)}, f32[1,96,9216]{2,1,0:T(8,128)}, u32[]{:S(2)}, u32[]{:S(2)}) collective-permute-start(f32[1,96,9216]{2,1,0:T(8,128)} %bitcast.31), channel_id=1, source_target_pairs={{9,4},{14,3},{6,11},{1,12},{25,20},{30,19},{22,27},{17,28}} | collective-permute-start | bytes 10616840 | tf_op jit(solution)/shard_map/ppermute | solution.py:409
  89.9 11.6 %collective-permute-start.9 = (f32[1,96,9216]{2,1,0:T(8,128)}, f32[1,96,9216]{2,1,0:T(8,128)}, u32[]{:S(2)}, u32[]{:S(2)}) collective-permute-start(f32[1,96,9216]{2,1,0:T(8,128)} %bitcast.16), channel_id=1, source_target_pairs={{11,14},{12,9},{4,1},{3,6},{27,30},{28,25},{20,17},{19,22}} | collective-permute-start | bytes 10616840 | tf_op jit(solution)/shard_map/ppermute | solution.py:409
  94.0 3.1 %collective-permute-start.7 = (f32[1,40,9216]{2,1,0:T(8,128)}, f32[1,40,9216]{2,1,0:T(8,128)}, u32[]{:S(2)}, u32[]{:S(2)}) collective-permute-start(f32[1,40,9216]{2,1,0:T(8,128)} %bitcast.33), channel_id=1, source_target_pairs={{9,11},{14,12},{6,4},{1,3},{25,27},{30,28},{22,20},{17,19}} | collective-permute-start | bytes 4423688 | tf_op jit(solution)/shard_map/ppermute | solution.py:409
  95.8 62.2 %collective-permute-start.6 = (f32[1,56,9216]{2,1,0:T(8,128)}, f32[1,56,9216]{2,1,0:T(8,128)}, u32[]{:S(2)}, u32[]{:S(2)}) collective-permute-start(f32[1,56,9216]{2,1,0:T(8,128)} %bitcast.32), channel_id=1, source_target_pairs={{9,15},{14,8},{6,0},{1,7},{25,31},{30,24},{22,16},{17,23}} | collective-permute-start | bytes 6193160 | tf_op jit(solution)/shard_map/ppermute | solution.py:409
  97.1 63.9 %collective-permute-start.8 = (f32[1,40,9216]{2,1,0:T(8,128)}, f32[1,40,9216]{2,1,0:T(8,128)}, u32[]{:S(2)}, u32[]{:S(2)}) collective-permute-start(f32[1,40,9216]{2,1,0:T(8,128)} %collective-permute-done.7), channel_id=1, source_target_pairs={{11,15},{12,8},{4,0},{3,7},{27,31},{28,24},{20,16},{19,23}} | collective-permute-start | bytes 4423688 | tf_op jit(solution)/shard_map/ppermute | solution.py:409

commit v4 on v3

--- a/solution.py
+++ b/solution.py
@@ -75,23 +75,22 @@
     return out[:, :LANES] + out[:, LANES:]
 
 
-def pair_body(points, slot, has, *refs):
+def pair_body(points, slot, jobs, has, *refs):
     refs = list(refs)
     flags_ref = refs.pop(0)
-    names = ["a", "b"] + [name for name in ("sum_a", "sum_b") if name in has]
+    a_names = ["a%d" % job for job in range(jobs)]
+    names = a_names + ["b"] + ["sum_a"] * ("sum_a" in has)
     far = {name: refs.pop(0) for name in names}
     if "then" in has:
         refs.pop(0)
     kernel_ref, left_ref, right_ref = refs.pop(0), refs.pop(0), refs.pop(0)
-    out_refs = {"for_a": refs.pop(0)}
+    outs = ["for_a%d" % job for job in range(jobs)]
     if "halves" in has:
-        out_refs["low_a"] = refs.pop(0)
+        outs.append("low_a0")
     if "for_b" in has:
-        out_refs["for_b"] = refs.pop(0)
-    if "hand_on" in has:
-        refs.pop(0)
+        outs.append("for_b")
+    out_refs = {name: refs.pop(0) for name in outs}
     held, near, near_kernel, near_out, sems, kernel_sems, out_sems = refs
-    outs = list(out_refs)
     step = pl.program_id(0)
     active = flags_ref[2 * slot] == 1
     with_sum = flags_ref[2 * slot + 1] == 1
@@ -99,6 +98,9 @@
     ys = columns // points
     per_step = points // PLANE_STEPS
     late = X_STEPS + PLANE_STEPS
+    steps = late + X_STEPS
+    job = step // steps if jobs > 1 else 0
+    at = step % steps if jobs > 1 else step
 
     def span_of(chunk):
         start = chunk * columns
@@ -118,9 +120,9 @@
 
     def give(name, chunk):
         span = span_of(chunk)
-        source = near_out.at[0 if name != "for_b" else 1]
+        source = near_out.at[jobs if name == "for_b" else int(name[-1])]
         if "halves" in has and name != "for_b":
-            rows = pl.ds(points - FAR_ROWS, FAR_ROWS) if name == "low_a" else pl.ds(0, points - FAR_ROWS)
+            rows = pl.ds(points - FAR_ROWS, FAR_ROWS) if name == "low_a0" else pl.ds(0, points - FAR_ROWS)
             source = source.at[rows, span]
         else:
             source = source.at[:, span]
@@ -129,19 +131,24 @@
         )
 
     def here(name, chunk):
-        return near[names.index(name), :, span_of(chunk)]
-
-    sums = [name for name in names if name.startswith("sum")]
+        place = job if name == "a" else names.index(name)
+        return near[place, :, span_of(chunk)]
+
+    def when_job(number, work):
+        if jobs > 1:
+            pl.when(job == number)(work)
+        elif number == 0:
+            work()
 
     @pl.when(active & (step == 0))
     def start_first():
         for chunk in range(2):
-            for name in ("a", "b"):
+            for name in ("a0", "b"):
                 fetch(name, chunk).start()
 
     @pl.when(active & (step + 2 < X_STEPS))
     def start_next():
-        for name in ("a", "b"):
+        for name in ("a0", "b"):
             fetch(name, step + 2).start()
 
     @pl.when(active & (step == X_STEPS - 2))
@@ -149,12 +156,11 @@
         for part in range(PLANE_STEPS):
             fetch_kernel(part).start()
 
-    if sums:
-        @pl.when(active & (step == X_STEPS))
-        def start_sums():
-            for chunk in range(X_STEPS):
-                for name in sums:
-                    fetch(name, chunk).start()
+    @pl.when(active & (step == X_STEPS))
+    def start_rest():
+        for chunk in range(X_STEPS):
+            for name in a_names[1:] + ["sum_a"] * ("sum_a" in has):
+                fetch(name, chunk).start()
 
     def lanes_apart(block):
         tail = jnp.zeros((points, LANES), jnp.float32)
@@ -169,24 +175,31 @@
     def side_by_side(block):
         return jnp.concatenate([block[i] for i in range(per_step)], 1)
 
-    @pl.when(active & (step < X_STEPS))
+    @pl.when(active & (at < X_STEPS))
     def forward_x():
-        for name in ("a", "b"):
-            fetch(name, step).wait()
-        spectrum = from_left(left_ref[...], here("a", step) * here("b", step))
-        start = pl.multiple_of(step * ys, ys)
+        chunk = at
+
+        def first_waits():
+            fetch("a0", chunk).wait()
+            fetch("b", chunk).wait()
+
+        when_job(0, first_waits)
+        for number in range(1, jobs):
+            when_job(number, fetch(a_names[number], chunk).wait)
+        spectrum = from_left(left_ref[...], here("a", chunk) * here("b", chunk))
+        start = pl.multiple_of(chunk * ys, ys)
         held[:, pl.ds(start, ys), :] = lanes_apart(spectrum)
 
-    @pl.when(active & (step >= X_STEPS) & (step < late))
+    @pl.when(active & (at >= X_STEPS) & (at < late))
     def planes():
+        part = at - X_STEPS
         left = left_ref[...]
         right = right_ref[...]
-        part = step - X_STEPS
         first = part * per_step
+        when_job(0, lambda: fetch_kernel(part).wait())
         block = held[pl.ds(first, per_step)].reshape(per_step * points, LANES)
         block = from_right(block, right).reshape(per_step, points, LANES)
         wide = from_left(left, side_by_side(block))
-        fetch_kernel(part).wait()
         wide = from_left(left, wide * side_by_side(near_kernel[pl.ds(first, per_step)]))
         block = jnp.concatenate(
             [wide[:, i * LANES:(i + 1) * LANES] for i in range(per_step)], 0
@@ -194,27 +207,33 @@
         block = from_right(block, right)
         held[pl.ds(first, per_step)] = block.reshape(per_step, points, LANES)
 
-    @pl.when(active & (step >= late))
+    @pl.when(active & (at >= late))
     def inverse_x():
-        chunk = step - late
+        chunk = at - late
         start = pl.multiple_of(chunk * ys, ys)
-        for name in sums:
-            fetch(name, chunk).wait()
+        if "sum_a" in has:
+            fetch("sum_a", chunk).wait()
         block = lanes_together(held[:, pl.ds(start, ys), :])
         potential = from_left(left_ref[...], block)
         for_a = here("b", chunk) * potential
         if "sum_a" in has:
             for_a = for_a + jnp.where(with_sum, here("sum_a", chunk), 0.0)
-        near_out[0, :, span_of(chunk)] = for_a
+        near_out[job, :, span_of(chunk)] = for_a
         if "for_b" in has:
             for_b = here("a", chunk) * potential
-            if "sum_b" in has:
-                for_b = for_b + here("sum_b", chunk)
-            near_out[1, :, span_of(chunk)] = for_b
-        for name in outs:
-            give(name, chunk).start()
-
-    @pl.when(active & (step == late + X_STEPS - 1))
+            if jobs > 1:
+                for_b = for_b + jnp.where(job > 0, near_out[jobs, :, span_of(chunk)], 0.0)
+            near_out[jobs, :, span_of(chunk)] = for_b
+
+        def give_all(number):
+            for name in outs:
+                if number == (jobs - 1 if name == "for_b" else int(name[-1])):
+                    give(name, chunk).start()
+
+        for number in range(jobs):
+            when_job(number, functools.partial(give_all, number))
+
+    @pl.when(active & (step == jobs * steps - 1))
     def wait_outs():
         for chunk in range(X_STEPS):
             for name in outs:
@@ -222,37 +241,30 @@
 
 
 def pair_terms(
-    flags, slot, a, b, constants, sum_a=None, sum_b=None, for_b=False, halves=False, in_place=False, then=None, hand_on=False
+    flags, slot, a, b, constants, sum_a=None, for_b=False, halves=False, in_place=False, then=None
 ):
-    points, plane = a.shape
+    points, plane = b.shape
     kernel, left, right = constants
-    optional = {"sum_a": sum_a, "sum_b": sum_b}
-    optional = {name: value for name, value in optional.items() if value is not None}
-    blocks = [a, b, *optional.values()]
+    jobs = len(a)
+    blocks = [*a, b] + [sum_a] * (sum_a is not None)
     waited = [] if then is None else [then]
-    has = list(optional) + ["for_b"] * for_b + ["halves"] * halves + ["then"] * len(waited)
-    has += ["hand_on"] * hand_on
-    rows = ([points - FAR_ROWS, FAR_ROWS] if halves else [points]) + [points] * for_b
-    aliases = {3: 0} if in_place else {}
-    if hand_on:
-        aliases[1] = len(rows)
+    has = ["sum_a"] * (sum_a is not None) + ["for_b"] * for_b + ["halves"] * halves + ["then"] * len(waited)
+    rows = ([points - FAR_ROWS, FAR_ROWS] if halves else [points] * jobs) + [points] * for_b
     anywhere = pl.BlockSpec(memory_space=pl.ANY)
-    out = pl.pallas_call(
-        functools.partial(pair_body, points, slot, has),
-        grid=(2 * X_STEPS + PLANE_STEPS,),
+    return pl.pallas_call(
+        functools.partial(pair_body, points, slot, jobs, has),
+        grid=(jobs * (2 * X_STEPS + PLANE_STEPS),),
         in_specs=[pl.BlockSpec(memory_space=pltpu.SMEM)]
         + [anywhere] * (len(blocks) + len(waited) + 1)
         + [pl.BlockSpec(table.shape, lambda i: (0, 0)) for table in (left, right)],
-        out_specs=[anywhere] * (len(rows) + hand_on),
-        out_shape=[
-            jax.ShapeDtypeStruct((n, plane), jnp.float32) for n in rows + [points] * hand_on
-        ],
-        input_output_aliases=aliases,
+        out_specs=[anywhere] * len(rows),
+        out_shape=[jax.ShapeDtypeStruct((n, plane), jnp.float32) for n in rows],
+        input_output_aliases={3: 0} if in_place else {},
         scratch_shapes=[
             pltpu.VMEM((points, points, LANES), jnp.float32),
             pltpu.VMEM((len(blocks), points, plane), jnp.float32),
             pltpu.VMEM((points, points, LANES), jnp.float32),
-            pltpu.VMEM((2 if for_b else 1, points, plane), jnp.float32),
+            pltpu.VMEM((jobs + for_b, points, plane), jnp.float32),
             pltpu.SemaphoreType.DMA((len(blocks), X_STEPS)),
             pltpu.SemaphoreType.DMA((PLANE_STEPS,)),
             pltpu.SemaphoreType.DMA((len(rows), X_STEPS)),
@@ -263,7 +275,6 @@
         ),
         name="pair_terms",
     )(flags, *blocks, *waited, kernel, left, right)
-    return out if len(out) > 1 else out[0]
 
 
 def copy_body(flags_ref, kernel_ref, block_ref, first_ref, second_ref):
@@ -300,7 +311,7 @@
     anywhere = pl.BlockSpec(memory_space=pl.ANY)
     return pl.pallas_call(
         gate_body,
-        in_specs=[in_vmem, in_vmem, anywhere, anywhere],
+        in_specs=[anywhere, in_vmem, anywhere, anywhere],
         out_specs=[in_vmem, anywhere],
         out_shape=[
             jax.ShapeDtypeStruct(left.shape, left.dtype),
@@ -329,24 +340,22 @@
     )(block, *then)
 
 
-def settle_body(flags_ref, home_ref, top_ref, bottom_ref, own_ref, out_ref, near, sems):
-    del own_ref
+def settle_body(wanted, count, flags_ref, *refs):
+    parts, (out_ref, near, sems) = refs[:count], refs[count + 1:]
     columns = out_ref.shape[1] // SETTLE_STEPS
-    split = top_ref.shape[0]
-
-    def move(parts):
+
+    @pl.when(flags_ref[RESULT] == wanted)
+    def move():
         copies = []
         for i in range(SETTLE_STEPS):
             span = pl.ds(i * columns, columns)
-            for j, (source_ref, start) in enumerate(parts):
-                rows = pl.ds(start, source_ref.shape[0])
+            start = 0
+            for j, part in enumerate(parts):
+                rows = pl.ds(start, part.shape[0])
+                start += part.shape[0]
                 copies.append((
-                    pltpu.make_async_copy(
-                        source_ref.at[:, span], near.at[rows, span], sems.at[0, j, i]
-                    ),
-                    pltpu.make_async_copy(
-                        near.at[rows, span], out_ref.at[rows, span], sems.at[1, j, i]
-                    ),
+                    pltpu.make_async_copy(part.at[:, span], near.at[rows, span], sems.at[0, j, i]),
+                    pltpu.make_async_copy(near.at[rows, span], out_ref.at[rows, span], sems.at[1, j, i]),
                 ))
         for inward, outward in copies:
             inward.start()
@@ -356,30 +365,23 @@
         for inward, outward in copies:
             outward.wait()
 
-    @pl.when(flags_ref[RESULT] == 1)
-    def from_home():
-        move([(home_ref, 0)])
-
-    @pl.when(flags_ref[RESULT] == 2)
-    def from_far():
-        move([(top_ref, 0), (bottom_ref, split)])
-
-
-def settle(flags, home, top, bottom, own_sum):
+
+def settle(flags, wanted, parts, own_sum):
     anywhere = pl.BlockSpec(memory_space=pl.ANY)
+    count = len(parts)
     return pl.pallas_call(
-        settle_body,
-        in_specs=[pl.BlockSpec(memory_space=pltpu.SMEM)] + [anywhere] * 4,
+        functools.partial(settle_body, wanted, count),
+        in_specs=[pl.BlockSpec(memory_space=pltpu.SMEM)] + [anywhere] * (count + 1),
         out_specs=anywhere,
         out_shape=jax.ShapeDtypeStruct(own_sum.shape, own_sum.dtype),
-        input_output_aliases={4: 0},
+        input_output_aliases={count + 1: 0},
         scratch_shapes=[
             pltpu.VMEM(own_sum.shape, own_sum.dtype),
-            pltpu.SemaphoreType.DMA((2, 2, SETTLE_STEPS)),
+            pltpu.SemaphoreType.DMA((2, count, SETTLE_STEPS)),
         ],
         compiler_params=pltpu.CompilerParams(vmem_limit_bytes=63 * 2**20),
         name="settle",
-    )(flags, home, top, bottom, own_sum)
+    )(flags, *parts, own_sum)
 
 
 def both_halves(*pairs):
@@ -397,9 +399,9 @@
 HOME_FAR = both_halves((9, 15), (14, 8))
 HOME_TURN = both_halves((9, 11), (14, 12))
 HOME_TURNED = both_halves((11, 15), (12, 8))
-RESULT = 12
-FLAGS = {i: (1, 0, 1, 0, 1, 1, 0, 0, 0, 0, 1, 1, 0) for i in (9, 14, 6, 1)}
-FLAGS.update({i: (0, 0, 0, 0, 0, 0, 1, 0, 1, 1, 0, 0, 0) for i in (10, 13, 5, 2)})
+RESULT = 10
+FLAGS = {i: (1, 0, 1, 1, 0, 0, 0, 0, 1, 1, 0) for i in (9, 14, 6, 1)}
+FLAGS.update({i: (0, 0, 0, 0, 1, 0, 1, 1, 0, 0, 0) for i in (10, 13, 5, 2)})
 FLAGS.update({i: (0,) * RESULT + (1,) for i in (3, 4, 11, 12)})
 FLAGS.update({i: (0,) * RESULT + (2,) for i in (15, 8, 0, 7)})
 
@@ -424,19 +426,21 @@
     beside = send(held_back, BESIDE)
     single = send(held_back, SINGLES)
 
-    partner_sum, crossed_sum = pair(0, partner, crossed, constants, for_b=True)
-    own_sum, crossed_sum = pair(1, own, crossed, constants, sum_b=crossed_sum, for_b=True, then=direct)
+    partner_sum, own_sum, crossed_sum = pair(
+        0, [partner, own], crossed, constants, for_b=True, then=direct
+    )
     home = send(crossed_sum, HOME_ACROSS)
     partner = hold(partner, own_sum)
     turned = send(partner, TURNED)
-    top, bottom = pair(2, partner, beside, constants, sum_a=partner_sum, halves=True)
+    top, bottom = pair(1, [partner], beside, constants, sum_a=partner_sum, halves=True)
     bottom = send(bottom, HOME_TURN)
     top = send(top, HOME_FAR)
     bottom = send(bottom, HOME_TURNED)
-    own_sum = pair(3, own, direct, constants, sum_a=own_sum, in_place=True)
-    own_sum = pair(4, own, single, constants, sum_a=own_sum, in_place=True, then=home)
-    own_sum = pair(5, own, turned, constants, sum_a=own_sum, in_place=True)
-    return settle(flags, home, top, bottom, own_sum)[None]
+    (own_sum,) = pair(2, [own], direct, constants, sum_a=own_sum, in_place=True)
+    (own_sum,) = pair(3, [own], single, constants, sum_a=own_sum, in_place=True)
+    own_sum = settle(flags, 1, [home], own_sum)
+    (own_sum,) = pair(4, [own], turned, constants, sum_a=own_sum, in_place=True)
+    return settle(flags, 2, [top, bottom], own_sum)[None]
 
 
 def any_bands(orbitals, constants):
@@ -444,8 +448,8 @@
     flags = jnp.ones((4,), jnp.int32)
     lower = from_behind(orbitals, "band", OFFSET)[0]
     upper = from_behind(orbitals, "band", -OFFSET)[0]
-    total = pair_terms(flags, 0, own, lower, constants)
-    return pair_terms(flags, 1, own, upper, constants, sum_a=total)[None]
+    (total,) = pair_terms(flags, 0, [own], lower, constants)
+    return pair_terms(flags, 1, [own], upper, constants, sum_a=total)[0][None]
 
 
 def local(bands, orbitals):

time: 166 us -> 168 us (1.012)
  waiting for transfers between devices: 109 us -> 111 us
    ppermute x11, waiting for transfers between devices: 109 us -> 111 us  [send(): return lax.ppermute(value[None], 'band', pairs)[0]]
where the time goes in v4:
time: 168 us; the launch traced here: 167 us
  waiting for transfers between devices  111 us (66%)
  starting transfers between devices  28.3 us (17%)
  Pallas kernels  20.2 us (12%)
  other arithmetic  5.29 us (3%)
  local copies, waits for them, and re-layouts  1.84 us (1%)
    ppermute x11, waiting for transfers between devices, send(): return lax.ppermute(value[None], 'band', pairs)[0]  111 us
    ppermute x11, starting transfers between devices, send(): return lax.ppermute(value[None], 'band', pairs)[0]  28.3 us
    pallas_call x5, Pallas kernels, pair_terms(): pl.pallas_call(functools.partial(pair_body, points, slot, jobs, has), gri...  8.76 us
    pallas_call x1, Pallas kernels, copied(): pl.pallas_call(copy_body, grid=(X_STEPS,), in_specs=[pl.BlockSpec(memory_...  5.23 us
    pallas_call x2, Pallas kernels, settle(): pl.pallas_call(functools.partial(settle_body, wanted, count), in_specs=[p...  4.63 us
    select_n x1, other arithmetic, screened_kernel(): return jnp.where(inside, kernel / -float(points * points * points), 0.0)  4.49 us
  transfers between devices with their start and end apart: 11, of which 4 were waited for; matrix products, arithmetic and copies ran while one was open for 4% of the time, Pallas kernels for 10%

profile of v4, /device:TPU:0, one launch (start us, length us, event | category | flops | bytes accessed | tf_op | source)
XLA Modules:
  0.0 167.3 jit_solution(3987485676924029086)
XLA Ops:
  0.0 7.7 %collective-permute-start = (f32[1,96,9216]{2,1,0:T(8,128)}, f32[1,96,9216]{2,1,0:T(8,128)}, u32[]{:S(2)}, u32[]{:S(2)}) collective-permute-start(f32[1,96,9216]{2,1,0:T(8,128)} %param.4), channel_id=1, source_target_pairs={{8,14},{15,9},{9,11},{14,12},{7,1},{0,6},{6,4},{1,3},{24,30},{31,2... | collective-permute-start | bytes 10616840 | tf_op jit(solution)/shard_map/ppermute | solution.py:411
  7.7 2.5 %collective-permute-start.1 = (f32[1,96,9216]{2,1,0:T(8,128)}, f32[1,96,9216]{2,1,0:T(8,128)}, u32[]{:S(2)}, u32[]{:S(2)}) collective-permute-start(f32[1,96,9216]{2,1,0:T(8,128)} %param.4), channel_id=1, source_target_pairs={{3,14},{4,9},{12,1},{11,6},{19,30},{20,25},{28,17},{27,22}} | collective-permute-start | bytes 10616840 | tf_op jit(solution)/shard_map/ppermute | solution.py:411
  10.2 1.3 dynamic-slice_bitcast_fusion.flags_ref.refs_0_
  11.4 0.1 broadcast_add_fusion
  11.5 4.5 %fusion.5.kernel_ref.refs_5_.refs_4_ = f32[96,96,128]{2,1,0:T(8,128)} fusion(f32[128]{0:T(128)S(1)} %fusion.12, f32[96,96]{1,0:T(8,128)S(1)} %broadcast_add_fusion, pred[128]{0:T(512)(128)(4,1)S(1)} %iota_compare_fusion), kind=kLoop, calls=%fused_computation.7 | loop fusion | flops 12976128 | bytes 4756096 | tf_op jit(solution)/shard_map/jit(_where)/select_n | solution.py:40
  16.0 5.2 %copied.1 = (f32[96,9216]{1,0:T(8,128)}, f32[96,9216]{1,0:T(8,128)}) custom-call(s32[11]{0:T(128)} %dynamic-slice_bitcast_fusion.flags_ref.refs_0_, f32[96,96,128]{2,1,0:T(8,128)} %fusion.5.kernel_ref.refs_5_.refs_4_, f32[96,9216]{1,0:T(8,128)} %bitcast.22), custom_call_target="tpu_custom_call" | custom-call | tf_op jit(solution)/shard_map/copied/pallas_call | solution.py:289
  21.2 23.9 %collective-permute-done = f32[1,96,9216]{2,1,0:T(8,128)} collective-permute-done((f32[1,96,9216]{2,1,0:T(8,128)}, f32[1,96,9216]{2,1,0:T(8,128)}, u32[]{:S(2)}, u32[]{:S(2)}) %collective-permute-start) | collective-permute-done | bytes 3538976 | tf_op jit(solution)/shard_map/ppermute | solution.py:411
  45.2 3.1 %collective-permute-start.2 = (f32[1,96,9216]{2,1,0:T(8,128)}, f32[1,96,9216]{2,1,0:T(8,128)}, u32[]{:S(2)}, u32[]{:S(2)}) collective-permute-start(f32[1,96,9216]{2,1,0:T(8,128)} %bitcast.27), channel_id=1, source_target_pairs={{15,10},{8,13},{0,5},{7,2},{31,26},{24,29},{16,21},{23,18}} | collective-permute-start | bytes 10616840 | tf_op jit(solution)/shard_map/ppermute | solution.py:411
  48.3 0.0 collective-permute-done.1
  48.3 0.7 fusion.9
  49.0 0.6 collective-permute-start.3
  49.6 0.0 collective-permute-done.3
  49.6 0.0 copy-start
  49.6 0.6 copy-done
  50.2 1.5 gate.1
  51.8 2.4 %collective-permute-start.4 = (f32[1,96,9216]{2,1,0:T(8,128)}, f32[1,96,9216]{2,1,0:T(8,128)}, u32[]{:S(2)}, u32[]{:S(2)}) collective-permute-start(f32[1,96,9216]{2,1,0:T(8,128)} %bitcast.28), channel_id=1, source_target_pairs={{13,14},{10,9},{2,1},{5,6},{29,30},{26,25},{18,17},{21,22}} | collective-permute-start | bytes 10616840 | tf_op jit(solution)/shard_map/ppermute | solution.py:411
  54.2 2.5 %collective-permute-start.10 = (f32[1,96,9216]{2,1,0:T(8,128)}, f32[1,96,9216]{2,1,0:T(8,128)}, u32[]{:S(2)}, u32[]{:S(2)}) collective-permute-start(f32[1,96,9216]{2,1,0:T(8,128)} %bitcast.29), channel_id=1, source_target_pairs={{5,10},{2,13},{10,5},{13,2},{21,26},{18,29},{26,21},{29,18}} | collective-permute-start | bytes 10616840 | tf_op jit(solution)/shard_map/ppermute | solution.py:411
  56.7 29.2 %collective-permute-done.2 = f32[1,96,9216]{2,1,0:T(8,128)} collective-permute-done((f32[1,96,9216]{2,1,0:T(8,128)}, f32[1,96,9216]{2,1,0:T(8,128)}, u32[]{:S(2)}, u32[]{:S(2)}) %collective-permute-start.2) | collective-permute-done | bytes 3538976 | tf_op jit(solution)/shard_map/ppermute | solution.py:411
  85.8 2.3 %pair_terms.5 = (f32[96,9216]{1,0:T(8,128)}, f32[96,9216]{1,0:T(8,128)}, f32[96,9216]{1,0:T(8,128)}) custom-call(s32[11]{0:T(128)} %dynamic-slice_bitcast_fusion.flags_ref.refs_0_, f32[96,9216]{1,0:T(8,128)} %bitcast.1.refs_1_.refs_0_, f32[96,9216]{1,0:T(8,128)} %bitcast.23, f32[96,9216]{1,0:T(8,128)} %bitcast.3.refs_3_, f32[96,9216]{1,0:T(8,128)} %bitcast.5.refs_4_.refs_2_, ...), custom_call_target="tpu_custom_call" | custom-call | flops 100000000 | bytes 1000000 | tf_op jit(solution)/shard_map/pair_terms/pallas_call | solution.py:254
  88.1 2.5 %collective-permute-start.9 = (f32[1,96,9216]{2,1,0:T(8,128)}, f32[1,96,9216]{2,1,0:T(8,128)}, u32[]{:S(2)}, u32[]{:S(2)}) collective-permute-start(f32[1,96,9216]{2,1,0:T(8,128)} %bitcast.31), channel_id=1, source_target_pairs={{9,4},{14,3},{6,11},{1,12},{25,20},{30,19},{22,27},{17,28}} | collective-permute-start | bytes 10616840 | tf_op jit(solution)/shard_map/ppermute | solution.py:411
  90.6 2.5 %collective-permute-start.8 = (f32[1,96,9216]{2,1,0:T(8,128)}, f32[1,96,9216]{2,1,0:T(8,128)}, u32[]{:S(2)}, u32[]{:S(2)}) collective-permute-start(f32[1,96,9216]{2,1,0:T(8,128)} %bitcast.14), channel_id=1, source_target_pairs={{11,14},{12,9},{4,1},{3,6},{27,30},{28,25},{20,17},{19,22}} | collective-permute-start | bytes 10616840 | tf_op jit(solution)/shard_map/ppermute | solution.py:411
  93.1 0.0 collective-permute-done.4
  93.1 1.6 pair_terms.6
  94.7 1.8 %collective-permute-start.6 = (f32[1,40,9216]{2,1,0:T(8,128)}, f32[1,40,9216]{2,1,0:T(8,128)}, u32[]{:S(2)}, u32[]{:S(2)}) collective-permute-start(f32[1,40,9216]{2,1,0:T(8,128)} %bitcast.33), channel_id=1, source_target_pairs={{9,11},{14,12},{6,4},{1,3},{25,27},{30,28},{22,20},{17,19}} | collective-permute-start | bytes 4423688 | tf_op jit(solution)/shard_map/ppermute | solution.py:411
  96.5 1.3 collective-permute-start.5
  97.8 0.0 collective-permute-done.6
  97.8 1.5 collective-permute-start.7
  99.2 1.6 pair_terms.7.refs_3_
  100.8 0.0 collective-permute-done.10
  100.8 1.6 pair_terms.8.refs_1_
  102.4 0.0 collective-permute-done.9
  102.4 0.8 settle.2.refs_3_
  103.2 0.0 collective-permute-done.8
  103.2 1.8 %pair_terms.9.refs_2_ = f32[96,9216]{1,0:T(8,128)} custom-call(s32[11]{0:T(128)} %dynamic-slice_bitcast_fusion.flags_ref.refs_0_, f32[96,9216]{1,0:T(8,128)} %bitcast.26, f32[96,9216]{1,0:T(8,128)} %bitcast.15.refs_2_, f32[96,9216]{1,0:T(8,128)} %settle.2.refs_3_, f32[96,96,128]{2,1,0:T(8,128)} %fusion.5.kernel_ref.refs_5_.refs_4_, ...), custom_call_target="tpu_custom_call", output_to_operand_aliasing={{}: (3, {})} | custom-call | flops 100000000 | bytes 1000000 | tf_op jit(solution)/shard_map/pair_terms/pallas_call | solution.py:254
  105.0 49.4 %collective-permute-done.5 = f32[1,56,9216]{2,1,0:T(8,128)} collective-permute-done((f32[1,56,9216]{2,1,0:T(8,128)}, f32[1,56,9216]{2,1,0:T(8,128)}, u32[]{:S(2)}, u32[]{:S(2)}) %collective-permute-start.5) | collective-permute-done | bytes 2064416 | tf_op jit(solution)/shard_map/ppermute | solution.py:411
  154.4 8.9 %collective-permute-done.7 = f32[1,40,9216]{2,1,0:T(8,128)} collective-permute-done((f32[1,40,9216]{2,1,0:T(8,128)}, f32[1,40,9216]{2,1,0:T(8,128)}, u32[]{:S(2)}, u32[]{:S(2)}) %collective-permute-start.7) | collective-permute-done | bytes 1474592 | tf_op jit(solution)/shard_map/ppermute | solution.py:411
  163.3 3.8 %settle.3 = f32[96,9216]{1,0:T(8,128)} custom-call(s32[11]{0:T(128)} %dynamic-slice_bitcast_fusion.flags_ref.refs_0_, f32[56,9216]{1,0:T(8,128)} %bitcast.11.refs_0_, f32[40,9216]{1,0:T(8,128)} %bitcast.13.refs_1_, f32[96,9216]{1,0:T(8,128)} %pair_terms.9.refs_2_), custom_call_target="tpu_custom_call", output_to_operand_aliasing={{}: (3, {})} | custom-call | tf_op jit(solution)/shard_map/settle/pallas_call | solution.py:372
  (6 shorter events, 0.0 us)
Async XLA Ops:
  0.0 45.2 %collective-permute-start = (f32[1,96,9216]{2,1,0:T(8,128)}, f32[1,96,9216]{2,1,0:T(8,128)}, u32[]{:S(2)}, u32[]{:S(2)}) collective-permute-start(f32[1,96,9216]{2,1,0:T(8,128)} %param.4), channel_id=1, source_target_pairs={{8,14},{15,9},{9,11},{14,12},{7,1},{0,6},{6,4},{1,3},{24,30},{31,2... | collective-permute-start | bytes 10616840 | tf_op jit(solution)/shard_map/ppermute | solution.py:411
  7.7 40.6 %collective-permute-start.1 = (f32[1,96,9216]{2,1,0:T(8,128)}, f32[1,96,9216]{2,1,0:T(8,128)}, u32[]{:S(2)}, u32[]{:S(2)}) collective-permute-start(f32[1,96,9216]{2,1,0:T(8,128)} %param.4), channel_id=1, source_target_pairs={{3,14},{4,9},{12,1},{11,6},{19,30},{20,25},{28,17},{27,22}} | collective-permute-start | bytes 10616840 | tf_op jit(solution)/shard_map/ppermute | solution.py:411
  45.2 40.6 %collective-permute-start.2 = (f32[1,96,9216]{2,1,0:T(8,128)}, f32[1,96,9216]{2,1,0:T(8,128)}, u32[]{:S(2)}, u32[]{:S(2)}) collective-permute-start(f32[1,96,9216]{2,1,0:T(8,128)} %bitcast.27), channel_id=1, source_target_pairs={{15,10},{8,13},{0,5},{7,2},{31,26},{24,29},{16,21},{23,18}} | collective-permute-start | bytes 10616840 | tf_op jit(solution)/shard_map/ppermute | solution.py:411
  49.0 0.7 collective-permute-start.3
  49.6 0.6 copy-start
  51.8 41.3 %collective-permute-start.4 = (f32[1,96,9216]{2,1,0:T(8,128)}, f32[1,96,9216]{2,1,0:T(8,128)}, u32[]{:S(2)}, u32[]{:S(2)}) collective-permute-start(f32[1,96,9216]{2,1,0:T(8,128)} %bitcast.28), channel_id=1, source_target_pairs={{13,14},{10,9},{2,1},{5,6},{29,30},{26,25},{18,17},{21,22}} | collective-permute-start | bytes 10616840 | tf_op jit(solution)/shard_map/ppermute | solution.py:411
  54.2 46.6 %collective-permute-start.10 = (f32[1,96,9216]{2,1,0:T(8,128)}, f32[1,96,9216]{2,1,0:T(8,128)}, u32[]{:S(2)}, u32[]{:S(2)}) collective-permute-start(f32[1,96,9216]{2,1,0:T(8,128)} %bitcast.29), channel_id=1, source_target_pairs={{5,10},{2,13},{10,5},{13,2},{21,26},{18,29},{26,21},{29,18}} | collective-permute-start | bytes 10616840 | tf_op jit(solution)/shard_map/ppermute | solution.py:411
  88.1 14.3 %collective-permute-start.9 = (f32[1,96,9216]{2,1,0:T(8,128)}, f32[1,96,9216]{2,1,0:T(8,128)}, u32[]{:S(2)}, u32[]{:S(2)}) collective-permute-start(f32[1,96,9216]{2,1,0:T(8,128)} %bitcast.31), channel_id=1, source_target_pairs={{9,4},{14,3},{6,11},{1,12},{25,20},{30,19},{22,27},{17,28}} | collective-permute-start | bytes 10616840 | tf_op jit(solution)/shard_map/ppermute | solution.py:411
  90.6 12.6 %collective-permute-start.8 = (f32[1,96,9216]{2,1,0:T(8,128)}, f32[1,96,9216]{2,1,0:T(8,128)}, u32[]{:S(2)}, u32[]{:S(2)}) collective-permute-start(f32[1,96,9216]{2,1,0:T(8,128)} %bitcast.14), channel_id=1, source_target_pairs={{11,14},{12,9},{4,1},{3,6},{27,30},{28,25},{20,17},{19,22}} | collective-permute-start | bytes 10616840 | tf_op jit(solution)/shard_map/ppermute | solution.py:411
  94.7 3.1 %collective-permute-start.6 = (f32[1,40,9216]{2,1,0:T(8,128)}, f32[1,40,9216]{2,1,0:T(8,128)}, u32[]{:S(2)}, u32[]{:S(2)}) collective-permute-start(f32[1,40,9216]{2,1,0:T(8,128)} %bitcast.33), channel_id=1, source_target_pairs={{9,11},{14,12},{6,4},{1,3},{25,27},{30,28},{22,20},{17,19}} | collective-permute-start | bytes 4423688 | tf_op jit(solution)/shard_map/ppermute | solution.py:411
  96.5 57.9 %collective-permute-start.5 = (f32[1,56,9216]{2,1,0:T(8,128)}, f32[1,56,9216]{2,1,0:T(8,128)}, u32[]{:S(2)}, u32[]{:S(2)}) collective-permute-start(f32[1,56,9216]{2,1,0:T(8,128)} %bitcast.32), channel_id=1, source_target_pairs={{9,15},{14,8},{6,0},{1,7},{25,31},{30,24},{22,16},{17,23}} | collective-permute-start | bytes 6193160 | tf_op jit(solution)/shard_map/ppermute | solution.py:411
  97.8 65.5 %collective-permute-start.7 = (f32[1,40,9216]{2,1,0:T(8,128)}, f32[1,40,9216]{2,1,0:T(8,128)}, u32[]{:S(2)}, u32[]{:S(2)}) collective-permute-start(f32[1,40,9216]{2,1,0:T(8,128)} %collective-permute-done.6), channel_id=1, source_target_pairs={{11,15},{12,8},{4,0},{3,7},{27,31},{28,24},{20,16},{19,23}} | collective-permute-start | bytes 4423688 | tf_op jit(solution)/shard_map/ppermute | solution.py:411

commit v5 on v4

--- a/solution.py
+++ b/solution.py
@@ -15,7 +15,7 @@
 X_STEPS = 3
 PLANE_STEPS = 2
 SETTLE_STEPS = 6
-FAR_ROWS = 40
+FAR_ROWS = 32
 
 
 def from_behind(value, axis, by):
@@ -301,23 +301,21 @@
     )(flags, kernel, block)
 
 
-def gate_body(token_ref, left_ref, partner_ref, block_ref, new_left_ref, new_block_ref):
-    del token_ref, partner_ref, block_ref, new_block_ref
-    new_left_ref[...] = left_ref[...]
+def gate_body(*refs):
+    del refs
 
 
 def gate(token, left, partner, block):
-    in_vmem = pl.BlockSpec(memory_space=pltpu.VMEM)
     anywhere = pl.BlockSpec(memory_space=pl.ANY)
     return pl.pallas_call(
         gate_body,
-        in_specs=[anywhere, in_vmem, anywhere, anywhere],
-        out_specs=[in_vmem, anywhere],
+        in_specs=[anywhere] * 4,
+        out_specs=[anywhere] * 2,
         out_shape=[
             jax.ShapeDtypeStruct(left.shape, left.dtype),
             jax.ShapeDtypeStruct(block.shape, block.dtype),
         ],
-        input_output_aliases={3: 1},
+        input_output_aliases={1: 0, 3: 1},
         compiler_params=pltpu.CompilerParams(vmem_limit_bytes=63 * 2**20),
         name="gate",
     )(token, left, partner, block)
@@ -435,9 +433,9 @@
     top, bottom = pair(1, [partner], beside, constants, sum_a=partner_sum, halves=True)
     bottom = send(bottom, HOME_TURN)
     top = send(top, HOME_FAR)
-    bottom = send(bottom, HOME_TURNED)
     (own_sum,) = pair(2, [own], direct, constants, sum_a=own_sum, in_place=True)
     (own_sum,) = pair(3, [own], single, constants, sum_a=own_sum, in_place=True)
+    bottom = send(hold(bottom, own_sum), HOME_TURNED)
     own_sum = settle(flags, 1, [home], own_sum)
     (own_sum,) = pair(4, [own], turned, constants, sum_a=own_sum, in_place=True)
     return settle(flags, 2, [top, bottom], own_sum)[None]

time: 168 us -> 161 us (0.958)
  waiting for transfers between devices: 111 us -> 105 us
  Pallas kernels: 20.2 us -> 18.3 us
    ppermute x11, waiting for transfers between devices: 111 us -> 105 us  [send(): return lax.ppermute(value[None], 'band', pairs)[0]]
  transfers between devices with their start and end apart: 11 -> 11, of which waited for: 4 -> 3; matrix products, arithmetic and copies ran while one was open for 4% -> 4% of each run, Pallas kernels for 10% -> 9%
where the time goes in v5:
time: 161 us; the launch traced here: 160 us
  waiting for transfers between devices  105 us (65%)
  starting transfers between devices  28.5 us (18%)
  Pallas kernels  18.3 us (11%)
  other arithmetic  5.26 us (3%)
  local copies, waits for them, and re-layouts  2.46 us (2%)
    ppermute x11, waiting for transfers between devices, send(): return lax.ppermute(value[None], 'band', pairs)[0]  105 us
    ppermute x11, starting transfers between devices, send(): return lax.ppermute(value[None], 'band', pairs)[0]  28.5 us
    pallas_call x5, Pallas kernels, pair_terms(): pl.pallas_call(functools.partial(pair_body, points, slot, jobs, has), gri...  8.54 us
    pallas_call x1, Pallas kernels, copied(): pl.pallas_call(copy_body, grid=(X_STEPS,), in_specs=[pl.BlockSpec(memory_...  5.23 us
    pallas_call x2, Pallas kernels, settle(): pl.pallas_call(functools.partial(settle_body, wanted, count), in_specs=[p...  4.53 us
    select_n x1, other arithmetic, screened_kernel(): return jnp.where(inside, kernel / -float(points * points * points), 0.0)  4.48 us
  transfers between devices with their start and end apart: 11, of which 3 were waited for; matrix products, arithmetic and copies ran while one was open for 4% of the time, Pallas kernels for 9%

profile of v5, /device:TPU:0, one launch (start us, length us, event | category | flops | bytes accessed | tf_op | source)
XLA Modules:
  0.0 160.1 jit_solution(4715240007859862371)
XLA Ops:
  0.0 7.7 %collective-permute-start = (f32[1,96,9216]{2,1,0:T(8,128)}, f32[1,96,9216]{2,1,0:T(8,128)}, u32[]{:S(2)}, u32[]{:S(2)}) collective-permute-start(f32[1,96,9216]{2,1,0:T(8,128)} %param.4), channel_id=1, source_target_pairs={{8,14},{15,9},{9,11},{14,12},{7,1},{0,6},{6,4},{1,3},{24,30},{31,2... | collective-permute-start | bytes 10616840 | tf_op jit(solution)/shard_map/ppermute | solution.py:409
  7.7 2.4 %collective-permute-start.1 = (f32[1,96,9216]{2,1,0:T(8,128)}, f32[1,96,9216]{2,1,0:T(8,128)}, u32[]{:S(2)}, u32[]{:S(2)}) collective-permute-start(f32[1,96,9216]{2,1,0:T(8,128)} %param.4), channel_id=1, source_target_pairs={{3,14},{4,9},{12,1},{11,6},{19,30},{20,25},{28,17},{27,22}} | collective-permute-start | bytes 10616840 | tf_op jit(solution)/shard_map/ppermute | solution.py:409
  10.1 1.2 dynamic-slice_bitcast_fusion.flags_ref.refs_0_
  11.4 0.1 broadcast_add_fusion
  11.4 4.5 %fusion.5.kernel_ref.refs_5_.refs_4_ = f32[96,96,128]{2,1,0:T(8,128)} fusion(f32[128]{0:T(128)S(1)} %fusion.12, f32[96,96]{1,0:T(8,128)S(1)} %broadcast_add_fusion, pred[128]{0:T(512)(128)(4,1)S(1)} %iota_compare_fusion), kind=kLoop, calls=%fused_computation.7 | loop fusion | flops 12976128 | bytes 4756096 | tf_op jit(solution)/shard_map/jit(_where)/select_n | solution.py:40
  15.9 5.2 %copied.1 = (f32[96,9216]{1,0:T(8,128)}, f32[96,9216]{1,0:T(8,128)}) custom-call(s32[11]{0:T(128)} %dynamic-slice_bitcast_fusion.flags_ref.refs_0_, f32[96,96,128]{2,1,0:T(8,128)} %fusion.5.kernel_ref.refs_5_.refs_4_, f32[96,9216]{1,0:T(8,128)} %bitcast.24), custom_call_target="tpu_custom_call" | custom-call | tf_op jit(solution)/shard_map/copied/pallas_call | solution.py:289
  21.2 24.0 %collective-permute-done = f32[1,96,9216]{2,1,0:T(8,128)} collective-permute-done((f32[1,96,9216]{2,1,0:T(8,128)}, f32[1,96,9216]{2,1,0:T(8,128)}, u32[]{:S(2)}, u32[]{:S(2)}) %collective-permute-start) | collective-permute-done | bytes 3538976 | tf_op jit(solution)/shard_map/ppermute | solution.py:409
  45.2 0.0 copy-start
  45.2 3.2 %collective-permute-start.2 = (f32[1,96,9216]{2,1,0:T(8,128)}, f32[1,96,9216]{2,1,0:T(8,128)}, u32[]{:S(2)}, u32[]{:S(2)}) collective-permute-start(f32[1,96,9216]{2,1,0:T(8,128)} %bitcast.29), channel_id=1, source_target_pairs={{15,10},{8,13},{0,5},{7,2},{31,26},{24,29},{16,21},{23,18}} | collective-permute-start | bytes 10616840 | tf_op jit(solution)/shard_map/ppermute | solution.py:409
  48.4 0.0 collective-permute-done.1
  48.4 0.7 fusion.9
  49.1 0.7 collective-permute-start.3
  49.7 0.0 copy-done
  49.7 0.6 copy.26.refs_1_
  50.4 0.0 collective-permute-done.3
  50.4 0.0 copy-start.1
  50.4 0.6 copy-done.1
  51.0 2.5 %collective-permute-start.4 = (f32[1,96,9216]{2,1,0:T(8,128)}, f32[1,96,9216]{2,1,0:T(8,128)}, u32[]{:S(2)}, u32[]{:S(2)}) collective-permute-start(f32[1,96,9216]{2,1,0:T(8,128)} %bitcast.30), channel_id=1, source_target_pairs={{13,14},{10,9},{2,1},{5,6},{29,30},{26,25},{18,17},{21,22}} | collective-permute-start | bytes 10616840 | tf_op jit(solution)/shard_map/ppermute | solution.py:409
  53.4 2.5 %collective-permute-start.7 = (f32[1,96,9216]{2,1,0:T(8,128)}, f32[1,96,9216]{2,1,0:T(8,128)}, u32[]{:S(2)}, u32[]{:S(2)}) collective-permute-start(f32[1,96,9216]{2,1,0:T(8,128)} %bitcast.31), channel_id=1, source_target_pairs={{5,10},{2,13},{10,5},{13,2},{21,26},{18,29},{26,21},{29,18}} | collective-permute-start | bytes 10616840 | tf_op jit(solution)/shard_map/ppermute | solution.py:409
  55.9 30.0 %collective-permute-done.2 = f32[1,96,9216]{2,1,0:T(8,128)} collective-permute-done((f32[1,96,9216]{2,1,0:T(8,128)}, f32[1,96,9216]{2,1,0:T(8,128)}, u32[]{:S(2)}, u32[]{:S(2)}) %collective-permute-start.2) | collective-permute-done | bytes 3538976 | tf_op jit(solution)/shard_map/ppermute | solution.py:409
  85.9 2.3 %pair_terms.5 = (f32[96,9216]{1,0:T(8,128)}, f32[96,9216]{1,0:T(8,128)}, f32[96,9216]{1,0:T(8,128)}) custom-call(s32[11]{0:T(128)} %dynamic-slice_bitcast_fusion.flags_ref.refs_0_, f32[96,9216]{1,0:T(8,128)} %bitcast.1.refs_1_.refs_0_, f32[96,9216]{1,0:T(8,128)} %bitcast.25, f32[96,9216]{1,0:T(8,128)} %bitcast.3.refs_3_, f32[96,9216]{1,0:T(8,128)} %bitcast.5.refs_4_.refs_2_, ...), custom_call_target="tpu_custom_call" | custom-call | flops 100000000 | bytes 1000000 | tf_op jit(solution)/shard_map/pair_terms/pallas_call | solution.py:254
  88.2 2.5 %collective-permute-start.10 = (f32[1,96,9216]{2,1,0:T(8,128)}, f32[1,96,9216]{2,1,0:T(8,128)}, u32[]{:S(2)}, u32[]{:S(2)}) collective-permute-start(f32[1,96,9216]{2,1,0:T(8,128)} %bitcast.33), channel_id=1, source_target_pairs={{9,4},{14,3},{6,11},{1,12},{25,20},{30,19},{22,27},{17,28}} | collective-permute-start | bytes 10616840 | tf_op jit(solution)/shard_map/ppermute | solution.py:409
  90.7 2.4 %collective-permute-start.9 = (f32[1,96,9216]{2,1,0:T(8,128)}, f32[1,96,9216]{2,1,0:T(8,128)}, u32[]{:S(2)}, u32[]{:S(2)}) collective-permute-start(f32[1,96,9216]{2,1,0:T(8,128)} %bitcast.17), channel_id=1, source_target_pairs={{11,14},{12,9},{4,1},{3,6},{27,30},{28,25},{20,17},{19,22}} | collective-permute-start | bytes 10616840 | tf_op jit(solution)/shard_map/ppermute | solution.py:409
  93.1 0.0 collective-permute-done.4
  93.1 1.6 pair_terms.6
  94.7 1.7 %collective-permute-start.6 = (f32[1,32,9216]{2,1,0:T(8,128)}, f32[1,32,9216]{2,1,0:T(8,128)}, u32[]{:S(2)}, u32[]{:S(2)}) collective-permute-start(f32[1,32,9216]{2,1,0:T(8,128)} %bitcast.35), channel_id=1, source_target_pairs={{9,11},{14,12},{6,4},{1,3},{25,27},{30,28},{22,20},{17,19}} | collective-permute-start | bytes 3538952 | tf_op jit(solution)/shard_map/ppermute | solution.py:409
  96.5 1.5 collective-permute-start.5
  97.9 1.6 pair_terms.7.refs_3_
  99.5 0.0 collective-permute-done.7
  99.5 1.6 pair_terms.8.refs_1_
  101.1 0.0 collective-permute-done.6
  101.1 1.5 collective-permute-start.8
  102.6 0.0 collective-permute-done.10
  102.6 0.8 settle.2.refs_3_
  103.4 0.0 collective-permute-done.9
  103.4 1.6 pair_terms.9.refs_2_
  105.0 51.2 %collective-permute-done.8 = f32[1,32,9216]{2,1,0:T(8,128)} collective-permute-done((f32[1,32,9216]{2,1,0:T(8,128)}, f32[1,32,9216]{2,1,0:T(8,128)}, u32[]{:S(2)}, u32[]{:S(2)}) %collective-permute-start.8) | collective-permute-done | bytes 1179680 | tf_op jit(solution)/shard_map/ppermute | solution.py:409
  156.2 0.0 collective-permute-done.5
  156.2 3.7 %settle.3 = f32[96,9216]{1,0:T(8,128)} custom-call(s32[11]{0:T(128)} %dynamic-slice_bitcast_fusion.flags_ref.refs_0_, f32[64,9216]{1,0:T(8,128)} %bitcast.11.refs_0_, f32[32,9216]{1,0:T(8,128)} %bitcast.16.refs_1_, f32[96,9216]{1,0:T(8,128)} %pair_terms.9.refs_2_), custom_call_target="tpu_custom_call", output_to_operand_aliasing={{}: (3, {})} | custom-call | tf_op jit(solution)/shard_map/settle/pallas_call | solution.py:370
  (8 shorter events, 0.0 us)
Async XLA Ops:
  0.0 45.2 %collective-permute-start = (f32[1,96,9216]{2,1,0:T(8,128)}, f32[1,96,9216]{2,1,0:T(8,128)}, u32[]{:S(2)}, u32[]{:S(2)}) collective-permute-start(f32[1,96,9216]{2,1,0:T(8,128)} %param.4), channel_id=1, source_target_pairs={{8,14},{15,9},{9,11},{14,12},{7,1},{0,6},{6,4},{1,3},{24,30},{31,2... | collective-permute-start | bytes 10616840 | tf_op jit(solution)/shard_map/ppermute | solution.py:409
  7.7 40.7 %collective-permute-start.1 = (f32[1,96,9216]{2,1,0:T(8,128)}, f32[1,96,9216]{2,1,0:T(8,128)}, u32[]{:S(2)}, u32[]{:S(2)}) collective-permute-start(f32[1,96,9216]{2,1,0:T(8,128)} %param.4), channel_id=1, source_target_pairs={{3,14},{4,9},{12,1},{11,6},{19,30},{20,25},{28,17},{27,22}} | collective-permute-start | bytes 10616840 | tf_op jit(solution)/shard_map/ppermute | solution.py:409
  45.2 4.6 %copy-start = (bf16[192,192]{1,0:T(8,128)(2,1)S(1)}, bf16[192,192]{1,0:T(8,128)(2,1)}, u32[]{:S(2)}) copy-start(bf16[192,192]{1,0:T(8,128)(2,1)} %constant.37.clone) | copy-start | bytes 221188
  45.2 40.8 %collective-permute-start.2 = (f32[1,96,9216]{2,1,0:T(8,128)}, f32[1,96,9216]{2,1,0:T(8,128)}, u32[]{:S(2)}, u32[]{:S(2)}) collective-permute-start(f32[1,96,9216]{2,1,0:T(8,128)} %bitcast.29), channel_id=1, source_target_pairs={{15,10},{8,13},{0,5},{7,2},{31,26},{24,29},{16,21},{23,18}} | collective-permute-start | bytes 10616840 | tf_op jit(solution)/shard_map/ppermute | solution.py:409
  49.1 1.3 collective-permute-start.3
  50.4 0.6 copy-start.1
  51.0 42.1 %collective-permute-start.4 = (f32[1,96,9216]{2,1,0:T(8,128)}, f32[1,96,9216]{2,1,0:T(8,128)}, u32[]{:S(2)}, u32[]{:S(2)}) collective-permute-start(f32[1,96,9216]{2,1,0:T(8,128)} %bitcast.30), channel_id=1, source_target_pairs={{13,14},{10,9},{2,1},{5,6},{29,30},{26,25},{18,17},{21,22}} | collective-permute-start | bytes 10616840 | tf_op jit(solution)/shard_map/ppermute | solution.py:409
  53.4 46.1 %collective-permute-start.7 = (f32[1,96,9216]{2,1,0:T(8,128)}, f32[1,96,9216]{2,1,0:T(8,128)}, u32[]{:S(2)}, u32[]{:S(2)}) collective-permute-start(f32[1,96,9216]{2,1,0:T(8,128)} %bitcast.31), channel_id=1, source_target_pairs={{5,10},{2,13},{10,5},{13,2},{21,26},{18,29},{26,21},{29,18}} | collective-permute-start | bytes 10616840 | tf_op jit(solution)/shard_map/ppermute | solution.py:409
  88.2 14.4 %collective-permute-start.10 = (f32[1,96,9216]{2,1,0:T(8,128)}, f32[1,96,9216]{2,1,0:T(8,128)}, u32[]{:S(2)}, u32[]{:S(2)}) collective-permute-start(f32[1,96,9216]{2,1,0:T(8,128)} %bitcast.33), channel_id=1, source_target_pairs={{9,4},{14,3},{6,11},{1,12},{25,20},{30,19},{22,27},{17,28}} | collective-permute-start | bytes 10616840 | tf_op jit(solution)/shard_map/ppermute | solution.py:409
  90.7 12.7 %collective-permute-start.9 = (f32[1,96,9216]{2,1,0:T(8,128)}, f32[1,96,9216]{2,1,0:T(8,128)}, u32[]{:S(2)}, u32[]{:S(2)}) collective-permute-start(f32[1,96,9216]{2,1,0:T(8,128)} %bitcast.17), channel_id=1, source_target_pairs={{11,14},{12,9},{4,1},{3,6},{27,30},{28,25},{20,17},{19,22}} | collective-permute-start | bytes 10616840 | tf_op jit(solution)/shard_map/ppermute | solution.py:409
  94.7 6.4 %collective-permute-start.6 = (f32[1,32,9216]{2,1,0:T(8,128)}, f32[1,32,9216]{2,1,0:T(8,128)}, u32[]{:S(2)}, u32[]{:S(2)}) collective-permute-start(f32[1,32,9216]{2,1,0:T(8,128)} %bitcast.35), channel_id=1, source_target_pairs={{9,11},{14,12},{6,4},{1,3},{25,27},{30,28},{22,20},{17,19}} | collective-permute-start | bytes 3538952 | tf_op jit(solution)/shard_map/ppermute | solution.py:409
  96.5 59.8 %collective-permute-start.5 = (f32[1,64,9216]{2,1,0:T(8,128)}, f32[1,64,9216]{2,1,0:T(8,128)}, u32[]{:S(2)}, u32[]{:S(2)}) collective-permute-start(f32[1,64,9216]{2,1,0:T(8,128)} %bitcast.34), channel_id=1, source_target_pairs={{9,15},{14,8},{6,0},{1,7},{25,31},{30,24},{22,16},{17,23}} | collective-permute-start | bytes 7077896 | tf_op jit(solution)/shard_map/ppermute | solution.py:409
  101.1 55.1 %collective-permute-start.8 = (f32[1,32,9216]{2,1,0:T(8,128)}, f32[1,32,9216]{2,1,0:T(8,128)}, u32[]{:S(2)}, u32[]{:S(2)}) collective-permute-start(f32[1,32,9216]{2,1,0:T(8,128)} %bitcast.15), channel_id=1, source_target_pairs={{11,15},{12,8},{4,0},{3,7},{27,31},{28,24},{20,16},{19,23}} | collective-permute-start | bytes 3538952 | tf_op jit(solution)/shard_map/ppermute | solution.py:409

commit v6 on v5

--- a/solution.py
+++ b/solution.py
@@ -277,13 +277,13 @@
     )(flags, *blocks, *waited, kernel, left, right)
 
 
-def copy_body(flags_ref, kernel_ref, block_ref, first_ref, second_ref):
-    del flags_ref, kernel_ref
+def copy_body(flags_ref, kernel_ref, left_ref, right_ref, block_ref, first_ref, second_ref):
+    del flags_ref, kernel_ref, left_ref, right_ref
     first_ref[...] = block_ref[...]
     second_ref[...] = block_ref[...]
 
 
-def copied(flags, kernel, block):
+def copied(flags, constants, block):
     points, plane = block.shape
     part = pl.BlockSpec((points, plane // X_STEPS), lambda i: (0, i))
     return pl.pallas_call(
@@ -291,34 +291,34 @@
         grid=(X_STEPS,),
         in_specs=[
             pl.BlockSpec(memory_space=pltpu.SMEM),
-            pl.BlockSpec(memory_space=pl.ANY),
+            *[pl.BlockSpec(memory_space=pl.ANY)] * 3,
             part,
         ],
         out_specs=[part, part],
         out_shape=[jax.ShapeDtypeStruct(block.shape, block.dtype)] * 2,
         compiler_params=pltpu.CompilerParams(vmem_limit_bytes=63 * 2**20),
         name="copied",
-    )(flags, kernel, block)
+    )(flags, *constants, block)
 
 
 def gate_body(*refs):
     del refs
 
 
-def gate(token, left, partner, block):
+def gate(token, kernel, partner, block):
     anywhere = pl.BlockSpec(memory_space=pl.ANY)
     return pl.pallas_call(
         gate_body,
         in_specs=[anywhere] * 4,
         out_specs=[anywhere] * 2,
         out_shape=[
-            jax.ShapeDtypeStruct(left.shape, left.dtype),
+            jax.ShapeDtypeStruct(kernel.shape, kernel.dtype),
             jax.ShapeDtypeStruct(block.shape, block.dtype),
         ],
         input_output_aliases={1: 0, 3: 1},
         compiler_params=pltpu.CompilerParams(vmem_limit_bytes=63 * 2**20),
         name="gate",
-    )(token, left, partner, block)
+    )(token, kernel, partner, block)
 
 
 def hold_body(*refs):
@@ -415,22 +415,22 @@
     pair = functools.partial(pair_terms, flags)
     crossed = send(own, CROSSING)
     partner = send(own, PARTNERS)
-    own_copy, direct_copy = copied(flags, kernel, own)
+    own_copy, direct_copy = copied(flags, constants, own)
     token = crossed[:8, :LANES] + own_copy[:8, :LANES]
     direct_copy = hold(direct_copy, partner)
     direct = send(direct_copy, DIRECT)
-    left, held_back = gate(send(token, ARRIVED), left, direct_copy, own_copy)
+    kernel, held_back = gate(send(token, ARRIVED), kernel, direct_copy, own_copy)
     constants = (kernel, left, right)
     beside = send(held_back, BESIDE)
     single = send(held_back, SINGLES)
 
     partner_sum, own_sum, crossed_sum = pair(
-        0, [partner, own], crossed, constants, for_b=True, then=direct
+        0, [partner, own], crossed, constants, for_b=True
     )
     home = send(crossed_sum, HOME_ACROSS)
     partner = hold(partner, own_sum)
     turned = send(partner, TURNED)
-    top, bottom = pair(1, [partner], beside, constants, sum_a=partner_sum, halves=True)
+    top, bottom = pair(1, [partner], beside, constants, sum_a=partner_sum, halves=True, then=direct)
     bottom = send(bottom, HOME_TURN)
     top = send(top, HOME_FAR)
     (own_sum,) = pair(2, [own], direct, constants, sum_a=own_sum, in_place=True)

time: 161 us -> 159 us (0.988)
  transfers between devices with their start and end apart: 11 -> 11, of which waited for: 3 -> 4; matrix products, arithmetic and copies ran while one was open for 4% -> 4% of each run, Pallas kernels for 9% -> 9%
where the time goes in v6:
time: 159 us
  waiting for transfers between devices  106 us (67%)
  starting transfers between devices  27.2 us (17%)
  Pallas kernels  18.3 us (12%)
  other arithmetic  5.27 us (3%)
  local copies, waits for them, and re-layouts  1.83 us (1%)
    ppermute x11, waiting for transfers between devices, send(): return lax.ppermute(value[None], 'band', pairs)[0]  106 us
    ppermute x11, starting transfers between devices, send(): return lax.ppermute(value[None], 'band', pairs)[0]  27.2 us
    pallas_call x5, Pallas kernels, pair_terms(): pl.pallas_call(functools.partial(pair_body, points, slot, jobs, has), gri...  8.54 us
    pallas_call x1, Pallas kernels, copied(): pl.pallas_call(copy_body, grid=(X_STEPS,), in_specs=[pl.BlockSpec(memory_...  5.22 us
    pallas_call x2, Pallas kernels, settle(): pl.pallas_call(functools.partial(settle_body, wanted, count), in_specs=[p...  4.53 us
    select_n x1, other arithmetic, screened_kernel(): return jnp.where(inside, kernel / -float(points * points * points), 0.0)  4.49 us
  transfers between devices with their start and end apart: 11, of which 4 were waited for; matrix products, arithmetic and copies ran while one was open for 4% of the time, Pallas kernels for 9%

profile of v6, /device:TPU:0, one launch (start us, length us, event | category | flops | bytes accessed | tf_op | source)
XLA Modules:
  0.0 158.7 jit_solution(675738608131136573)
XLA Ops:
  0.0 2.4 %collective-permute-start.1 = (f32[1,96,9216]{2,1,0:T(8,128)}, f32[1,96,9216]{2,1,0:T(8,128)}, u32[]{:S(2)}, u32[]{:S(2)}) collective-permute-start(f32[1,96,9216]{2,1,0:T(8,128)} %param.4), channel_id=1, source_target_pairs={{3,14},{4,9},{12,1},{11,6},{19,30},{20,25},{28,17},{27,22}} | collective-permute-start | bytes 10616840 | tf_op jit(solution)/shard_map/ppermute | solution.py:409
  2.4 6.6 %collective-permute-start = (f32[1,96,9216]{2,1,0:T(8,128)}, f32[1,96,9216]{2,1,0:T(8,128)}, u32[]{:S(2)}, u32[]{:S(2)}) collective-permute-start(f32[1,96,9216]{2,1,0:T(8,128)} %param.4), channel_id=1, source_target_pairs={{8,14},{15,9},{9,11},{14,12},{7,1},{0,6},{6,4},{1,3},{24,30},{31,2... | collective-permute-start | bytes 10616840 | tf_op jit(solution)/shard_map/ppermute | solution.py:409
  9.0 1.2 dynamic-slice_bitcast_fusion.flags_ref.refs_0_
  10.3 0.1 broadcast_add_fusion
  10.3 4.5 %fusion.5.kernel_ref.refs_1_ = f32[96,96,128]{2,1,0:T(8,128)} fusion(f32[128]{0:T(128)S(1)} %fusion.12, f32[96,96]{1,0:T(8,128)S(1)} %broadcast_add_fusion, pred[128]{0:T(512)(128)(4,1)S(1)} %iota_compare_fusion), kind=kLoop, calls=%fused_computation.7 | loop fusion | flops 12976128 | bytes 4756096 | tf_op jit(solution)/shard_map/jit(_where)/select_n | solution.py:40
  14.8 5.2 %copied.1 = (f32[96,9216]{1,0:T(8,128)}, f32[96,9216]{1,0:T(8,128)}) custom-call(s32[11]{0:T(128)} %dynamic-slice_bitcast_fusion.flags_ref.refs_0_, f32[96,96,128]{2,1,0:T(8,128)} %fusion.5.kernel_ref.refs_1_, bf16[192,192]{1,0:T(8,128)(2,1)} %constant.37.clone.left_ref.refs_5_.refs_6_, bf16[256,256]{1,0:T(8,128)(2,1)} %constant.38.clone.right_ref.refs_6_.refs_7_, ...), custom_call_target="tpu_custom_call" | custom-call | tf_op jit(solution)/shard_map/copied/pallas_call | solution.py:289
  20.0 0.0 collective-permute-done.1
  20.0 0.7 fusion.9
  20.7 0.6 collective-permute-start.2
  21.4 25.1 %collective-permute-done = f32[1,96,9216]{2,1,0:T(8,128)} collective-permute-done((f32[1,96,9216]{2,1,0:T(8,128)}, f32[1,96,9216]{2,1,0:T(8,128)}, u32[]{:S(2)}, u32[]{:S(2)}) %collective-permute-start) | collective-permute-done | bytes 3538976 | tf_op jit(solution)/shard_map/ppermute | solution.py:409
  46.5 3.1 %collective-permute-start.4 = (f32[1,96,9216]{2,1,0:T(8,128)}, f32[1,96,9216]{2,1,0:T(8,128)}, u32[]{:S(2)}, u32[]{:S(2)}) collective-permute-start(f32[1,96,9216]{2,1,0:T(8,128)} %bitcast.29), channel_id=1, source_target_pairs={{15,10},{8,13},{0,5},{7,2},{31,26},{24,29},{16,21},{23,18}} | collective-permute-start | bytes 10616840 | tf_op jit(solution)/shard_map/ppermute | solution.py:409
  49.6 0.0 collective-permute-done.2
  49.6 0.0 copy-start
  49.6 0.6 copy-done
  50.2 2.4 %collective-permute-start.3 = (f32[1,96,9216]{2,1,0:T(8,128)}, f32[1,96,9216]{2,1,0:T(8,128)}, u32[]{:S(2)}, u32[]{:S(2)}) collective-permute-start(f32[1,96,9216]{2,1,0:T(8,128)} %bitcast.30), channel_id=1, source_target_pairs={{13,14},{10,9},{2,1},{5,6},{29,30},{26,25},{18,17},{21,22}} | collective-permute-start | bytes 10616840 | tf_op jit(solution)/shard_map/ppermute | solution.py:409
  52.6 2.5 %collective-permute-start.7 = (f32[1,96,9216]{2,1,0:T(8,128)}, f32[1,96,9216]{2,1,0:T(8,128)}, u32[]{:S(2)}, u32[]{:S(2)}) collective-permute-start(f32[1,96,9216]{2,1,0:T(8,128)} %bitcast.31), channel_id=1, source_target_pairs={{5,10},{2,13},{10,5},{13,2},{21,26},{18,29},{26,21},{29,18}} | collective-permute-start | bytes 10616840 | tf_op jit(solution)/shard_map/ppermute | solution.py:409
  55.1 2.3 %pair_terms.5 = (f32[96,9216]{1,0:T(8,128)}, f32[96,9216]{1,0:T(8,128)}, f32[96,9216]{1,0:T(8,128)}) custom-call(s32[11]{0:T(128)} %dynamic-slice_bitcast_fusion.flags_ref.refs_0_, f32[96,9216]{1,0:T(8,128)} %bitcast.1.refs_1_.refs_0_, f32[96,9216]{1,0:T(8,128)} %bitcast.25, f32[96,9216]{1,0:T(8,128)} %bitcast.3.refs_3_, ...), custom_call_target="tpu_custom_call" | custom-call | flops 100000000 | bytes 1000000 | tf_op jit(solution)/shard_map/pair_terms/pallas_call | solution.py:254
  57.4 2.5 %collective-permute-start.10 = (f32[1,96,9216]{2,1,0:T(8,128)}, f32[1,96,9216]{2,1,0:T(8,128)}, u32[]{:S(2)}, u32[]{:S(2)}) collective-permute-start(f32[1,96,9216]{2,1,0:T(8,128)} %bitcast.33), channel_id=1, source_target_pairs={{9,4},{14,3},{6,11},{1,12},{25,20},{30,19},{22,27},{17,28}} | collective-permute-start | bytes 10616840 | tf_op jit(solution)/shard_map/ppermute | solution.py:409
  59.8 2.4 %collective-permute-start.9 = (f32[1,96,9216]{2,1,0:T(8,128)}, f32[1,96,9216]{2,1,0:T(8,128)}, u32[]{:S(2)}, u32[]{:S(2)}) collective-permute-start(f32[1,96,9216]{2,1,0:T(8,128)} %bitcast.17), channel_id=1, source_target_pairs={{11,14},{12,9},{4,1},{3,6},{27,30},{28,25},{20,17},{19,22}} | collective-permute-start | bytes 10616840 | tf_op jit(solution)/shard_map/ppermute | solution.py:409
  62.3 24.8 %collective-permute-done.4 = f32[1,96,9216]{2,1,0:T(8,128)} collective-permute-done((f32[1,96,9216]{2,1,0:T(8,128)}, f32[1,96,9216]{2,1,0:T(8,128)}, u32[]{:S(2)}, u32[]{:S(2)}) %collective-permute-start.4) | collective-permute-done | bytes 3538976 | tf_op jit(solution)/shard_map/ppermute | solution.py:409
  87.1 0.0 collective-permute-done.3
  87.1 1.6 %pair_terms.6 = (f32[64,9216]{1,0:T(8,128)}, f32[32,9216]{1,0:T(8,128)}) custom-call(s32[11]{0:T(128)} %dynamic-slice_bitcast_fusion.flags_ref.refs_0_, f32[96,9216]{1,0:T(8,128)} %hold.4.refs_1_, f32[96,9216]{1,0:T(8,128)} %bitcast.7.refs_2_, f32[96,9216]{1,0:T(8,128)} %get-tuple-element.19.refs_3_, f32[96,9216]{1,0:T(8,128)} %bitcast.9.refs_4_.refs_2_, ...), custom_call_target="tpu_custom_call" | custom-call | flops 100000000 | bytes 1000000 | tf_op jit(solution)/shard_map/pair_terms/pallas_call | solution.py:254
  88.7 1.7 %collective-permute-start.6 = (f32[1,32,9216]{2,1,0:T(8,128)}, f32[1,32,9216]{2,1,0:T(8,128)}, u32[]{:S(2)}, u32[]{:S(2)}) collective-permute-start(f32[1,32,9216]{2,1,0:T(8,128)} %bitcast.35), channel_id=1, source_target_pairs={{9,11},{14,12},{6,4},{1,3},{25,27},{30,28},{22,20},{17,19}} | collective-permute-start | bytes 3538952 | tf_op jit(solution)/shard_map/ppermute | solution.py:409
  90.4 1.5 collective-permute-start.5
  91.9 1.6 pair_terms.7.refs_3_
  93.4 0.0 collective-permute-done.7
  93.4 1.6 pair_terms.8.refs_1_
  95.0 0.0 collective-permute-done.6
  95.0 1.5 collective-permute-start.8
  96.6 0.0 collective-permute-done.10
  96.6 0.8 settle.2.refs_3_
  97.4 0.0 collective-permute-done.9
  97.4 1.6 pair_terms.9.refs_2_
  98.9 55.6 %collective-permute-done.8 = f32[1,32,9216]{2,1,0:T(8,128)} collective-permute-done((f32[1,32,9216]{2,1,0:T(8,128)}, f32[1,32,9216]{2,1,0:T(8,128)}, u32[]{:S(2)}, u32[]{:S(2)}) %collective-permute-start.8) | collective-permute-done | bytes 1179680 | tf_op jit(solution)/shard_map/ppermute | solution.py:409
  154.5 0.2 collective-permute-done.5
  154.8 3.7 %settle.3 = f32[96,9216]{1,0:T(8,128)} custom-call(s32[11]{0:T(128)} %dynamic-slice_bitcast_fusion.flags_ref.refs_0_, f32[64,9216]{1,0:T(8,128)} %bitcast.11.refs_0_, f32[32,9216]{1,0:T(8,128)} %bitcast.16.refs_1_, f32[96,9216]{1,0:T(8,128)} %pair_terms.9.refs_2_), custom_call_target="tpu_custom_call", output_to_operand_aliasing={{}: (3, {})} | custom-call | tf_op jit(solution)/shard_map/settle/pallas_call | solution.py:370
  (8 shorter events, 0.0 us)
Async XLA Ops:
  0.0 20.0 %collective-permute-start.1 = (f32[1,96,9216]{2,1,0:T(8,128)}, f32[1,96,9216]{2,1,0:T(8,128)}, u32[]{:S(2)}, u32[]{:S(2)}) collective-permute-start(f32[1,96,9216]{2,1,0:T(8,128)} %param.4), channel_id=1, source_target_pairs={{3,14},{4,9},{12,1},{11,6},{19,30},{20,25},{28,17},{27,22}} | collective-permute-start | bytes 10616840 | tf_op jit(solution)/shard_map/ppermute | solution.py:409
  2.4 44.1 %collective-permute-start = (f32[1,96,9216]{2,1,0:T(8,128)}, f32[1,96,9216]{2,1,0:T(8,128)}, u32[]{:S(2)}, u32[]{:S(2)}) collective-permute-start(f32[1,96,9216]{2,1,0:T(8,128)} %param.4), channel_id=1, source_target_pairs={{8,14},{15,9},{9,11},{14,12},{7,1},{0,6},{6,4},{1,3},{24,30},{31,2... | collective-permute-start | bytes 10616840 | tf_op jit(solution)/shard_map/ppermute | solution.py:409
  20.7 28.8 %collective-permute-start.2 = (f32[1,8,128]{2,1,0:T(8,128)S(1)}, f32[1,8,128]{2,1,0:T(8,128)S(1)}, u32[]{:S(2)}, u32[]{:S(2)}) collective-permute-start(f32[1,8,128]{2,1,0:T(8,128)S(1)} %fusion.9), channel_id=1, source_target_pairs={{14,2},{9,5},{1,13},{6,10},{30,18},{25,21},{17,29},{22,26}} | collective-permute-start | bytes 12296 | tf_op jit(solution)/shard_map/ppermute | solution.py:409
  46.5 40.6 %collective-permute-start.4 = (f32[1,96,9216]{2,1,0:T(8,128)}, f32[1,96,9216]{2,1,0:T(8,128)}, u32[]{:S(2)}, u32[]{:S(2)}) collective-permute-start(f32[1,96,9216]{2,1,0:T(8,128)} %bitcast.29), channel_id=1, source_target_pairs={{15,10},{8,13},{0,5},{7,2},{31,26},{24,29},{16,21},{23,18}} | collective-permute-start | bytes 10616840 | tf_op jit(solution)/shard_map/ppermute | solution.py:409
  49.6 0.6 copy-start
  50.2 36.9 %collective-permute-start.3 = (f32[1,96,9216]{2,1,0:T(8,128)}, f32[1,96,9216]{2,1,0:T(8,128)}, u32[]{:S(2)}, u32[]{:S(2)}) collective-permute-start(f32[1,96,9216]{2,1,0:T(8,128)} %bitcast.30), channel_id=1, source_target_pairs={{13,14},{10,9},{2,1},{5,6},{29,30},{26,25},{18,17},{21,22}} | collective-permute-start | bytes 10616840 | tf_op jit(solution)/shard_map/ppermute | solution.py:409
  52.6 40.8 %collective-permute-start.7 = (f32[1,96,9216]{2,1,0:T(8,128)}, f32[1,96,9216]{2,1,0:T(8,128)}, u32[]{:S(2)}, u32[]{:S(2)}) collective-permute-start(f32[1,96,9216]{2,1,0:T(8,128)} %bitcast.31), channel_id=1, source_target_pairs={{5,10},{2,13},{10,5},{13,2},{21,26},{18,29},{26,21},{29,18}} | collective-permute-start | bytes 10616840 | tf_op jit(solution)/shard_map/ppermute | solution.py:409
  57.4 39.2 %collective-permute-start.10 = (f32[1,96,9216]{2,1,0:T(8,128)}, f32[1,96,9216]{2,1,0:T(8,128)}, u32[]{:S(2)}, u32[]{:S(2)}) collective-permute-start(f32[1,96,9216]{2,1,0:T(8,128)} %bitcast.33), channel_id=1, source_target_pairs={{9,4},{14,3},{6,11},{1,12},{25,20},{30,19},{22,27},{17,28}} | collective-permute-start | bytes 10616840 | tf_op jit(solution)/shard_map/ppermute | solution.py:409
  59.8 37.5 %collective-permute-start.9 = (f32[1,96,9216]{2,1,0:T(8,128)}, f32[1,96,9216]{2,1,0:T(8,128)}, u32[]{:S(2)}, u32[]{:S(2)}) collective-permute-start(f32[1,96,9216]{2,1,0:T(8,128)} %bitcast.17), channel_id=1, source_target_pairs={{11,14},{12,9},{4,1},{3,6},{27,30},{28,25},{20,17},{19,22}} | collective-permute-start | bytes 10616840 | tf_op jit(solution)/shard_map/ppermute | solution.py:409
  88.7 6.3 %collective-permute-start.6 = (f32[1,32,9216]{2,1,0:T(8,128)}, f32[1,32,9216]{2,1,0:T(8,128)}, u32[]{:S(2)}, u32[]{:S(2)}) collective-permute-start(f32[1,32,9216]{2,1,0:T(8,128)} %bitcast.35), channel_id=1, source_target_pairs={{9,11},{14,12},{6,4},{1,3},{25,27},{30,28},{22,20},{17,19}} | collective-permute-start | bytes 3538952 | tf_op jit(solution)/shard_map/ppermute | solution.py:409
  90.4 64.4 %collective-permute-start.5 = (f32[1,64,9216]{2,1,0:T(8,128)}, f32[1,64,9216]{2,1,0:T(8,128)}, u32[]{:S(2)}, u32[]{:S(2)}) collective-permute-start(f32[1,64,9216]{2,1,0:T(8,128)} %bitcast.34), channel_id=1, source_target_pairs={{9,15},{14,8},{6,0},{1,7},{25,31},{30,24},{22,16},{17,23}} | collective-permute-start | bytes 7077896 | tf_op jit(solution)/shard_map/ppermute | solution.py:409
  95.0 59.5 %collective-permute-start.8 = (f32[1,32,9216]{2,1,0:T(8,128)}, f32[1,32,9216]{2,1,0:T(8,128)}, u32[]{:S(2)}, u32[]{:S(2)}) collective-permute-start(f32[1,32,9216]{2,1,0:T(8,128)} %bitcast.15), channel_id=1, source_target_pairs={{11,15},{12,8},{4,0},{3,7},{27,31},{28,24},{20,16},{19,23}} | collective-permute-start | bytes 3538952 | tf_op jit(solution)/shard_map/ppermute | solution.py:409

commit v7 on v6

--- a/solution.py
+++ b/solution.py
@@ -13,7 +13,6 @@
 screening = 5.44
 LANES = 128
 X_STEPS = 3
-PLANE_STEPS = 2
 SETTLE_STEPS = 6
 FAR_ROWS = 32
 
@@ -75,7 +74,7 @@
     return out[:, :LANES] + out[:, LANES:]
 
 
-def pair_body(points, slot, jobs, has, *refs):
+def pair_body(points, slot, jobs, plane_steps, has, *refs):
     refs = list(refs)
     flags_ref = refs.pop(0)
     a_names = ["a%d" % job for job in range(jobs)]
@@ -96,8 +95,8 @@
     with_sum = flags_ref[2 * slot + 1] == 1
     columns = near.shape[2] // X_STEPS
     ys = columns // points
-    per_step = points // PLANE_STEPS
-    late = X_STEPS + PLANE_STEPS
+    per_step = points // plane_steps
+    late = X_STEPS + plane_steps
     steps = late + X_STEPS
     job = step // steps if jobs > 1 else 0
     at = step % steps if jobs > 1 else step
@@ -151,9 +150,9 @@
         for name in ("a0", "b"):
             fetch(name, step + 2).start()
 
-    @pl.when(active & (step == X_STEPS - 2))
+    @pl.when(active & (step == 0))
     def start_kernel():
-        for part in range(PLANE_STEPS):
+        for part in range(plane_steps):
             fetch_kernel(part).start()
 
     @pl.when(active & (step == X_STEPS))
@@ -241,7 +240,8 @@
 
 
 def pair_terms(
-    flags, slot, a, b, constants, sum_a=None, for_b=False, halves=False, in_place=False, then=None
+    flags, slot, a, b, constants, sum_a=None, for_b=False, halves=False, in_place=False, then=None,
+    plane_steps=2,
 ):
     points, plane = b.shape
     kernel, left, right = constants
@@ -252,8 +252,8 @@
     rows = ([points - FAR_ROWS, FAR_ROWS] if halves else [points] * jobs) + [points] * for_b
     anywhere = pl.BlockSpec(memory_space=pl.ANY)
     return pl.pallas_call(
-        functools.partial(pair_body, points, slot, jobs, has),
-        grid=(jobs * (2 * X_STEPS + PLANE_STEPS),),
+        functools.partial(pair_body, points, slot, jobs, plane_steps, has),
+        grid=(jobs * (2 * X_STEPS + plane_steps),),
         in_specs=[pl.BlockSpec(memory_space=pltpu.SMEM)]
         + [anywhere] * (len(blocks) + len(waited) + 1)
         + [pl.BlockSpec(table.shape, lambda i: (0, 0)) for table in (left, right)],
@@ -266,7 +266,7 @@
             pltpu.VMEM((points, points, LANES), jnp.float32),
             pltpu.VMEM((jobs + for_b, points, plane), jnp.float32),
             pltpu.SemaphoreType.DMA((len(blocks), X_STEPS)),
-            pltpu.SemaphoreType.DMA((PLANE_STEPS,)),
+            pltpu.SemaphoreType.DMA((plane_steps,)),
             pltpu.SemaphoreType.DMA((len(rows), X_STEPS)),
         ],
         compiler_params=pltpu.CompilerParams(vmem_limit_bytes=63 * 2**20),
@@ -425,12 +425,12 @@
     single = send(held_back, SINGLES)
 
     partner_sum, own_sum, crossed_sum = pair(
-        0, [partner, own], crossed, constants, for_b=True
+        0, [partner, own], crossed, constants, for_b=True, plane_steps=1
     )
     home = send(crossed_sum, HOME_ACROSS)
     partner = hold(partner, own_sum)
     turned = send(partner, TURNED)
-    top, bottom = pair(1, [partner], beside, constants, sum_a=partner_sum, halves=True, then=direct)
+    top, bottom = pair(1, [partner], beside, constants, sum_a=partner_sum, halves=True, then=direct, plane_steps=1)
     bottom = send(bottom, HOME_TURN)
     top = send(top, HOME_FAR)
     (own_sum,) = pair(2, [own], direct, constants, sum_a=own_sum, in_place=True)

time: 159 us -> 159 us (level)
  transfers between devices with their start and end apart: 11 -> 11, of which waited for: 4 -> 3; matrix products, arithmetic and copies ran while one was open for 4% -> 4% of each run, Pallas kernels for 9% -> 9%
where the time goes in v7:
time: 159 us; the launch traced here: 158 us
  waiting for transfers between devices  106 us (67%)
  starting transfers between devices  27.3 us (17%)
  Pallas kernels  18.1 us (11%)
  other arithmetic  5.27 us (3%)
  local copies, waits for them, and re-layouts  1.83 us (1%)
    ppermute x11, waiting for transfers between devices, send(): return lax.ppermute(value[None], 'band', pairs)[0]  106 us
    ppermute x11, starting transfers between devices, send(): return lax.ppermute(value[None], 'band', pairs)[0]  27.3 us
    pallas_call x5, Pallas kernels, pair_terms(): pl.pallas_call(functools.partial(pair_body, points, slot, jobs, plane_ste...  8.35 us
    pallas_call x1, Pallas kernels, copied(): pl.pallas_call(copy_body, grid=(X_STEPS,), in_specs=[pl.BlockSpec(memory_...  5.22 us
    pallas_call x2, Pallas kernels, settle(): pl.pallas_call(functools.partial(settle_body, wanted, count), in_specs=[p...  4.53 us
    select_n x1, other arithmetic, screened_kernel(): return jnp.where(inside, kernel / -float(points * points * points), 0.0)  4.49 us
  transfers between devices with their start and end apart: 11, of which 3 were waited for; matrix products, arithmetic and copies ran while one was open for 4% of the time, Pallas kernels for 9%

profile of v7, /device:TPU:0, one launch (start us, length us, event | category | flops | bytes accessed | tf_op | source)
XLA Modules:
  0.0 158.5 jit_solution(2367974837728805193)
XLA Ops:
  0.0 2.4 %collective-permute-start.1 = (f32[1,96,9216]{2,1,0:T(8,128)}, f32[1,96,9216]{2,1,0:T(8,128)}, u32[]{:S(2)}, u32[]{:S(2)}) collective-permute-start(f32[1,96,9216]{2,1,0:T(8,128)} %param.4), channel_id=1, source_target_pairs={{3,14},{4,9},{12,1},{11,6},{19,30},{20,25},{28,17},{27,22}} | collective-permute-start | bytes 10616840 | tf_op jit(solution)/shard_map/ppermute | solution.py:409
  2.4 6.6 %collective-permute-start = (f32[1,96,9216]{2,1,0:T(8,128)}, f32[1,96,9216]{2,1,0:T(8,128)}, u32[]{:S(2)}, u32[]{:S(2)}) collective-permute-start(f32[1,96,9216]{2,1,0:T(8,128)} %param.4), channel_id=1, source_target_pairs={{8,14},{15,9},{9,11},{14,12},{7,1},{0,6},{6,4},{1,3},{24,30},{31,2... | collective-permute-start | bytes 10616840 | tf_op jit(solution)/shard_map/ppermute | solution.py:409
  9.0 1.2 dynamic-slice_bitcast_fusion.flags_ref.refs_0_
  10.3 0.1 broadcast_add_fusion
  10.3 4.5 %fusion.5.kernel_ref.refs_1_ = f32[96,96,128]{2,1,0:T(8,128)} fusion(f32[128]{0:T(128)S(1)} %fusion.12, f32[96,96]{1,0:T(8,128)S(1)} %broadcast_add_fusion, pred[128]{0:T(512)(128)(4,1)S(1)} %iota_compare_fusion), kind=kLoop, calls=%fused_computation.7 | loop fusion | flops 12976128 | bytes 4756096 | tf_op jit(solution)/shard_map/jit(_where)/select_n | solution.py:39
  14.8 5.2 %copied.1 = (f32[96,9216]{1,0:T(8,128)}, f32[96,9216]{1,0:T(8,128)}) custom-call(s32[11]{0:T(128)} %dynamic-slice_bitcast_fusion.flags_ref.refs_0_, f32[96,96,128]{2,1,0:T(8,128)} %fusion.5.kernel_ref.refs_1_, bf16[192,192]{1,0:T(8,128)(2,1)} %constant.37.clone.left_ref.refs_5_.refs_6_, bf16[256,256]{1,0:T(8,128)(2,1)} %constant.38.clone.right_ref.refs_6_.refs_7_, ...), custom_call_target="tpu_custom_call" | custom-call | tf_op jit(solution)/shard_map/copied/pallas_call | solution.py:289
  20.0 0.0 collective-permute-done.1
  20.0 0.7 fusion.9
  20.7 0.6 collective-permute-start.2
  21.4 25.1 %collective-permute-done = f32[1,96,9216]{2,1,0:T(8,128)} collective-permute-done((f32[1,96,9216]{2,1,0:T(8,128)}, f32[1,96,9216]{2,1,0:T(8,128)}, u32[]{:S(2)}, u32[]{:S(2)}) %collective-permute-start) | collective-permute-done | bytes 3538976 | tf_op jit(solution)/shard_map/ppermute | solution.py:409
  46.5 3.1 %collective-permute-start.4 = (f32[1,96,9216]{2,1,0:T(8,128)}, f32[1,96,9216]{2,1,0:T(8,128)}, u32[]{:S(2)}, u32[]{:S(2)}) collective-permute-start(f32[1,96,9216]{2,1,0:T(8,128)} %bitcast.29), channel_id=1, source_target_pairs={{15,10},{8,13},{0,5},{7,2},{31,26},{24,29},{16,21},{23,18}} | collective-permute-start | bytes 10616840 | tf_op jit(solution)/shard_map/ppermute | solution.py:409
  49.6 0.0 collective-permute-done.2
  49.6 0.0 copy-start
  49.6 0.6 copy-done
  50.2 2.4 %collective-permute-start.3 = (f32[1,96,9216]{2,1,0:T(8,128)}, f32[1,96,9216]{2,1,0:T(8,128)}, u32[]{:S(2)}, u32[]{:S(2)}) collective-permute-start(f32[1,96,9216]{2,1,0:T(8,128)} %bitcast.30), channel_id=1, source_target_pairs={{13,14},{10,9},{2,1},{5,6},{29,30},{26,25},{18,17},{21,22}} | collective-permute-start | bytes 10616840 | tf_op jit(solution)/shard_map/ppermute | solution.py:409
  52.6 2.5 %collective-permute-start.7 = (f32[1,96,9216]{2,1,0:T(8,128)}, f32[1,96,9216]{2,1,0:T(8,128)}, u32[]{:S(2)}, u32[]{:S(2)}) collective-permute-start(f32[1,96,9216]{2,1,0:T(8,128)} %bitcast.31), channel_id=1, source_target_pairs={{5,10},{2,13},{10,5},{13,2},{21,26},{18,29},{26,21},{29,18}} | collective-permute-start | bytes 10616840 | tf_op jit(solution)/shard_map/ppermute | solution.py:409
  55.1 2.1 %pair_terms.5 = (f32[96,9216]{1,0:T(8,128)}, f32[96,9216]{1,0:T(8,128)}, f32[96,9216]{1,0:T(8,128)}) custom-call(s32[11]{0:T(128)} %dynamic-slice_bitcast_fusion.flags_ref.refs_0_, f32[96,9216]{1,0:T(8,128)} %bitcast.1.refs_1_.refs_0_, f32[96,9216]{1,0:T(8,128)} %bitcast.25, f32[96,9216]{1,0:T(8,128)} %bitcast.3.refs_3_, ...), custom_call_target="tpu_custom_call" | custom-call | flops 100000000 | bytes 1000000 | tf_op jit(solution)/shard_map/pair_terms/pallas_call | solution.py:254
  57.2 2.5 %collective-permute-start.10 = (f32[1,96,9216]{2,1,0:T(8,128)}, f32[1,96,9216]{2,1,0:T(8,128)}, u32[]{:S(2)}, u32[]{:S(2)}) collective-permute-start(f32[1,96,9216]{2,1,0:T(8,128)} %bitcast.33), channel_id=1, source_target_pairs={{9,4},{14,3},{6,11},{1,12},{25,20},{30,19},{22,27},{17,28}} | collective-permute-start | bytes 10616840 | tf_op jit(solution)/shard_map/ppermute | solution.py:409
  59.7 2.4 %collective-permute-start.9 = (f32[1,96,9216]{2,1,0:T(8,128)}, f32[1,96,9216]{2,1,0:T(8,128)}, u32[]{:S(2)}, u32[]{:S(2)}) collective-permute-start(f32[1,96,9216]{2,1,0:T(8,128)} %bitcast.17), channel_id=1, source_target_pairs={{11,14},{12,9},{4,1},{3,6},{27,30},{28,25},{20,17},{19,22}} | collective-permute-start | bytes 10616840 | tf_op jit(solution)/shard_map/ppermute | solution.py:409
  62.1 24.9 %collective-permute-done.4 = f32[1,96,9216]{2,1,0:T(8,128)} collective-permute-done((f32[1,96,9216]{2,1,0:T(8,128)}, f32[1,96,9216]{2,1,0:T(8,128)}, u32[]{:S(2)}, u32[]{:S(2)}) %collective-permute-start.4) | collective-permute-done | bytes 3538976 | tf_op jit(solution)/shard_map/ppermute | solution.py:409
  87.1 0.0 collective-permute-done.3
  87.1 1.5 pair_terms.6
  88.6 1.7 %collective-permute-start.6 = (f32[1,32,9216]{2,1,0:T(8,128)}, f32[1,32,9216]{2,1,0:T(8,128)}, u32[]{:S(2)}, u32[]{:S(2)}) collective-permute-start(f32[1,32,9216]{2,1,0:T(8,128)} %bitcast.35), channel_id=1, source_target_pairs={{9,11},{14,12},{6,4},{1,3},{25,27},{30,28},{22,20},{17,19}} | collective-permute-start | bytes 3538952 | tf_op jit(solution)/shard_map/ppermute | solution.py:409
  90.3 1.5 collective-permute-start.5
  91.8 1.6 pair_terms.7.refs_3_
  93.4 0.0 collective-permute-done.7
  93.4 1.6 pair_terms.8.refs_1_
  95.0 0.0 collective-permute-done.6
  95.0 1.6 collective-permute-start.8
  96.6 0.0 collective-permute-done.10
  96.6 0.8 settle.2.refs_3_
  97.4 0.0 collective-permute-done.9
  97.4 1.6 pair_terms.9.refs_2_
  99.0 55.6 %collective-permute-done.8 = f32[1,32,9216]{2,1,0:T(8,128)} collective-permute-done((f32[1,32,9216]{2,1,0:T(8,128)}, f32[1,32,9216]{2,1,0:T(8,128)}, u32[]{:S(2)}, u32[]{:S(2)}) %collective-permute-start.8) | collective-permute-done | bytes 1179680 | tf_op jit(solution)/shard_map/ppermute | solution.py:409
  154.5 0.0 collective-permute-done.5
  154.5 3.7 %settle.3 = f32[96,9216]{1,0:T(8,128)} custom-call(s32[11]{0:T(128)} %dynamic-slice_bitcast_fusion.flags_ref.refs_0_, f32[64,9216]{1,0:T(8,128)} %bitcast.11.refs_0_, f32[32,9216]{1,0:T(8,128)} %bitcast.16.refs_1_, f32[96,9216]{1,0:T(8,128)} %pair_terms.9.refs_2_), custom_call_target="tpu_custom_call", output_to_operand_aliasing={{}: (3, {})} | custom-call | tf_op jit(solution)/shard_map/settle/pallas_call | solution.py:370
  (8 shorter events, 0.0 us)
Async XLA Ops:
  0.0 20.0 %collective-permute-start.1 = (f32[1,96,9216]{2,1,0:T(8,128)}, f32[1,96,9216]{2,1,0:T(8,128)}, u32[]{:S(2)}, u32[]{:S(2)}) collective-permute-start(f32[1,96,9216]{2,1,0:T(8,128)} %param.4), channel_id=1, source_target_pairs={{3,14},{4,9},{12,1},{11,6},{19,30},{20,25},{28,17},{27,22}} | collective-permute-start | bytes 10616840 | tf_op jit(solution)/shard_map/ppermute | solution.py:409
  2.4 44.1 %collective-permute-start = (f32[1,96,9216]{2,1,0:T(8,128)}, f32[1,96,9216]{2,1,0:T(8,128)}, u32[]{:S(2)}, u32[]{:S(2)}) collective-permute-start(f32[1,96,9216]{2,1,0:T(8,128)} %param.4), channel_id=1, source_target_pairs={{8,14},{15,9},{9,11},{14,12},{7,1},{0,6},{6,4},{1,3},{24,30},{31,2... | collective-permute-start | bytes 10616840 | tf_op jit(solution)/shard_map/ppermute | solution.py:409
  20.7 28.8 %collective-permute-start.2 = (f32[1,8,128]{2,1,0:T(8,128)S(1)}, f32[1,8,128]{2,1,0:T(8,128)S(1)}, u32[]{:S(2)}, u32[]{:S(2)}) collective-permute-start(f32[1,8,128]{2,1,0:T(8,128)S(1)} %fusion.9), channel_id=1, source_target_pairs={{14,2},{9,5},{1,13},{6,10},{30,18},{25,21},{17,29},{22,26}} | collective-permute-start | bytes 12296 | tf_op jit(solution)/shard_map/ppermute | solution.py:409
  46.5 40.6 %collective-permute-start.4 = (f32[1,96,9216]{2,1,0:T(8,128)}, f32[1,96,9216]{2,1,0:T(8,128)}, u32[]{:S(2)}, u32[]{:S(2)}) collective-permute-start(f32[1,96,9216]{2,1,0:T(8,128)} %bitcast.29), channel_id=1, source_target_pairs={{15,10},{8,13},{0,5},{7,2},{31,26},{24,29},{16,21},{23,18}} | collective-permute-start | bytes 10616840 | tf_op jit(solution)/shard_map/ppermute | solution.py:409
  49.6 0.6 copy-start
  50.2 36.9 %collective-permute-start.3 = (f32[1,96,9216]{2,1,0:T(8,128)}, f32[1,96,9216]{2,1,0:T(8,128)}, u32[]{:S(2)}, u32[]{:S(2)}) collective-permute-start(f32[1,96,9216]{2,1,0:T(8,128)} %bitcast.30), channel_id=1, source_target_pairs={{13,14},{10,9},{2,1},{5,6},{29,30},{26,25},{18,17},{21,22}} | collective-permute-start | bytes 10616840 | tf_op jit(solution)/shard_map/ppermute | solution.py:409
  52.6 40.8 %collective-permute-start.7 = (f32[1,96,9216]{2,1,0:T(8,128)}, f32[1,96,9216]{2,1,0:T(8,128)}, u32[]{:S(2)}, u32[]{:S(2)}) collective-permute-start(f32[1,96,9216]{2,1,0:T(8,128)} %bitcast.31), channel_id=1, source_target_pairs={{5,10},{2,13},{10,5},{13,2},{21,26},{18,29},{26,21},{29,18}} | collective-permute-start | bytes 10616840 | tf_op jit(solution)/shard_map/ppermute | solution.py:409
  57.2 39.3 %collective-permute-start.10 = (f32[1,96,9216]{2,1,0:T(8,128)}, f32[1,96,9216]{2,1,0:T(8,128)}, u32[]{:S(2)}, u32[]{:S(2)}) collective-permute-start(f32[1,96,9216]{2,1,0:T(8,128)} %bitcast.33), channel_id=1, source_target_pairs={{9,4},{14,3},{6,11},{1,12},{25,20},{30,19},{22,27},{17,28}} | collective-permute-start | bytes 10616840 | tf_op jit(solution)/shard_map/ppermute | solution.py:409
  59.7 37.7 %collective-permute-start.9 = (f32[1,96,9216]{2,1,0:T(8,128)}, f32[1,96,9216]{2,1,0:T(8,128)}, u32[]{:S(2)}, u32[]{:S(2)}) collective-permute-start(f32[1,96,9216]{2,1,0:T(8,128)} %bitcast.17), channel_id=1, source_target_pairs={{11,14},{12,9},{4,1},{3,6},{27,30},{28,25},{20,17},{19,22}} | collective-permute-start | bytes 10616840 | tf_op jit(solution)/shard_map/ppermute | solution.py:409
  88.6 6.4 %collective-permute-start.6 = (f32[1,32,9216]{2,1,0:T(8,128)}, f32[1,32,9216]{2,1,0:T(8,128)}, u32[]{:S(2)}, u32[]{:S(2)}) collective-permute-start(f32[1,32,9216]{2,1,0:T(8,128)} %bitcast.35), channel_id=1, source_target_pairs={{9,11},{14,12},{6,4},{1,3},{25,27},{30,28},{22,20},{17,19}} | collective-permute-start | bytes 3538952 | tf_op jit(solution)/shard_map/ppermute | solution.py:409
  90.3 64.2 %collective-permute-start.5 = (f32[1,64,9216]{2,1,0:T(8,128)}, f32[1,64,9216]{2,1,0:T(8,128)}, u32[]{:S(2)}, u32[]{:S(2)}) collective-permute-start(f32[1,64,9216]{2,1,0:T(8,128)} %bitcast.34), channel_id=1, source_target_pairs={{9,15},{14,8},{6,0},{1,7},{25,31},{30,24},{22,16},{17,23}} | collective-permute-start | bytes 7077896 | tf_op jit(solution)/shard_map/ppermute | solution.py:409
  95.0 59.5 %collective-permute-start.8 = (f32[1,32,9216]{2,1,0:T(8,128)}, f32[1,32,9216]{2,1,0:T(8,128)}, u32[]{:S(2)}, u32[]{:S(2)}) collective-permute-start(f32[1,32,9216]{2,1,0:T(8,128)} %bitcast.15), channel_id=1, source_target_pairs={{11,15},{12,8},{4,0},{3,7},{27,31},{28,24},{20,16},{19,23}} | collective-permute-start | bytes 3538952 | tf_op jit(solution)/shard_map/ppermute | solution.py:409

commit v8 on v7

--- a/solution.py
+++ b/solution.py
@@ -161,15 +161,15 @@
             for name in a_names[1:] + ["sum_a"] * ("sum_a" in has):
                 fetch(name, chunk).start()
 
-    def lanes_apart(block):
-        tail = jnp.zeros((points, LANES), jnp.float32)
-        wide = jnp.concatenate([block, tail], 1)
-        rows = [wide[:, q * points:q * points + LANES] for q in range(ys)]
-        return jnp.swapaxes(jnp.stack(rows, 0), 0, 1)
-
-    def lanes_together(block):
-        block = jnp.swapaxes(block, 0, 1)
-        return jnp.concatenate([block[q][:, :points] for q in range(ys)], 1)
+    def put_apart(block, start):
+        wide = jnp.concatenate([block, jnp.zeros((points, LANES), jnp.float32)], 1)
+        for q in range(ys):
+            held[pl.ds(start + q, points, stride=points), :] = wide[:, q * points:q * points + LANES]
+
+    def get_together(start):
+        return jnp.concatenate(
+            [held[pl.ds(start + q, points, stride=points), :][:, :points] for q in range(ys)], 1
+        )
 
     def side_by_side(block):
         return jnp.concatenate([block[i] for i in range(per_step)], 1)
@@ -187,7 +187,7 @@
             when_job(number, fetch(a_names[number], chunk).wait)
         spectrum = from_left(left_ref[...], here("a", chunk) * here("b", chunk))
         start = pl.multiple_of(chunk * ys, ys)
-        held[:, pl.ds(start, ys), :] = lanes_apart(spectrum)
+        put_apart(spectrum, start)
 
     @pl.when(active & (at >= X_STEPS) & (at < late))
     def planes():
@@ -196,7 +196,8 @@
         right = right_ref[...]
         first = part * per_step
         when_job(0, lambda: fetch_kernel(part).wait())
-        block = held[pl.ds(first, per_step)].reshape(per_step * points, LANES)
+        rows = pl.ds(pl.multiple_of(first * points, points), per_step * points)
+        block = held[rows, :]
         block = from_right(block, right).reshape(per_step, points, LANES)
         wide = from_left(left, side_by_side(block))
         wide = from_left(left, wide * side_by_side(near_kernel[pl.ds(first, per_step)]))
@@ -204,7 +205,7 @@
             [wide[:, i * LANES:(i + 1) * LANES] for i in range(per_step)], 0
         )
         block = from_right(block, right)
-        held[pl.ds(first, per_step)] = block.reshape(per_step, points, LANES)
+        held[rows, :] = block
 
     @pl.when(active & (at >= late))
     def inverse_x():
@@ -212,7 +213,7 @@
         start = pl.multiple_of(chunk * ys, ys)
         if "sum_a" in has:
             fetch("sum_a", chunk).wait()
-        block = lanes_together(held[:, pl.ds(start, ys), :])
+        block = get_together(start)
         potential = from_left(left_ref[...], block)
         for_a = here("b", chunk) * potential
         if "sum_a" in has:
@@ -261,7 +262,7 @@
         out_shape=[jax.ShapeDtypeStruct((n, plane), jnp.float32) for n in rows],
         input_output_aliases={3: 0} if in_place else {},
         scratch_shapes=[
-            pltpu.VMEM((points, points, LANES), jnp.float32),
+            pltpu.VMEM((points * points, LANES), jnp.float32),
             pltpu.VMEM((len(blocks), points, plane), jnp.float32),
             pltpu.VMEM((points, points, LANES), jnp.float32),
             pltpu.VMEM((jobs + for_b, points, plane), jnp.float32),

time: 159 us -> 164 us (1.031)
  waiting for transfers between devices: 106 us -> 111 us
    ppermute x11, waiting for transfers between devices: 106 us -> 111 us  [send(): return lax.ppermute(value[None], 'band', pairs)[0]]
  transfers between devices with their start and end apart: 11 -> 11, of which waited for: 3 -> 4; matrix products, arithmetic and copies ran while one was open for 4% -> 4% of each run, Pallas kernels for 9% -> 9%
where the time goes in v8:
time: 164 us
  waiting for transfers between devices  111 us (68%)
  starting transfers between devices  27.3 us (17%)
  Pallas kernels  18.1 us (11%)
  other arithmetic  5.27 us (3%)
  local copies, waits for them, and re-layouts  1.83 us (1%)
    ppermute x11, waiting for transfers between devices, send(): return lax.ppermute(value[None], 'band', pairs)[0]  111 us
    ppermute x11, starting transfers between devices, send(): return lax.ppermute(value[None], 'band', pairs)[0]  27.3 us
    pallas_call x5, Pallas kernels, pair_terms(): pl.pallas_call(functools.partial(pair_body, points, slot, jobs, plane_ste...  8.35 us
    pallas_call x1, Pallas kernels, copied(): pl.pallas_call(copy_body, grid=(X_STEPS,), in_specs=[pl.BlockSpec(memory_...  5.22 us
    pallas_call x2, Pallas kernels, settle(): pl.pallas_call(functools.partial(settle_body, wanted, count), in_specs=[p...  4.53 us
    select_n x1, other arithmetic, screened_kernel(): return jnp.where(inside, kernel / -float(points * points * points), 0.0)  4.49 us
  transfers between devices with their start and end apart: 11, of which 4 were waited for; matrix products, arithmetic and copies ran while one was open for 4% of the time, Pallas kernels for 9%

profile of v8, /device:TPU:0, one launch (start us, length us, event | category | flops | bytes accessed | tf_op | source)
XLA Modules:
  0.0 163.6 jit_solution(14899343890588397130)
XLA Ops:
  0.0 2.4 %collective-permute-start.1 = (f32[1,96,9216]{2,1,0:T(8,128)}, f32[1,96,9216]{2,1,0:T(8,128)}, u32[]{:S(2)}, u32[]{:S(2)}) collective-permute-start(f32[1,96,9216]{2,1,0:T(8,128)} %param.4), channel_id=1, source_target_pairs={{3,14},{4,9},{12,1},{11,6},{19,30},{20,25},{28,17},{27,22}} | collective-permute-start | bytes 10616840 | tf_op jit(solution)/shard_map/ppermute | solution.py:410
  2.4 6.6 %collective-permute-start = (f32[1,96,9216]{2,1,0:T(8,128)}, f32[1,96,9216]{2,1,0:T(8,128)}, u32[]{:S(2)}, u32[]{:S(2)}) collective-permute-start(f32[1,96,9216]{2,1,0:T(8,128)} %param.4), channel_id=1, source_target_pairs={{8,14},{15,9},{9,11},{14,12},{7,1},{0,6},{6,4},{1,3},{24,30},{31,2... | collective-permute-start | bytes 10616840 | tf_op jit(solution)/shard_map/ppermute | solution.py:410
  9.0 1.2 dynamic-slice_bitcast_fusion.flags_ref.refs_0_
  10.3 0.1 broadcast_add_fusion
  10.3 4.5 %fusion.5.kernel_ref.refs_1_ = f32[96,96,128]{2,1,0:T(8,128)} fusion(f32[128]{0:T(128)S(1)} %fusion.12, f32[96,96]{1,0:T(8,128)S(1)} %broadcast_add_fusion, pred[128]{0:T(512)(128)(4,1)S(1)} %iota_compare_fusion), kind=kLoop, calls=%fused_computation.7 | loop fusion | flops 12976128 | bytes 4756096 | tf_op jit(solution)/shard_map/jit(_where)/select_n | solution.py:39
  14.8 5.2 %copied.1 = (f32[96,9216]{1,0:T(8,128)}, f32[96,9216]{1,0:T(8,128)}) custom-call(s32[11]{0:T(128)} %dynamic-slice_bitcast_fusion.flags_ref.refs_0_, f32[96,96,128]{2,1,0:T(8,128)} %fusion.5.kernel_ref.refs_1_, bf16[192,192]{1,0:T(8,128)(2,1)} %constant.37.clone.left_ref.refs_5_.refs_6_, bf16[256,256]{1,0:T(8,128)(2,1)} %constant.38.clone.right_ref.refs_6_.refs_7_, ...), custom_call_target="tpu_custom_call" | custom-call | tf_op jit(solution)/shard_map/copied/pallas_call | solution.py:290
  20.0 0.0 collective-permute-done.1
  20.0 0.7 fusion.9
  20.7 0.6 collective-permute-start.2
  21.4 25.1 %collective-permute-done = f32[1,96,9216]{2,1,0:T(8,128)} collective-permute-done((f32[1,96,9216]{2,1,0:T(8,128)}, f32[1,96,9216]{2,1,0:T(8,128)}, u32[]{:S(2)}, u32[]{:S(2)}) %collective-permute-start) | collective-permute-done | bytes 3538976 | tf_op jit(solution)/shard_map/ppermute | solution.py:410
  46.5 3.1 %collective-permute-start.4 = (f32[1,96,9216]{2,1,0:T(8,128)}, f32[1,96,9216]{2,1,0:T(8,128)}, u32[]{:S(2)}, u32[]{:S(2)}) collective-permute-start(f32[1,96,9216]{2,1,0:T(8,128)} %bitcast.29), channel_id=1, source_target_pairs={{15,10},{8,13},{0,5},{7,2},{31,26},{24,29},{16,21},{23,18}} | collective-permute-start | bytes 10616840 | tf_op jit(solution)/shard_map/ppermute | solution.py:410
  49.6 0.0 collective-permute-done.2
  49.6 0.0 copy-start
  49.6 0.6 copy-done
  50.2 2.4 %collective-permute-start.3 = (f32[1,96,9216]{2,1,0:T(8,128)}, f32[1,96,9216]{2,1,0:T(8,128)}, u32[]{:S(2)}, u32[]{:S(2)}) collective-permute-start(f32[1,96,9216]{2,1,0:T(8,128)} %bitcast.30), channel_id=1, source_target_pairs={{13,14},{10,9},{2,1},{5,6},{29,30},{26,25},{18,17},{21,22}} | collective-permute-start | bytes 10616840 | tf_op jit(solution)/shard_map/ppermute | solution.py:410
  52.6 2.5 %collective-permute-start.7 = (f32[1,96,9216]{2,1,0:T(8,128)}, f32[1,96,9216]{2,1,0:T(8,128)}, u32[]{:S(2)}, u32[]{:S(2)}) collective-permute-start(f32[1,96,9216]{2,1,0:T(8,128)} %bitcast.31), channel_id=1, source_target_pairs={{5,10},{2,13},{10,5},{13,2},{21,26},{18,29},{26,21},{29,18}} | collective-permute-start | bytes 10616840 | tf_op jit(solution)/shard_map/ppermute | solution.py:410
  55.1 2.1 %pair_terms.5 = (f32[96,9216]{1,0:T(8,128)}, f32[96,9216]{1,0:T(8,128)}, f32[96,9216]{1,0:T(8,128)}) custom-call(s32[11]{0:T(128)} %dynamic-slice_bitcast_fusion.flags_ref.refs_0_, f32[96,9216]{1,0:T(8,128)} %bitcast.1.refs_1_.refs_0_, f32[96,9216]{1,0:T(8,128)} %bitcast.25, f32[96,9216]{1,0:T(8,128)} %bitcast.3.refs_3_, ...), custom_call_target="tpu_custom_call" | custom-call | flops 100000000 | bytes 1000000 | tf_op jit(solution)/shard_map/pair_terms/pallas_call | solution.py:255
  57.2 2.5 %collective-permute-start.10 = (f32[1,96,9216]{2,1,0:T(8,128)}, f32[1,96,9216]{2,1,0:T(8,128)}, u32[]{:S(2)}, u32[]{:S(2)}) collective-permute-start(f32[1,96,9216]{2,1,0:T(8,128)} %bitcast.33), channel_id=1, source_target_pairs={{9,4},{14,3},{6,11},{1,12},{25,20},{30,19},{22,27},{17,28}} | collective-permute-start | bytes 10616840 | tf_op jit(solution)/shard_map/ppermute | solution.py:410
  59.7 2.4 %collective-permute-start.9 = (f32[1,96,9216]{2,1,0:T(8,128)}, f32[1,96,9216]{2,1,0:T(8,128)}, u32[]{:S(2)}, u32[]{:S(2)}) collective-permute-start(f32[1,96,9216]{2,1,0:T(8,128)} %bitcast.17), channel_id=1, source_target_pairs={{11,14},{12,9},{4,1},{3,6},{27,30},{28,25},{20,17},{19,22}} | collective-permute-start | bytes 10616840 | tf_op jit(solution)/shard_map/ppermute | solution.py:410
  62.1 24.9 %collective-permute-done.4 = f32[1,96,9216]{2,1,0:T(8,128)} collective-permute-done((f32[1,96,9216]{2,1,0:T(8,128)}, f32[1,96,9216]{2,1,0:T(8,128)}, u32[]{:S(2)}, u32[]{:S(2)}) %collective-permute-start.4) | collective-permute-done | bytes 3538976 | tf_op jit(solution)/shard_map/ppermute | solution.py:410
  87.1 0.0 collective-permute-done.3
  87.1 1.5 pair_terms.6
  88.6 1.7 %collective-permute-start.6 = (f32[1,32,9216]{2,1,0:T(8,128)}, f32[1,32,9216]{2,1,0:T(8,128)}, u32[]{:S(2)}, u32[]{:S(2)}) collective-permute-start(f32[1,32,9216]{2,1,0:T(8,128)} %bitcast.35), channel_id=1, source_target_pairs={{9,11},{14,12},{6,4},{1,3},{25,27},{30,28},{22,20},{17,19}} | collective-permute-start | bytes 3538952 | tf_op jit(solution)/shard_map/ppermute | solution.py:410
  90.3 1.5 collective-permute-start.5
  91.8 1.6 pair_terms.7.refs_3_
  93.4 0.0 collective-permute-done.7
  93.4 1.6 pair_terms.8.refs_1_
  95.0 0.0 collective-permute-done.6
  95.0 1.6 collective-permute-start.8
  96.6 0.0 collective-permute-done.10
  96.6 0.8 settle.2.refs_3_
  97.4 0.0 collective-permute-done.9
  97.4 1.6 pair_terms.9.refs_2_
  99.0 55.6 %collective-permute-done.8 = f32[1,32,9216]{2,1,0:T(8,128)} collective-permute-done((f32[1,32,9216]{2,1,0:T(8,128)}, f32[1,32,9216]{2,1,0:T(8,128)}, u32[]{:S(2)}, u32[]{:S(2)}) %collective-permute-start.8) | collective-permute-done | bytes 1179680 | tf_op jit(solution)/shard_map/ppermute | solution.py:410
  154.5 5.1 %collective-permute-done.5 = f32[1,64,9216]{2,1,0:T(8,128)} collective-permute-done((f32[1,64,9216]{2,1,0:T(8,128)}, f32[1,64,9216]{2,1,0:T(8,128)}, u32[]{:S(2)}, u32[]{:S(2)}) %collective-permute-start.5) | collective-permute-done | bytes 2359328 | tf_op jit(solution)/shard_map/ppermute | solution.py:410
  159.7 3.7 %settle.3 = f32[96,9216]{1,0:T(8,128)} custom-call(s32[11]{0:T(128)} %dynamic-slice_bitcast_fusion.flags_ref.refs_0_, f32[64,9216]{1,0:T(8,128)} %bitcast.11.refs_0_, f32[32,9216]{1,0:T(8,128)} %bitcast.16.refs_1_, f32[96,9216]{1,0:T(8,128)} %pair_terms.9.refs_2_), custom_call_target="tpu_custom_call", output_to_operand_aliasing={{}: (3, {})} | custom-call | tf_op jit(solution)/shard_map/settle/pallas_call | solution.py:371
  (8 shorter events, 0.0 us)
Async XLA Ops:
  0.0 20.0 %collective-permute-start.1 = (f32[1,96,9216]{2,1,0:T(8,128)}, f32[1,96,9216]{2,1,0:T(8,128)}, u32[]{:S(2)}, u32[]{:S(2)}) collective-permute-start(f32[1,96,9216]{2,1,0:T(8,128)} %param.4), channel_id=1, source_target_pairs={{3,14},{4,9},{12,1},{11,6},{19,30},{20,25},{28,17},{27,22}} | collective-permute-start | bytes 10616840 | tf_op jit(solution)/shard_map/ppermute | solution.py:410
  2.4 44.1 %collective-permute-start = (f32[1,96,9216]{2,1,0:T(8,128)}, f32[1,96,9216]{2,1,0:T(8,128)}, u32[]{:S(2)}, u32[]{:S(2)}) collective-permute-start(f32[1,96,9216]{2,1,0:T(8,128)} %param.4), channel_id=1, source_target_pairs={{8,14},{15,9},{9,11},{14,12},{7,1},{0,6},{6,4},{1,3},{24,30},{31,2... | collective-permute-start | bytes 10616840 | tf_op jit(solution)/shard_map/ppermute | solution.py:410
  20.7 28.8 %collective-permute-start.2 = (f32[1,8,128]{2,1,0:T(8,128)S(1)}, f32[1,8,128]{2,1,0:T(8,128)S(1)}, u32[]{:S(2)}, u32[]{:S(2)}) collective-permute-start(f32[1,8,128]{2,1,0:T(8,128)S(1)} %fusion.9), channel_id=1, source_target_pairs={{14,2},{9,5},{1,13},{6,10},{30,18},{25,21},{17,29},{22,26}} | collective-permute-start | bytes 12296 | tf_op jit(solution)/shard_map/ppermute | solution.py:410
  46.5 40.6 %collective-permute-start.4 = (f32[1,96,9216]{2,1,0:T(8,128)}, f32[1,96,9216]{2,1,0:T(8,128)}, u32[]{:S(2)}, u32[]{:S(2)}) collective-permute-start(f32[1,96,9216]{2,1,0:T(8,128)} %bitcast.29), channel_id=1, source_target_pairs={{15,10},{8,13},{0,5},{7,2},{31,26},{24,29},{16,21},{23,18}} | collective-permute-start | bytes 10616840 | tf_op jit(solution)/shard_map/ppermute | solution.py:410
  49.6 0.6 copy-start
  50.2 36.9 %collective-permute-start.3 = (f32[1,96,9216]{2,1,0:T(8,128)}, f32[1,96,9216]{2,1,0:T(8,128)}, u32[]{:S(2)}, u32[]{:S(2)}) collective-permute-start(f32[1,96,9216]{2,1,0:T(8,128)} %bitcast.30), channel_id=1, source_target_pairs={{13,14},{10,9},{2,1},{5,6},{29,30},{26,25},{18,17},{21,22}} | collective-permute-start | bytes 10616840 | tf_op jit(solution)/shard_map/ppermute | solution.py:410
  52.6 40.8 %collective-permute-start.7 = (f32[1,96,9216]{2,1,0:T(8,128)}, f32[1,96,9216]{2,1,0:T(8,128)}, u32[]{:S(2)}, u32[]{:S(2)}) collective-permute-start(f32[1,96,9216]{2,1,0:T(8,128)} %bitcast.31), channel_id=1, source_target_pairs={{5,10},{2,13},{10,5},{13,2},{21,26},{18,29},{26,21},{29,18}} | collective-permute-start | bytes 10616840 | tf_op jit(solution)/shard_map/ppermute | solution.py:410
  57.2 39.3 %collective-permute-start.10 = (f32[1,96,9216]{2,1,0:T(8,128)}, f32[1,96,9216]{2,1,0:T(8,128)}, u32[]{:S(2)}, u32[]{:S(2)}) collective-permute-start(f32[1,96,9216]{2,1,0:T(8,128)} %bitcast.33), channel_id=1, source_target_pairs={{9,4},{14,3},{6,11},{1,12},{25,20},{30,19},{22,27},{17,28}} | collective-permute-start | bytes 10616840 | tf_op jit(solution)/shard_map/ppermute | solution.py:410
  59.7 37.7 %collective-permute-start.9 = (f32[1,96,9216]{2,1,0:T(8,128)}, f32[1,96,9216]{2,1,0:T(8,128)}, u32[]{:S(2)}, u32[]{:S(2)}) collective-permute-start(f32[1,96,9216]{2,1,0:T(8,128)} %bitcast.17), channel_id=1, source_target_pairs={{11,14},{12,9},{4,1},{3,6},{27,30},{28,25},{20,17},{19,22}} | collective-permute-start | bytes 10616840 | tf_op jit(solution)/shard_map/ppermute | solution.py:410
  88.6 6.4 %collective-permute-start.6 = (f32[1,32,9216]{2,1,0:T(8,128)}, f32[1,32,9216]{2,1,0:T(8,128)}, u32[]{:S(2)}, u32[]{:S(2)}) collective-permute-start(f32[1,32,9216]{2,1,0:T(8,128)} %bitcast.35), channel_id=1, source_target_pairs={{9,11},{14,12},{6,4},{1,3},{25,27},{30,28},{22,20},{17,19}} | collective-permute-start | bytes 3538952 | tf_op jit(solution)/shard_map/ppermute | solution.py:410
  90.3 69.3 %collective-permute-start.5 = (f32[1,64,9216]{2,1,0:T(8,128)}, f32[1,64,9216]{2,1,0:T(8,128)}, u32[]{:S(2)}, u32[]{:S(2)}) collective-permute-start(f32[1,64,9216]{2,1,0:T(8,128)} %bitcast.34), channel_id=1, source_target_pairs={{9,15},{14,8},{6,0},{1,7},{25,31},{30,24},{22,16},{17,23}} | collective-permute-start | bytes 7077896 | tf_op jit(solution)/shard_map/ppermute | solution.py:410
  95.0 59.5 %collective-permute-start.8 = (f32[1,32,9216]{2,1,0:T(8,128)}, f32[1,32,9216]{2,1,0:T(8,128)}, u32[]{:S(2)}, u32[]{:S(2)}) collective-permute-start(f32[1,32,9216]{2,1,0:T(8,128)} %bitcast.15), channel_id=1, source_target_pairs={{11,15},{12,8},{4,0},{3,7},{27,31},{28,24},{20,16},{19,23}} | collective-permute-start | bytes 3538952 | tf_op jit(solution)/shard_map/ppermute | solution.py:410

commit v9 on v7

--- a/solution.py
+++ b/solution.py
@@ -14,7 +14,7 @@
 LANES = 128
 X_STEPS = 3
 SETTLE_STEPS = 6
-FAR_ROWS = 32
+FAR_ROWS = 40
 
 
 def from_behind(value, axis, by):
@@ -421,6 +421,7 @@
     direct = send(direct_copy, DIRECT)
     kernel, held_back = gate(send(token, ARRIVED), kernel, direct_copy, own_copy)
     constants = (kernel, left, right)
+    turned = send(partner, TURNED)
     beside = send(held_back, BESIDE)
     single = send(held_back, SINGLES)
 
@@ -428,16 +429,14 @@
         0, [partner, own], crossed, constants, for_b=True, plane_steps=1
     )
     home = send(crossed_sum, HOME_ACROSS)
-    partner = hold(partner, own_sum)
-    turned = send(partner, TURNED)
     top, bottom = pair(1, [partner], beside, constants, sum_a=partner_sum, halves=True, then=direct, plane_steps=1)
     bottom = send(bottom, HOME_TURN)
     top = send(top, HOME_FAR)
     (own_sum,) = pair(2, [own], direct, constants, sum_a=own_sum, in_place=True)
+    (own_sum,) = pair(4, [own], turned, constants, sum_a=own_sum, in_place=True, then=single)
     (own_sum,) = pair(3, [own], single, constants, sum_a=own_sum, in_place=True)
     bottom = send(hold(bottom, own_sum), HOME_TURNED)
     own_sum = settle(flags, 1, [home], own_sum)
-    (own_sum,) = pair(4, [own], turned, constants, sum_a=own_sum, in_place=True)
     return settle(flags, 2, [top, bottom], own_sum)[None]
 
 

time: 159 us -> 168 us (1.057); the launches traced: 158 us -> 166 us
  waiting for transfers between devices: 106 us -> 113 us
    ppermute x11, waiting for transfers between devices: 106 us -> 113 us  [send(): return lax.ppermute(value[None], 'band', pairs)[0]]
  transfers between devices with their start and end apart: 11 -> 11, of which waited for: 3 -> 4; matrix products, arithmetic and copies ran while one was open for 4% -> 4% of each run, Pallas kernels for 9% -> 9%
where the time goes in v9:
time: 168 us; the launch traced here: 166 us
  waiting for transfers between devices  113 us (67%)
  starting transfers between devices  27.1 us (16%)
  Pallas kernels  18.5 us (11%)
  other arithmetic  5.27 us (3%)
  local copies, waits for them, and re-layouts  1.83 us (1%)
    ppermute x11, waiting for transfers between devices, send(): return lax.ppermute(value[None], 'band', pairs)[0]  113 us
    ppermute x11, starting transfers between devices, send(): return lax.ppermute(value[None], 'band', pairs)[0]  27.1 us
    pallas_call x5, Pallas kernels, pair_terms(): pl.pallas_call(functools.partial(pair_body, points, slot, jobs, plane_ste...  8.61 us
    pallas_call x1, Pallas kernels, copied(): pl.pallas_call(copy_body, grid=(X_STEPS,), in_specs=[pl.BlockSpec(memory_...  5.22 us
    pallas_call x2, Pallas kernels, settle(): pl.pallas_call(functools.partial(settle_body, wanted, count), in_specs=[p...  4.63 us
    select_n x1, other arithmetic, screened_kernel(): return jnp.where(inside, kernel / -float(points * points * points), 0.0)  4.49 us
  transfers between devices with their start and end apart: 11, of which 4 were waited for; matrix products, arithmetic and copies ran while one was open for 4% of the time, Pallas kernels for 9%

profile of v9, /device:TPU:0, one launch (start us, length us, event | category | flops | bytes accessed | tf_op | source)
XLA Modules:
  0.0 165.7 jit_solution(1023832435541942529)
XLA Ops:
  0.0 2.4 %collective-permute-start.1 = (f32[1,96,9216]{2,1,0:T(8,128)}, f32[1,96,9216]{2,1,0:T(8,128)}, u32[]{:S(2)}, u32[]{:S(2)}) collective-permute-start(f32[1,96,9216]{2,1,0:T(8,128)} %param.4), channel_id=1, source_target_pairs={{3,14},{4,9},{12,1},{11,6},{19,30},{20,25},{28,17},{27,22}} | collective-permute-start | bytes 10616840 | tf_op jit(solution)/shard_map/ppermute | solution.py:409
  2.4 6.5 %collective-permute-start = (f32[1,96,9216]{2,1,0:T(8,128)}, f32[1,96,9216]{2,1,0:T(8,128)}, u32[]{:S(2)}, u32[]{:S(2)}) collective-permute-start(f32[1,96,9216]{2,1,0:T(8,128)} %param.4), channel_id=1, source_target_pairs={{8,14},{15,9},{9,11},{14,12},{7,1},{0,6},{6,4},{1,3},{24,30},{31,2... | collective-permute-start | bytes 10616840 | tf_op jit(solution)/shard_map/ppermute | solution.py:409
  9.0 1.2 dynamic-slice_bitcast_fusion.flags_ref.refs_0_
  10.2 0.1 broadcast_add_fusion
  10.3 4.5 %fusion.5.kernel_ref.refs_1_ = f32[96,96,128]{2,1,0:T(8,128)} fusion(f32[128]{0:T(128)S(1)} %fusion.12, f32[96,96]{1,0:T(8,128)S(1)} %broadcast_add_fusion, pred[128]{0:T(512)(128)(4,1)S(1)} %iota_compare_fusion), kind=kLoop, calls=%fused_computation.7 | loop fusion | flops 12976128 | bytes 4756096 | tf_op jit(solution)/shard_map/jit(_where)/select_n | solution.py:39
  14.8 5.2 %copied.1 = (f32[96,9216]{1,0:T(8,128)}, f32[96,9216]{1,0:T(8,128)}) custom-call(s32[11]{0:T(128)} %dynamic-slice_bitcast_fusion.flags_ref.refs_0_, f32[96,96,128]{2,1,0:T(8,128)} %fusion.5.kernel_ref.refs_1_, bf16[192,192]{1,0:T(8,128)(2,1)} %constant.37.clone.left_ref.refs_5_.refs_6_, bf16[256,256]{1,0:T(8,128)(2,1)} %constant.38.clone.right_ref.refs_6_.refs_7_, ...), custom_call_target="tpu_custom_call" | custom-call | tf_op jit(solution)/shard_map/copied/pallas_call | solution.py:289
  20.0 0.0 collective-permute-done.1
  20.0 0.7 fusion.9
  20.7 0.6 collective-permute-start.2
  21.4 25.1 %collective-permute-done = f32[1,96,9216]{2,1,0:T(8,128)} collective-permute-done((f32[1,96,9216]{2,1,0:T(8,128)}, f32[1,96,9216]{2,1,0:T(8,128)}, u32[]{:S(2)}, u32[]{:S(2)}) %collective-permute-start) | collective-permute-done | bytes 3538976 | tf_op jit(solution)/shard_map/ppermute | solution.py:409
  46.5 3.1 %collective-permute-start.4 = (f32[1,96,9216]{2,1,0:T(8,128)}, f32[1,96,9216]{2,1,0:T(8,128)}, u32[]{:S(2)}, u32[]{:S(2)}) collective-permute-start(f32[1,96,9216]{2,1,0:T(8,128)} %bitcast.28), channel_id=1, source_target_pairs={{15,10},{8,13},{0,5},{7,2},{31,26},{24,29},{16,21},{23,18}} | collective-permute-start | bytes 10616840 | tf_op jit(solution)/shard_map/ppermute | solution.py:409
  49.6 0.0 collective-permute-done.2
  49.6 0.0 copy-start
  49.6 0.6 copy-done
  50.2 2.4 %collective-permute-start.3 = (f32[1,96,9216]{2,1,0:T(8,128)}, f32[1,96,9216]{2,1,0:T(8,128)}, u32[]{:S(2)}, u32[]{:S(2)}) collective-permute-start(f32[1,96,9216]{2,1,0:T(8,128)} %bitcast.29), channel_id=1, source_target_pairs={{13,14},{10,9},{2,1},{5,6},{29,30},{26,25},{18,17},{21,22}} | collective-permute-start | bytes 10616840 | tf_op jit(solution)/shard_map/ppermute | solution.py:409
  52.6 2.5 %collective-permute-start.8 = (f32[1,96,9216]{2,1,0:T(8,128)}, f32[1,96,9216]{2,1,0:T(8,128)}, u32[]{:S(2)}, u32[]{:S(2)}) collective-permute-start(f32[1,96,9216]{2,1,0:T(8,128)} %collective-permute-done), channel_id=1, source_target_pairs={{11,14},{12,9},{4,1},{3,6},{27,30},{28,25},{20,17},{19,22}} | collective-permute-start | bytes 10616840 | tf_op jit(solution)/shard_map/ppermute | solution.py:409
  55.1 2.5 %collective-permute-start.7 = (f32[1,96,9216]{2,1,0:T(8,128)}, f32[1,96,9216]{2,1,0:T(8,128)}, u32[]{:S(2)}, u32[]{:S(2)}) collective-permute-start(f32[1,96,9216]{2,1,0:T(8,128)} %bitcast.30), channel_id=1, source_target_pairs={{5,10},{2,13},{10,5},{13,2},{21,26},{18,29},{26,21},{29,18}} | collective-permute-start | bytes 10616840 | tf_op jit(solution)/shard_map/ppermute | solution.py:409
  57.6 2.1 %pair_terms.5 = (f32[96,9216]{1,0:T(8,128)}, f32[96,9216]{1,0:T(8,128)}, f32[96,9216]{1,0:T(8,128)}) custom-call(s32[11]{0:T(128)} %dynamic-slice_bitcast_fusion.flags_ref.refs_0_, f32[96,9216]{1,0:T(8,128)} %bitcast.1.refs_1_, f32[96,9216]{1,0:T(8,128)} %bitcast.24, f32[96,9216]{1,0:T(8,128)} %bitcast.2.refs_3_, ...), custom_call_target="tpu_custom_call" | custom-call | flops 100000000 | bytes 1000000 | tf_op jit(solution)/shard_map/pair_terms/pallas_call | solution.py:254
  59.7 2.4 %collective-permute-start.10 = (f32[1,96,9216]{2,1,0:T(8,128)}, f32[1,96,9216]{2,1,0:T(8,128)}, u32[]{:S(2)}, u32[]{:S(2)}) collective-permute-start(f32[1,96,9216]{2,1,0:T(8,128)} %bitcast.32), channel_id=1, source_target_pairs={{9,4},{14,3},{6,11},{1,12},{25,20},{30,19},{22,27},{17,28}} | collective-permute-start | bytes 10616840 | tf_op jit(solution)/shard_map/ppermute | solution.py:409
  62.2 24.9 %collective-permute-done.4 = f32[1,96,9216]{2,1,0:T(8,128)} collective-permute-done((f32[1,96,9216]{2,1,0:T(8,128)}, f32[1,96,9216]{2,1,0:T(8,128)}, u32[]{:S(2)}, u32[]{:S(2)}) %collective-permute-start.4) | collective-permute-done | bytes 3538976 | tf_op jit(solution)/shard_map/ppermute | solution.py:409
  87.1 0.0 collective-permute-done.3
  87.1 1.5 pair_terms.6
  88.6 1.8 %collective-permute-start.6 = (f32[1,40,9216]{2,1,0:T(8,128)}, f32[1,40,9216]{2,1,0:T(8,128)}, u32[]{:S(2)}, u32[]{:S(2)}) collective-permute-start(f32[1,40,9216]{2,1,0:T(8,128)} %bitcast.34), channel_id=1, source_target_pairs={{9,11},{14,12},{6,4},{1,3},{25,27},{30,28},{22,20},{17,19}} | collective-permute-start | bytes 4423688 | tf_op jit(solution)/shard_map/ppermute | solution.py:409
  90.4 1.5 collective-permute-start.5
  91.9 1.6 pair_terms.7.refs_3_
  93.5 0.0 collective-permute-done.8
  93.5 0.0 collective-permute-done.7
  93.5 1.6 pair_terms.8.refs_3_
  95.1 1.8 %pair_terms.9.refs_1_ = f32[96,9216]{1,0:T(8,128)} custom-call(s32[11]{0:T(128)} %dynamic-slice_bitcast_fusion.flags_ref.refs_0_, f32[96,9216]{1,0:T(8,128)} %bitcast.27, f32[96,9216]{1,0:T(8,128)} %bitcast.14.refs_4_.refs_2_, f32[96,9216]{1,0:T(8,128)} %pair_terms.8.refs_3_, ...), custom_call_target="tpu_custom_call", output_to_operand_aliasing={{}: (3, {})} | custom-call | flops 100000000 | bytes 1000000 | tf_op jit(solution)/shard_map/pair_terms/pallas_call | solution.py:254
  96.9 0.0 collective-permute-done.6
  96.9 1.3 collective-permute-start.9
  98.2 0.0 collective-permute-done.10
  98.2 0.8 settle.2.refs_2_
  99.0 53.1 %collective-permute-done.5 = f32[1,56,9216]{2,1,0:T(8,128)} collective-permute-done((f32[1,56,9216]{2,1,0:T(8,128)}, f32[1,56,9216]{2,1,0:T(8,128)}, u32[]{:S(2)}, u32[]{:S(2)}) %collective-permute-start.5) | collective-permute-done | bytes 2064416 | tf_op jit(solution)/shard_map/ppermute | solution.py:409
  152.1 9.5 %collective-permute-done.9 = f32[1,40,9216]{2,1,0:T(8,128)} collective-permute-done((f32[1,40,9216]{2,1,0:T(8,128)}, f32[1,40,9216]{2,1,0:T(8,128)}, u32[]{:S(2)}, u32[]{:S(2)}) %collective-permute-start.9) | collective-permute-done | bytes 1474592 | tf_op jit(solution)/shard_map/ppermute | solution.py:409
  161.6 3.8 %settle.3 = f32[96,9216]{1,0:T(8,128)} custom-call(s32[11]{0:T(128)} %dynamic-slice_bitcast_fusion.flags_ref.refs_0_, f32[56,9216]{1,0:T(8,128)} %bitcast.11.refs_0_, f32[40,9216]{1,0:T(8,128)} %bitcast.17.refs_1_, f32[96,9216]{1,0:T(8,128)} %settle.2.refs_2_), custom_call_target="tpu_custom_call", output_to_operand_aliasing={{}: (3, {})} | custom-call | tf_op jit(solution)/shard_map/settle/pallas_call | solution.py:370
  (7 shorter events, 0.0 us)
Async XLA Ops:
  0.0 20.0 %collective-permute-start.1 = (f32[1,96,9216]{2,1,0:T(8,128)}, f32[1,96,9216]{2,1,0:T(8,128)}, u32[]{:S(2)}, u32[]{:S(2)}) collective-permute-start(f32[1,96,9216]{2,1,0:T(8,128)} %param.4), channel_id=1, source_target_pairs={{3,14},{4,9},{12,1},{11,6},{19,30},{20,25},{28,17},{27,22}} | collective-permute-start | bytes 10616840 | tf_op jit(solution)/shard_map/ppermute | solution.py:409
  2.4 44.1 %collective-permute-start = (f32[1,96,9216]{2,1,0:T(8,128)}, f32[1,96,9216]{2,1,0:T(8,128)}, u32[]{:S(2)}, u32[]{:S(2)}) collective-permute-start(f32[1,96,9216]{2,1,0:T(8,128)} %param.4), channel_id=1, source_target_pairs={{8,14},{15,9},{9,11},{14,12},{7,1},{0,6},{6,4},{1,3},{24,30},{31,2... | collective-permute-start | bytes 10616840 | tf_op jit(solution)/shard_map/ppermute | solution.py:409
  20.7 28.9 %collective-permute-start.2 = (f32[1,8,128]{2,1,0:T(8,128)S(1)}, f32[1,8,128]{2,1,0:T(8,128)S(1)}, u32[]{:S(2)}, u32[]{:S(2)}) collective-permute-start(f32[1,8,128]{2,1,0:T(8,128)S(1)} %fusion.9), channel_id=1, source_target_pairs={{14,2},{9,5},{1,13},{6,10},{30,18},{25,21},{17,29},{22,26}} | collective-permute-start | bytes 12296 | tf_op jit(solution)/shard_map/ppermute | solution.py:409
  46.5 40.6 %collective-permute-start.4 = (f32[1,96,9216]{2,1,0:T(8,128)}, f32[1,96,9216]{2,1,0:T(8,128)}, u32[]{:S(2)}, u32[]{:S(2)}) collective-permute-start(f32[1,96,9216]{2,1,0:T(8,128)} %bitcast.28), channel_id=1, source_target_pairs={{15,10},{8,13},{0,5},{7,2},{31,26},{24,29},{16,21},{23,18}} | collective-permute-start | bytes 10616840 | tf_op jit(solution)/shard_map/ppermute | solution.py:409
  49.6 0.6 copy-start
  50.2 36.9 %collective-permute-start.3 = (f32[1,96,9216]{2,1,0:T(8,128)}, f32[1,96,9216]{2,1,0:T(8,128)}, u32[]{:S(2)}, u32[]{:S(2)}) collective-permute-start(f32[1,96,9216]{2,1,0:T(8,128)} %bitcast.29), channel_id=1, source_target_pairs={{13,14},{10,9},{2,1},{5,6},{29,30},{26,25},{18,17},{21,22}} | collective-permute-start | bytes 10616840 | tf_op jit(solution)/shard_map/ppermute | solution.py:409
  52.6 40.9 %collective-permute-start.8 = (f32[1,96,9216]{2,1,0:T(8,128)}, f32[1,96,9216]{2,1,0:T(8,128)}, u32[]{:S(2)}, u32[]{:S(2)}) collective-permute-start(f32[1,96,9216]{2,1,0:T(8,128)} %collective-permute-done), channel_id=1, source_target_pairs={{11,14},{12,9},{4,1},{3,6},{27,30},{28,25},{20,17},{19,22}} | collective-permute-start | bytes 10616840 | tf_op jit(solution)/shard_map/ppermute | solution.py:409
  55.1 38.4 %collective-permute-start.7 = (f32[1,96,9216]{2,1,0:T(8,128)}, f32[1,96,9216]{2,1,0:T(8,128)}, u32[]{:S(2)}, u32[]{:S(2)}) collective-permute-start(f32[1,96,9216]{2,1,0:T(8,128)} %bitcast.30), channel_id=1, source_target_pairs={{5,10},{2,13},{10,5},{13,2},{21,26},{18,29},{26,21},{29,18}} | collective-permute-start | bytes 10616840 | tf_op jit(solution)/shard_map/ppermute | solution.py:409
  59.7 38.5 %collective-permute-start.10 = (f32[1,96,9216]{2,1,0:T(8,128)}, f32[1,96,9216]{2,1,0:T(8,128)}, u32[]{:S(2)}, u32[]{:S(2)}) collective-permute-start(f32[1,96,9216]{2,1,0:T(8,128)} %bitcast.32), channel_id=1, source_target_pairs={{9,4},{14,3},{6,11},{1,12},{25,20},{30,19},{22,27},{17,28}} | collective-permute-start | bytes 10616840 | tf_op jit(solution)/shard_map/ppermute | solution.py:409
  88.6 8.3 %collective-permute-start.6 = (f32[1,40,9216]{2,1,0:T(8,128)}, f32[1,40,9216]{2,1,0:T(8,128)}, u32[]{:S(2)}, u32[]{:S(2)}) collective-permute-start(f32[1,40,9216]{2,1,0:T(8,128)} %bitcast.34), channel_id=1, source_target_pairs={{9,11},{14,12},{6,4},{1,3},{25,27},{30,28},{22,20},{17,19}} | collective-permute-start | bytes 4423688 | tf_op jit(solution)/shard_map/ppermute | solution.py:409
  90.4 61.7 %collective-permute-start.5 = (f32[1,56,9216]{2,1,0:T(8,128)}, f32[1,56,9216]{2,1,0:T(8,128)}, u32[]{:S(2)}, u32[]{:S(2)}) collective-permute-start(f32[1,56,9216]{2,1,0:T(8,128)} %bitcast.33), channel_id=1, source_target_pairs={{9,15},{14,8},{6,0},{1,7},{25,31},{30,24},{22,16},{17,23}} | collective-permute-start | bytes 6193160 | tf_op jit(solution)/shard_map/ppermute | solution.py:409
  96.9 64.7 %collective-permute-start.9 = (f32[1,40,9216]{2,1,0:T(8,128)}, f32[1,40,9216]{2,1,0:T(8,128)}, u32[]{:S(2)}, u32[]{:S(2)}) collective-permute-start(f32[1,40,9216]{2,1,0:T(8,128)} %bitcast.16), channel_id=1, source_target_pairs={{11,15},{12,8},{4,0},{3,7},{27,31},{28,24},{20,16},{19,23}} | collective-permute-start | bytes 4423688 | tf_op jit(solution)/shard_map/ppermute | solution.py:409

commit v10 on v7

--- a/solution.py
+++ b/solution.py
@@ -417,20 +417,19 @@
     partner = send(own, PARTNERS)
     own_copy, direct_copy = copied(flags, constants, own)
     token = crossed[:8, :LANES] + own_copy[:8, :LANES]
-    direct_copy = hold(direct_copy, partner)
     direct = send(direct_copy, DIRECT)
-    kernel, held_back = gate(send(token, ARRIVED), kernel, direct_copy, own_copy)
+    kernel, held_back = gate(send(token, ARRIVED), kernel, partner, own_copy)
     constants = (kernel, left, right)
     beside = send(held_back, BESIDE)
     single = send(held_back, SINGLES)
 
     partner_sum, own_sum, crossed_sum = pair(
-        0, [partner, own], crossed, constants, for_b=True, plane_steps=1
+        0, [partner, own], crossed, constants, for_b=True, then=direct, plane_steps=1
     )
     home = send(crossed_sum, HOME_ACROSS)
     partner = hold(partner, own_sum)
     turned = send(partner, TURNED)
-    top, bottom = pair(1, [partner], beside, constants, sum_a=partner_sum, halves=True, then=direct, plane_steps=1)
+    top, bottom = pair(1, [partner], beside, constants, sum_a=partner_sum, halves=True, plane_steps=1)
     bottom = send(bottom, HOME_TURN)
     top = send(top, HOME_FAR)
     (own_sum,) = pair(2, [own], direct, constants, sum_a=own_sum, in_place=True)

time: 159 us -> 159 us (level)
  no operation moved by 1% of the time
where the time goes in v10:
time: 159 us; the launch traced here: 158 us
  waiting for transfers between devices  105 us (66%)
  starting transfers between devices  27.3 us (17%)
  Pallas kernels  18.1 us (11%)
  other arithmetic  5.27 us (3%)
  local copies, waits for them, and re-layouts  1.82 us (1%)
    ppermute x11, waiting for transfers between devices, send(): return lax.ppermute(value[None], 'band', pairs)[0]  105 us
    ppermute x11, starting transfers between devices, send(): return lax.ppermute(value[None], 'band', pairs)[0]  27.3 us
    pallas_call x5, Pallas kernels, pair_terms(): pl.pallas_call(functools.partial(pair_body, points, slot, jobs, plane_ste...  8.35 us
    pallas_call x1, Pallas kernels, copied(): pl.pallas_call(copy_body, grid=(X_STEPS,), in_specs=[pl.BlockSpec(memory_...  5.23 us
    pallas_call x2, Pallas kernels, settle(): pl.pallas_call(functools.partial(settle_body, wanted, count), in_specs=[p...  4.53 us
    select_n x1, other arithmetic, screened_kernel(): return jnp.where(inside, kernel / -float(points * points * points), 0.0)  4.49 us
  transfers between devices with their start and end apart: 11, of which 3 were waited for; matrix products, arithmetic and copies ran while one was open for 4% of the time, Pallas kernels for 9%

profile of v10, /device:TPU:0, one launch (start us, length us, event | category | flops | bytes accessed | tf_op | source)
XLA Modules:
  0.0 158.2 jit_solution(3104739241617826503)
XLA Ops:
  0.0 2.4 %collective-permute-start.1 = (f32[1,96,9216]{2,1,0:T(8,128)}, f32[1,96,9216]{2,1,0:T(8,128)}, u32[]{:S(2)}, u32[]{:S(2)}) collective-permute-start(f32[1,96,9216]{2,1,0:T(8,128)} %param.4), channel_id=1, source_target_pairs={{3,14},{4,9},{12,1},{11,6},{19,30},{20,25},{28,17},{27,22}} | collective-permute-start | bytes 10616840 | tf_op jit(solution)/shard_map/ppermute | solution.py:409
  2.4 6.6 %collective-permute-start = (f32[1,96,9216]{2,1,0:T(8,128)}, f32[1,96,9216]{2,1,0:T(8,128)}, u32[]{:S(2)}, u32[]{:S(2)}) collective-permute-start(f32[1,96,9216]{2,1,0:T(8,128)} %param.4), channel_id=1, source_target_pairs={{8,14},{15,9},{9,11},{14,12},{7,1},{0,6},{6,4},{1,3},{24,30},{31,2... | collective-permute-start | bytes 10616840 | tf_op jit(solution)/shard_map/ppermute | solution.py:409
  9.0 1.2 dynamic-slice_bitcast_fusion.flags_ref.refs_0_
  10.3 0.1 broadcast_add_fusion
  10.3 4.5 %fusion.5.kernel_ref.refs_1_ = f32[96,96,128]{2,1,0:T(8,128)} fusion(f32[128]{0:T(128)S(1)} %fusion.12, f32[96,96]{1,0:T(8,128)S(1)} %broadcast_add_fusion, pred[128]{0:T(512)(128)(4,1)S(1)} %iota_compare_fusion), kind=kLoop, calls=%fused_computation.7 | loop fusion | flops 12976128 | bytes 4756096 | tf_op jit(solution)/shard_map/jit(_where)/select_n | solution.py:39
  14.8 5.2 %copied.1 = (f32[96,9216]{1,0:T(8,128)}, f32[96,9216]{1,0:T(8,128)}) custom-call(s32[11]{0:T(128)} %dynamic-slice_bitcast_fusion.flags_ref.refs_0_, f32[96,96,128]{2,1,0:T(8,128)} %fusion.5.kernel_ref.refs_1_, bf16[192,192]{1,0:T(8,128)(2,1)} %constant.37.clone.left_ref.refs_6_.refs_5_, bf16[256,256]{1,0:T(8,128)(2,1)} %constant.38.clone.right_ref.refs_7_.refs_6_, ...), custom_call_target="tpu_custom_call" | custom-call | tf_op jit(solution)/shard_map/copied/pallas_call | solution.py:289
  20.0 3.1 %collective-permute-start.2 = (f32[1,96,9216]{2,1,0:T(8,128)}, f32[1,96,9216]{2,1,0:T(8,128)}, u32[]{:S(2)}, u32[]{:S(2)}) collective-permute-start(f32[1,96,9216]{2,1,0:T(8,128)} %bitcast.33), channel_id=1, source_target_pairs={{15,10},{8,13},{0,5},{7,2},{31,26},{24,29},{16,21},{23,18}} | collective-permute-start | bytes 10616840 | tf_op jit(solution)/shard_map/ppermute | solution.py:409
  23.1 0.0 collective-permute-done.1
  23.1 0.7 fusion.9
  23.8 0.6 collective-permute-start.3
  24.5 22.0 %collective-permute-done = f32[1,96,9216]{2,1,0:T(8,128)} collective-permute-done((f32[1,96,9216]{2,1,0:T(8,128)}, f32[1,96,9216]{2,1,0:T(8,128)}, u32[]{:S(2)}, u32[]{:S(2)}) %collective-permute-start) | collective-permute-done | bytes 3538976 | tf_op jit(solution)/shard_map/ppermute | solution.py:409
  46.5 0.0 collective-permute-done.3
  46.5 0.0 copy-start
  46.5 0.6 copy-done
  47.1 2.4 %collective-permute-start.4 = (f32[1,96,9216]{2,1,0:T(8,128)}, f32[1,96,9216]{2,1,0:T(8,128)}, u32[]{:S(2)}, u32[]{:S(2)}) collective-permute-start(f32[1,96,9216]{2,1,0:T(8,128)} %bitcast.29), channel_id=1, source_target_pairs={{13,14},{10,9},{2,1},{5,6},{29,30},{26,25},{18,17},{21,22}} | collective-permute-start | bytes 10616840 | tf_op jit(solution)/shard_map/ppermute | solution.py:409
  49.5 2.5 %collective-permute-start.7 = (f32[1,96,9216]{2,1,0:T(8,128)}, f32[1,96,9216]{2,1,0:T(8,128)}, u32[]{:S(2)}, u32[]{:S(2)}) collective-permute-start(f32[1,96,9216]{2,1,0:T(8,128)} %bitcast.30), channel_id=1, source_target_pairs={{5,10},{2,13},{10,5},{13,2},{21,26},{18,29},{26,21},{29,18}} | collective-permute-start | bytes 10616840 | tf_op jit(solution)/shard_map/ppermute | solution.py:409
  52.0 32.5 %collective-permute-done.2 = f32[1,96,9216]{2,1,0:T(8,128)} collective-permute-done((f32[1,96,9216]{2,1,0:T(8,128)}, f32[1,96,9216]{2,1,0:T(8,128)}, u32[]{:S(2)}, u32[]{:S(2)}) %collective-permute-start.2) | collective-permute-done | bytes 3538976 | tf_op jit(solution)/shard_map/ppermute | solution.py:409
  84.4 2.1 %pair_terms.5 = (f32[96,9216]{1,0:T(8,128)}, f32[96,9216]{1,0:T(8,128)}, f32[96,9216]{1,0:T(8,128)}) custom-call(s32[11]{0:T(128)} %dynamic-slice_bitcast_fusion.flags_ref.refs_0_, f32[96,9216]{1,0:T(8,128)} %bitcast.1.refs_2_.refs_1_.refs_0_, f32[96,9216]{1,0:T(8,128)} %bitcast.25, f32[96,9216]{1,0:T(8,128)} %bitcast.3.refs_3_, ...), custom_call_target="tpu_custom_call" | custom-call | flops 100000000 | bytes 1000000 | tf_op jit(solution)/shard_map/pair_terms/pallas_call | solution.py:254
  86.6 2.5 %collective-permute-start.10 = (f32[1,96,9216]{2,1,0:T(8,128)}, f32[1,96,9216]{2,1,0:T(8,128)}, u32[]{:S(2)}, u32[]{:S(2)}) collective-permute-start(f32[1,96,9216]{2,1,0:T(8,128)} %bitcast.32), channel_id=1, source_target_pairs={{9,4},{14,3},{6,11},{1,12},{25,20},{30,19},{22,27},{17,28}} | collective-permute-start | bytes 10616840 | tf_op jit(solution)/shard_map/ppermute | solution.py:409
  89.1 2.4 %collective-permute-start.9 = (f32[1,96,9216]{2,1,0:T(8,128)}, f32[1,96,9216]{2,1,0:T(8,128)}, u32[]{:S(2)}, u32[]{:S(2)}) collective-permute-start(f32[1,96,9216]{2,1,0:T(8,128)} %bitcast.17), channel_id=1, source_target_pairs={{11,14},{12,9},{4,1},{3,6},{27,30},{28,25},{20,17},{19,22}} | collective-permute-start | bytes 10616840 | tf_op jit(solution)/shard_map/ppermute | solution.py:409
  91.5 0.0 collective-permute-done.4
  91.5 1.5 pair_terms.6
  93.0 1.7 %collective-permute-start.6 = (f32[1,32,9216]{2,1,0:T(8,128)}, f32[1,32,9216]{2,1,0:T(8,128)}, u32[]{:S(2)}, u32[]{:S(2)}) collective-permute-start(f32[1,32,9216]{2,1,0:T(8,128)} %bitcast.35), channel_id=1, source_target_pairs={{9,11},{14,12},{6,4},{1,3},{25,27},{30,28},{22,20},{17,19}} | collective-permute-start | bytes 3538952 | tf_op jit(solution)/shard_map/ppermute | solution.py:409
  94.8 1.5 collective-permute-start.5
  96.3 1.6 pair_terms.7.refs_3_
  97.8 0.0 collective-permute-done.7
  97.9 1.6 pair_terms.8.refs_1_
  99.4 0.0 collective-permute-done.6
  99.4 1.6 collective-permute-start.8
  101.0 0.0 collective-permute-done.10
  101.0 0.8 settle.2.refs_3_
  101.8 0.0 collective-permute-done.9
  101.8 1.6 pair_terms.9.refs_2_
  103.4 50.9 %collective-permute-done.8 = f32[1,32,9216]{2,1,0:T(8,128)} collective-permute-done((f32[1,32,9216]{2,1,0:T(8,128)}, f32[1,32,9216]{2,1,0:T(8,128)}, u32[]{:S(2)}, u32[]{:S(2)}) %collective-permute-start.8) | collective-permute-done | bytes 1179680 | tf_op jit(solution)/shard_map/ppermute | solution.py:409
  154.3 0.0 collective-permute-done.5
  154.3 3.7 %settle.3 = f32[96,9216]{1,0:T(8,128)} custom-call(s32[11]{0:T(128)} %dynamic-slice_bitcast_fusion.flags_ref.refs_0_, f32[64,9216]{1,0:T(8,128)} %bitcast.11.refs_0_, f32[32,9216]{1,0:T(8,128)} %bitcast.16.refs_1_, f32[96,9216]{1,0:T(8,128)} %pair_terms.9.refs_2_), custom_call_target="tpu_custom_call", output_to_operand_aliasing={{}: (3, {})} | custom-call | tf_op jit(solution)/shard_map/settle/pallas_call | solution.py:370
  (7 shorter events, 0.0 us)
Async XLA Ops:
  0.0 23.1 %collective-permute-start.1 = (f32[1,96,9216]{2,1,0:T(8,128)}, f32[1,96,9216]{2,1,0:T(8,128)}, u32[]{:S(2)}, u32[]{:S(2)}) collective-permute-start(f32[1,96,9216]{2,1,0:T(8,128)} %param.4), channel_id=1, source_target_pairs={{3,14},{4,9},{12,1},{11,6},{19,30},{20,25},{28,17},{27,22}} | collective-permute-start | bytes 10616840 | tf_op jit(solution)/shard_map/ppermute | solution.py:409
  2.4 44.1 %collective-permute-start = (f32[1,96,9216]{2,1,0:T(8,128)}, f32[1,96,9216]{2,1,0:T(8,128)}, u32[]{:S(2)}, u32[]{:S(2)}) collective-permute-start(f32[1,96,9216]{2,1,0:T(8,128)} %param.4), channel_id=1, source_target_pairs={{8,14},{15,9},{9,11},{14,12},{7,1},{0,6},{6,4},{1,3},{24,30},{31,2... | collective-permute-start | bytes 10616840 | tf_op jit(solution)/shard_map/ppermute | solution.py:409
  20.0 64.4 %collective-permute-start.2 = (f32[1,96,9216]{2,1,0:T(8,128)}, f32[1,96,9216]{2,1,0:T(8,128)}, u32[]{:S(2)}, u32[]{:S(2)}) collective-permute-start(f32[1,96,9216]{2,1,0:T(8,128)} %bitcast.33), channel_id=1, source_target_pairs={{15,10},{8,13},{0,5},{7,2},{31,26},{24,29},{16,21},{23,18}} | collective-permute-start | bytes 10616840 | tf_op jit(solution)/shard_map/ppermute | solution.py:409
  23.8 22.7 %collective-permute-start.3 = (f32[1,8,128]{2,1,0:T(8,128)S(1)}, f32[1,8,128]{2,1,0:T(8,128)S(1)}, u32[]{:S(2)}, u32[]{:S(2)}) collective-permute-start(f32[1,8,128]{2,1,0:T(8,128)S(1)} %fusion.9), channel_id=1, source_target_pairs={{14,2},{9,5},{1,13},{6,10},{30,18},{25,21},{17,29},{22,26}} | collective-permute-start | bytes 12296 | tf_op jit(solution)/shard_map/ppermute | solution.py:409
  46.5 0.6 copy-start
  47.1 44.4 %collective-permute-start.4 = (f32[1,96,9216]{2,1,0:T(8,128)}, f32[1,96,9216]{2,1,0:T(8,128)}, u32[]{:S(2)}, u32[]{:S(2)}) collective-permute-start(f32[1,96,9216]{2,1,0:T(8,128)} %bitcast.29), channel_id=1, source_target_pairs={{13,14},{10,9},{2,1},{5,6},{29,30},{26,25},{18,17},{21,22}} | collective-permute-start | bytes 10616840 | tf_op jit(solution)/shard_map/ppermute | solution.py:409
  49.5 48.3 %collective-permute-start.7 = (f32[1,96,9216]{2,1,0:T(8,128)}, f32[1,96,9216]{2,1,0:T(8,128)}, u32[]{:S(2)}, u32[]{:S(2)}) collective-permute-start(f32[1,96,9216]{2,1,0:T(8,128)} %bitcast.30), channel_id=1, source_target_pairs={{5,10},{2,13},{10,5},{13,2},{21,26},{18,29},{26,21},{29,18}} | collective-permute-start | bytes 10616840 | tf_op jit(solution)/shard_map/ppermute | solution.py:409
  86.6 14.4 %collective-permute-start.10 = (f32[1,96,9216]{2,1,0:T(8,128)}, f32[1,96,9216]{2,1,0:T(8,128)}, u32[]{:S(2)}, u32[]{:S(2)}) collective-permute-start(f32[1,96,9216]{2,1,0:T(8,128)} %bitcast.32), channel_id=1, source_target_pairs={{9,4},{14,3},{6,11},{1,12},{25,20},{30,19},{22,27},{17,28}} | collective-permute-start | bytes 10616840 | tf_op jit(solution)/shard_map/ppermute | solution.py:409
  89.1 12.7 %collective-permute-start.9 = (f32[1,96,9216]{2,1,0:T(8,128)}, f32[1,96,9216]{2,1,0:T(8,128)}, u32[]{:S(2)}, u32[]{:S(2)}) collective-permute-start(f32[1,96,9216]{2,1,0:T(8,128)} %bitcast.17), channel_id=1, source_target_pairs={{11,14},{12,9},{4,1},{3,6},{27,30},{28,25},{20,17},{19,22}} | collective-permute-start | bytes 10616840 | tf_op jit(solution)/shard_map/ppermute | solution.py:409
  93.0 6.4 %collective-permute-start.6 = (f32[1,32,9216]{2,1,0:T(8,128)}, f32[1,32,9216]{2,1,0:T(8,128)}, u32[]{:S(2)}, u32[]{:S(2)}) collective-permute-start(f32[1,32,9216]{2,1,0:T(8,128)} %bitcast.35), channel_id=1, source_target_pairs={{9,11},{14,12},{6,4},{1,3},{25,27},{30,28},{22,20},{17,19}} | collective-permute-start | bytes 3538952 | tf_op jit(solution)/shard_map/ppermute | solution.py:409
  94.8 59.5 %collective-permute-start.5 = (f32[1,64,9216]{2,1,0:T(8,128)}, f32[1,64,9216]{2,1,0:T(8,128)}, u32[]{:S(2)}, u32[]{:S(2)}) collective-permute-start(f32[1,64,9216]{2,1,0:T(8,128)} %bitcast.34), channel_id=1, source_target_pairs={{9,15},{14,8},{6,0},{1,7},{25,31},{30,24},{22,16},{17,23}} | collective-permute-start | bytes 7077896 | tf_op jit(solution)/shard_map/ppermute | solution.py:409
  99.4 54.8 %collective-permute-start.8 = (f32[1,32,9216]{2,1,0:T(8,128)}, f32[1,32,9216]{2,1,0:T(8,128)}, u32[]{:S(2)}, u32[]{:S(2)}) collective-permute-start(f32[1,32,9216]{2,1,0:T(8,128)} %bitcast.15), channel_id=1, source_target_pairs={{11,15},{12,8},{4,0},{3,7},{27,31},{28,24},{20,16},{19,23}} | collective-permute-start | bytes 3538952 | tf_op jit(solution)/shard_map/ppermute | solution.py:409

commit v11 on v10

--- a/solution.py
+++ b/solution.py
@@ -13,7 +13,7 @@
 screening = 5.44
 LANES = 128
 X_STEPS = 3
-SETTLE_STEPS = 6
+SETTLE_ROWS = 8
 FAR_ROWS = 32
 
 
@@ -340,21 +340,21 @@
 
 def settle_body(wanted, count, flags_ref, *refs):
     parts, (out_ref, near, sems) = refs[:count], refs[count + 1:]
-    columns = out_ref.shape[1] // SETTLE_STEPS
 
     @pl.when(flags_ref[RESULT] == wanted)
     def move():
         copies = []
-        for i in range(SETTLE_STEPS):
-            span = pl.ds(i * columns, columns)
-            start = 0
-            for j, part in enumerate(parts):
-                rows = pl.ds(start, part.shape[0])
-                start += part.shape[0]
+        start = 0
+        for part in parts:
+            for row in range(0, part.shape[0], SETTLE_ROWS):
+                rows = pl.ds(start + row, SETTLE_ROWS)
+                place = (start + row) // SETTLE_ROWS
+                source = part.at[pl.ds(row, SETTLE_ROWS), :]
                 copies.append((
-                    pltpu.make_async_copy(part.at[:, span], near.at[rows, span], sems.at[0, j, i]),
-                    pltpu.make_async_copy(near.at[rows, span], out_ref.at[rows, span], sems.at[1, j, i]),
+                    pltpu.make_async_copy(source, near.at[rows, :], sems.at[0, place]),
+                    pltpu.make_async_copy(near.at[rows, :], out_ref.at[rows, :], sems.at[1, place]),
                 ))
+            start += part.shape[0]
         for inward, outward in copies:
             inward.start()
         for inward, outward in copies:
@@ -375,7 +375,7 @@
         input_output_aliases={count + 1: 0},
         scratch_shapes=[
             pltpu.VMEM(own_sum.shape, own_sum.dtype),
-            pltpu.SemaphoreType.DMA((2, count, SETTLE_STEPS)),
+            pltpu.SemaphoreType.DMA((2, own_sum.shape[0] // SETTLE_ROWS)),
         ],
         compiler_params=pltpu.CompilerParams(vmem_limit_bytes=63 * 2**20),
         name="settle",

time: 159 us -> 159 us (level)
  no operation moved by 1% of the time
where the time goes in v11:
time: 159 us; the launch traced here: 158 us
  waiting for transfers between devices  105 us (66%)
  starting transfers between devices  27.3 us (17%)
  Pallas kernels  18.2 us (11%)
  other arithmetic  5.27 us (3%)
  local copies, waits for them, and re-layouts  1.82 us (1%)
    ppermute x11, waiting for transfers between devices, send(): return lax.ppermute(value[None], 'band', pairs)[0]  105 us
    ppermute x11, starting transfers between devices, send(): return lax.ppermute(value[None], 'band', pairs)[0]  27.3 us
    pallas_call x5, Pallas kernels, pair_terms(): pl.pallas_call(functools.partial(pair_body, points, slot, jobs, plane_ste...  8.35 us
    pallas_call x1, Pallas kernels, copied(): pl.pallas_call(copy_body, grid=(X_STEPS,), in_specs=[pl.BlockSpec(memory_...  5.23 us
    pallas_call x2, Pallas kernels, settle(): pl.pallas_call(functools.partial(settle_body, wanted, count), in_specs=[p...  4.67 us
    select_n x1, other arithmetic, screened_kernel(): return jnp.where(inside, kernel / -float(points * points * points), 0.0)  4.49 us
  transfers between devices with their start and end apart: 11, of which 3 were waited for; matrix products, arithmetic and copies ran while one was open for 4% of the time, Pallas kernels for 9%

profile of v11, /device:TPU:0, one launch (start us, length us, event | category | flops | bytes accessed | tf_op | source)
XLA Modules:
  0.0 158.2 jit_solution(11381012554407069863)
XLA Ops:
  0.0 2.4 %collective-permute-start.1 = (f32[1,96,9216]{2,1,0:T(8,128)}, f32[1,96,9216]{2,1,0:T(8,128)}, u32[]{:S(2)}, u32[]{:S(2)}) collective-permute-start(f32[1,96,9216]{2,1,0:T(8,128)} %param.4), channel_id=1, source_target_pairs={{3,14},{4,9},{12,1},{11,6},{19,30},{20,25},{28,17},{27,22}} | collective-permute-start | bytes 10616840 | tf_op jit(solution)/shard_map/ppermute | solution.py:409
  2.4 6.6 %collective-permute-start = (f32[1,96,9216]{2,1,0:T(8,128)}, f32[1,96,9216]{2,1,0:T(8,128)}, u32[]{:S(2)}, u32[]{:S(2)}) collective-permute-start(f32[1,96,9216]{2,1,0:T(8,128)} %param.4), channel_id=1, source_target_pairs={{8,14},{15,9},{9,11},{14,12},{7,1},{0,6},{6,4},{1,3},{24,30},{31,2... | collective-permute-start | bytes 10616840 | tf_op jit(solution)/shard_map/ppermute | solution.py:409
  9.0 1.2 dynamic-slice_bitcast_fusion.flags_ref.refs_0_
  10.3 0.1 broadcast_add_fusion
  10.3 4.5 %fusion.5.kernel_ref.refs_1_ = f32[96,96,128]{2,1,0:T(8,128)} fusion(f32[128]{0:T(128)S(1)} %fusion.12, f32[96,96]{1,0:T(8,128)S(1)} %broadcast_add_fusion, pred[128]{0:T(512)(128)(4,1)S(1)} %iota_compare_fusion), kind=kLoop, calls=%fused_computation.7 | loop fusion | flops 12976128 | bytes 4756096 | tf_op jit(solution)/shard_map/jit(_where)/select_n | solution.py:39
  14.8 5.2 %copied.1 = (f32[96,9216]{1,0:T(8,128)}, f32[96,9216]{1,0:T(8,128)}) custom-call(s32[11]{0:T(128)} %dynamic-slice_bitcast_fusion.flags_ref.refs_0_, f32[96,96,128]{2,1,0:T(8,128)} %fusion.5.kernel_ref.refs_1_, bf16[192,192]{1,0:T(8,128)(2,1)} %constant.37.clone.left_ref.refs_6_.refs_5_, bf16[256,256]{1,0:T(8,128)(2,1)} %constant.38.clone.right_ref.refs_7_.refs_6_, ...), custom_call_target="tpu_custom_call" | custom-call | tf_op jit(solution)/shard_map/copied/pallas_call | solution.py:289
  20.0 3.1 %collective-permute-start.2 = (f32[1,96,9216]{2,1,0:T(8,128)}, f32[1,96,9216]{2,1,0:T(8,128)}, u32[]{:S(2)}, u32[]{:S(2)}) collective-permute-start(f32[1,96,9216]{2,1,0:T(8,128)} %bitcast.33), channel_id=1, source_target_pairs={{15,10},{8,13},{0,5},{7,2},{31,26},{24,29},{16,21},{23,18}} | collective-permute-start | bytes 10616840 | tf_op jit(solution)/shard_map/ppermute | solution.py:409
  23.1 0.0 collective-permute-done.1
  23.1 0.7 fusion.9
  23.8 0.6 collective-permute-start.3
  24.5 22.0 %collective-permute-done = f32[1,96,9216]{2,1,0:T(8,128)} collective-permute-done((f32[1,96,9216]{2,1,0:T(8,128)}, f32[1,96,9216]{2,1,0:T(8,128)}, u32[]{:S(2)}, u32[]{:S(2)}) %collective-permute-start) | collective-permute-done | bytes 3538976 | tf_op jit(solution)/shard_map/ppermute | solution.py:409
  46.5 0.0 collective-permute-done.3
  46.5 0.0 copy-start
  46.5 0.6 copy-done
  47.1 2.4 %collective-permute-start.4 = (f32[1,96,9216]{2,1,0:T(8,128)}, f32[1,96,9216]{2,1,0:T(8,128)}, u32[]{:S(2)}, u32[]{:S(2)}) collective-permute-start(f32[1,96,9216]{2,1,0:T(8,128)} %bitcast.29), channel_id=1, source_target_pairs={{13,14},{10,9},{2,1},{5,6},{29,30},{26,25},{18,17},{21,22}} | collective-permute-start | bytes 10616840 | tf_op jit(solution)/shard_map/ppermute | solution.py:409
  49.5 2.5 %collective-permute-start.7 = (f32[1,96,9216]{2,1,0:T(8,128)}, f32[1,96,9216]{2,1,0:T(8,128)}, u32[]{:S(2)}, u32[]{:S(2)}) collective-permute-start(f32[1,96,9216]{2,1,0:T(8,128)} %bitcast.30), channel_id=1, source_target_pairs={{5,10},{2,13},{10,5},{13,2},{21,26},{18,29},{26,21},{29,18}} | collective-permute-start | bytes 10616840 | tf_op jit(solution)/shard_map/ppermute | solution.py:409
  52.0 32.5 %collective-permute-done.2 = f32[1,96,9216]{2,1,0:T(8,128)} collective-permute-done((f32[1,96,9216]{2,1,0:T(8,128)}, f32[1,96,9216]{2,1,0:T(8,128)}, u32[]{:S(2)}, u32[]{:S(2)}) %collective-permute-start.2) | collective-permute-done | bytes 3538976 | tf_op jit(solution)/shard_map/ppermute | solution.py:409
  84.4 2.1 %pair_terms.5 = (f32[96,9216]{1,0:T(8,128)}, f32[96,9216]{1,0:T(8,128)}, f32[96,9216]{1,0:T(8,128)}) custom-call(s32[11]{0:T(128)} %dynamic-slice_bitcast_fusion.flags_ref.refs_0_, f32[96,9216]{1,0:T(8,128)} %bitcast.1.refs_2_.refs_1_.refs_0_, f32[96,9216]{1,0:T(8,128)} %bitcast.25, f32[96,9216]{1,0:T(8,128)} %bitcast.3.refs_3_, ...), custom_call_target="tpu_custom_call" | custom-call | flops 100000000 | bytes 1000000 | tf_op jit(solution)/shard_map/pair_terms/pallas_call | solution.py:254
  86.6 2.5 %collective-permute-start.10 = (f32[1,96,9216]{2,1,0:T(8,128)}, f32[1,96,9216]{2,1,0:T(8,128)}, u32[]{:S(2)}, u32[]{:S(2)}) collective-permute-start(f32[1,96,9216]{2,1,0:T(8,128)} %bitcast.32), channel_id=1, source_target_pairs={{9,4},{14,3},{6,11},{1,12},{25,20},{30,19},{22,27},{17,28}} | collective-permute-start | bytes 10616840 | tf_op jit(solution)/shard_map/ppermute | solution.py:409
  89.1 2.4 %collective-permute-start.9 = (f32[1,96,9216]{2,1,0:T(8,128)}, f32[1,96,9216]{2,1,0:T(8,128)}, u32[]{:S(2)}, u32[]{:S(2)}) collective-permute-start(f32[1,96,9216]{2,1,0:T(8,128)} %bitcast.17), channel_id=1, source_target_pairs={{11,14},{12,9},{4,1},{3,6},{27,30},{28,25},{20,17},{19,22}} | collective-permute-start | bytes 10616840 | tf_op jit(solution)/shard_map/ppermute | solution.py:409
  91.5 0.0 collective-permute-done.4
  91.5 1.5 pair_terms.6
  93.0 1.7 %collective-permute-start.6 = (f32[1,32,9216]{2,1,0:T(8,128)}, f32[1,32,9216]{2,1,0:T(8,128)}, u32[]{:S(2)}, u32[]{:S(2)}) collective-permute-start(f32[1,32,9216]{2,1,0:T(8,128)} %bitcast.35), channel_id=1, source_target_pairs={{9,11},{14,12},{6,4},{1,3},{25,27},{30,28},{22,20},{17,19}} | collective-permute-start | bytes 3538952 | tf_op jit(solution)/shard_map/ppermute | solution.py:409
  94.8 1.5 collective-permute-start.5
  96.3 1.6 pair_terms.7.refs_3_
  97.8 0.0 collective-permute-done.7
  97.9 1.6 pair_terms.8.refs_1_
  99.4 0.0 collective-permute-done.6
  99.4 1.6 collective-permute-start.8
  101.0 0.0 collective-permute-done.10
  101.0 0.9 settle.2.refs_3_
  101.9 0.0 collective-permute-done.9
  102.0 1.6 pair_terms.9.refs_2_
  103.5 50.7 %collective-permute-done.8 = f32[1,32,9216]{2,1,0:T(8,128)} collective-permute-done((f32[1,32,9216]{2,1,0:T(8,128)}, f32[1,32,9216]{2,1,0:T(8,128)}, u32[]{:S(2)}, u32[]{:S(2)}) %collective-permute-start.8) | collective-permute-done | bytes 1179680 | tf_op jit(solution)/shard_map/ppermute | solution.py:409
  154.3 0.0 collective-permute-done.5
  154.3 3.7 %settle.3 = f32[96,9216]{1,0:T(8,128)} custom-call(s32[11]{0:T(128)} %dynamic-slice_bitcast_fusion.flags_ref.refs_0_, f32[64,9216]{1,0:T(8,128)} %bitcast.11.refs_0_, f32[32,9216]{1,0:T(8,128)} %bitcast.16.refs_1_, f32[96,9216]{1,0:T(8,128)} %pair_terms.9.refs_2_), custom_call_target="tpu_custom_call", output_to_operand_aliasing={{}: (3, {})} | custom-call | tf_op jit(solution)/shard_map/settle/pallas_call | solution.py:370
  (7 shorter events, 0.0 us)
Async XLA Ops:
  0.0 23.1 %collective-permute-start.1 = (f32[1,96,9216]{2,1,0:T(8,128)}, f32[1,96,9216]{2,1,0:T(8,128)}, u32[]{:S(2)}, u32[]{:S(2)}) collective-permute-start(f32[1,96,9216]{2,1,0:T(8,128)} %param.4), channel_id=1, source_target_pairs={{3,14},{4,9},{12,1},{11,6},{19,30},{20,25},{28,17},{27,22}} | collective-permute-start | bytes 10616840 | tf_op jit(solution)/shard_map/ppermute | solution.py:409
  2.4 44.1 %collective-permute-start = (f32[1,96,9216]{2,1,0:T(8,128)}, f32[1,96,9216]{2,1,0:T(8,128)}, u32[]{:S(2)}, u32[]{:S(2)}) collective-permute-start(f32[1,96,9216]{2,1,0:T(8,128)} %param.4), channel_id=1, source_target_pairs={{8,14},{15,9},{9,11},{14,12},{7,1},{0,6},{6,4},{1,3},{24,30},{31,2... | collective-permute-start | bytes 10616840 | tf_op jit(solution)/shard_map/ppermute | solution.py:409
  20.0 64.4 %collective-permute-start.2 = (f32[1,96,9216]{2,1,0:T(8,128)}, f32[1,96,9216]{2,1,0:T(8,128)}, u32[]{:S(2)}, u32[]{:S(2)}) collective-permute-start(f32[1,96,9216]{2,1,0:T(8,128)} %bitcast.33), channel_id=1, source_target_pairs={{15,10},{8,13},{0,5},{7,2},{31,26},{24,29},{16,21},{23,18}} | collective-permute-start | bytes 10616840 | tf_op jit(solution)/shard_map/ppermute | solution.py:409
  23.8 22.7 %collective-permute-start.3 = (f32[1,8,128]{2,1,0:T(8,128)S(1)}, f32[1,8,128]{2,1,0:T(8,128)S(1)}, u32[]{:S(2)}, u32[]{:S(2)}) collective-permute-start(f32[1,8,128]{2,1,0:T(8,128)S(1)} %fusion.9), channel_id=1, source_target_pairs={{14,2},{9,5},{1,13},{6,10},{30,18},{25,21},{17,29},{22,26}} | collective-permute-start | bytes 12296 | tf_op jit(solution)/shard_map/ppermute | solution.py:409
  46.5 0.6 copy-start
  47.1 44.4 %collective-permute-start.4 = (f32[1,96,9216]{2,1,0:T(8,128)}, f32[1,96,9216]{2,1,0:T(8,128)}, u32[]{:S(2)}, u32[]{:S(2)}) collective-permute-start(f32[1,96,9216]{2,1,0:T(8,128)} %bitcast.29), channel_id=1, source_target_pairs={{13,14},{10,9},{2,1},{5,6},{29,30},{26,25},{18,17},{21,22}} | collective-permute-start | bytes 10616840 | tf_op jit(solution)/shard_map/ppermute | solution.py:409
  49.5 48.3 %collective-permute-start.7 = (f32[1,96,9216]{2,1,0:T(8,128)}, f32[1,96,9216]{2,1,0:T(8,128)}, u32[]{:S(2)}, u32[]{:S(2)}) collective-permute-start(f32[1,96,9216]{2,1,0:T(8,128)} %bitcast.30), channel_id=1, source_target_pairs={{5,10},{2,13},{10,5},{13,2},{21,26},{18,29},{26,21},{29,18}} | collective-permute-start | bytes 10616840 | tf_op jit(solution)/shard_map/ppermute | solution.py:409
  86.6 14.4 %collective-permute-start.10 = (f32[1,96,9216]{2,1,0:T(8,128)}, f32[1,96,9216]{2,1,0:T(8,128)}, u32[]{:S(2)}, u32[]{:S(2)}) collective-permute-start(f32[1,96,9216]{2,1,0:T(8,128)} %bitcast.32), channel_id=1, source_target_pairs={{9,4},{14,3},{6,11},{1,12},{25,20},{30,19},{22,27},{17,28}} | collective-permute-start | bytes 10616840 | tf_op jit(solution)/shard_map/ppermute | solution.py:409
  89.1 12.9 %collective-permute-start.9 = (f32[1,96,9216]{2,1,0:T(8,128)}, f32[1,96,9216]{2,1,0:T(8,128)}, u32[]{:S(2)}, u32[]{:S(2)}) collective-permute-start(f32[1,96,9216]{2,1,0:T(8,128)} %bitcast.17), channel_id=1, source_target_pairs={{11,14},{12,9},{4,1},{3,6},{27,30},{28,25},{20,17},{19,22}} | collective-permute-start | bytes 10616840 | tf_op jit(solution)/shard_map/ppermute | solution.py:409
  93.0 6.4 %collective-permute-start.6 = (f32[1,32,9216]{2,1,0:T(8,128)}, f32[1,32,9216]{2,1,0:T(8,128)}, u32[]{:S(2)}, u32[]{:S(2)}) collective-permute-start(f32[1,32,9216]{2,1,0:T(8,128)} %bitcast.35), channel_id=1, source_target_pairs={{9,11},{14,12},{6,4},{1,3},{25,27},{30,28},{22,20},{17,19}} | collective-permute-start | bytes 3538952 | tf_op jit(solution)/shard_map/ppermute | solution.py:409
  94.8 59.5 %collective-permute-start.5 = (f32[1,64,9216]{2,1,0:T(8,128)}, f32[1,64,9216]{2,1,0:T(8,128)}, u32[]{:S(2)}, u32[]{:S(2)}) collective-permute-start(f32[1,64,9216]{2,1,0:T(8,128)} %bitcast.34), channel_id=1, source_target_pairs={{9,15},{14,8},{6,0},{1,7},{25,31},{30,24},{22,16},{17,23}} | collective-permute-start | bytes 7077896 | tf_op jit(solution)/shard_map/ppermute | solution.py:409
  99.4 54.8 %collective-permute-start.8 = (f32[1,32,9216]{2,1,0:T(8,128)}, f32[1,32,9216]{2,1,0:T(8,128)}, u32[]{:S(2)}, u32[]{:S(2)}) collective-permute-start(f32[1,32,9216]{2,1,0:T(8,128)} %bitcast.15), channel_id=1, source_target_pairs={{11,15},{12,8},{4,0},{3,7},{27,31},{28,24},{20,16},{19,23}} | collective-permute-start | bytes 3538952 | tf_op jit(solution)/shard_map/ppermute | solution.py:409

commit v12 on v10

--- a/solution.py
+++ b/solution.py
@@ -416,7 +416,7 @@
     crossed = send(own, CROSSING)
     partner = send(own, PARTNERS)
     own_copy, direct_copy = copied(flags, constants, own)
-    token = crossed[:8, :LANES] + own_copy[:8, :LANES]
+    token = hold(own_copy[:8, :LANES], crossed)
     direct = send(direct_copy, DIRECT)
     kernel, held_back = gate(send(token, ARRIVED), kernel, partner, own_copy)
     constants = (kernel, left, right)

time: 159 us -> 158 us (level)
  no operation moved by 1% of the time
where the time goes in v12:
time: 158 us
  waiting for transfers between devices  104 us (66%)
  starting transfers between devices  27.4 us (17%)
  Pallas kernels  18.1 us (11%)
  other arithmetic  4.59 us (3%)
  local copies, waits for them, and re-layouts  3.1 us (2%)
    ppermute x11, waiting for transfers between devices, send(): return lax.ppermute(value[None], 'band', pairs)[0]  104 us
    ppermute x11, starting transfers between devices, send(): return lax.ppermute(value[None], 'band', pairs)[0]  27.4 us
    pallas_call x5, Pallas kernels, pair_terms(): pl.pallas_call(functools.partial(pair_body, points, slot, jobs, plane_ste...  8.35 us
    pallas_call x1, Pallas kernels, copied(): pl.pallas_call(copy_body, grid=(X_STEPS,), in_specs=[pl.BlockSpec(memory_...  5.23 us
    pallas_call x2, Pallas kernels, settle(): pl.pallas_call(functools.partial(settle_body, wanted, count), in_specs=[p...  4.53 us
    select_n x1, other arithmetic, screened_kernel(): return jnp.where(inside, kernel / -float(points * points * points), 0.0)  4.49 us
  transfers between devices with their start and end apart: 11, of which 3 were waited for; matrix products, arithmetic and copies ran while one was open for 4% of the time, Pallas kernels for 9%

profile of v12, /device:TPU:0, one launch (start us, length us, event | category | flops | bytes accessed | tf_op | source)
XLA Modules:
  0.0 157.7 jit_solution(14555115521455627715)
XLA Ops:
  0.0 2.5 %collective-permute-start.1 = (f32[1,96,9216]{2,1,0:T(8,128)}, f32[1,96,9216]{2,1,0:T(8,128)}, u32[]{:S(2)}, u32[]{:S(2)}) collective-permute-start(f32[1,96,9216]{2,1,0:T(8,128)} %param.4), channel_id=1, source_target_pairs={{3,14},{4,9},{12,1},{11,6},{19,30},{20,25},{28,17},{27,22}} | collective-permute-start | bytes 10616840 | tf_op jit(solution)/shard_map/ppermute | solution.py:409
  2.5 6.5 %collective-permute-start = (f32[1,96,9216]{2,1,0:T(8,128)}, f32[1,96,9216]{2,1,0:T(8,128)}, u32[]{:S(2)}, u32[]{:S(2)}) collective-permute-start(f32[1,96,9216]{2,1,0:T(8,128)} %param.4), channel_id=1, source_target_pairs={{8,14},{15,9},{9,11},{14,12},{7,1},{0,6},{6,4},{1,3},{24,30},{31,2... | collective-permute-start | bytes 10616840 | tf_op jit(solution)/shard_map/ppermute | solution.py:409
  9.0 1.2 dynamic-slice_bitcast_fusion.flags_ref.refs_0_
  10.3 0.1 broadcast_add_fusion
  10.3 4.5 %fusion.5.kernel_ref.refs_1_ = f32[96,96,128]{2,1,0:T(8,128)} fusion(f32[128]{0:T(128)S(1)} %fusion.11, f32[96,96]{1,0:T(8,128)S(1)} %broadcast_add_fusion, pred[128]{0:T(512)(128)(4,1)S(1)} %iota_compare_fusion), kind=kLoop, calls=%fused_computation.7 | loop fusion | flops 12976128 | bytes 4756096 | tf_op jit(solution)/shard_map/jit(_where)/select_n | solution.py:39
  14.8 5.2 %copied.1 = (f32[96,9216]{1,0:T(8,128)}, f32[96,9216]{1,0:T(8,128)}) custom-call(s32[11]{0:T(128)} %dynamic-slice_bitcast_fusion.flags_ref.refs_0_, f32[96,96,128]{2,1,0:T(8,128)} %fusion.5.kernel_ref.refs_1_, bf16[192,192]{1,0:T(8,128)(2,1)} %constant.37.clone.left_ref.refs_6_.refs_5_, bf16[256,256]{1,0:T(8,128)(2,1)} %constant.38.clone.right_ref.refs_7_.refs_6_, ...), custom_call_target="tpu_custom_call" | custom-call | tf_op jit(solution)/shard_map/copied/pallas_call | solution.py:289
  20.0 3.1 %collective-permute-start.2 = (f32[1,96,9216]{2,1,0:T(8,128)}, f32[1,96,9216]{2,1,0:T(8,128)}, u32[]{:S(2)}, u32[]{:S(2)}) collective-permute-start(f32[1,96,9216]{2,1,0:T(8,128)} %bitcast.33), channel_id=1, source_target_pairs={{15,10},{8,13},{0,5},{7,2},{31,26},{24,29},{16,21},{23,18}} | collective-permute-start | bytes 10616840 | tf_op jit(solution)/shard_map/ppermute | solution.py:409
  23.1 1.3 slice.10.refs_0_
  24.4 0.0 collective-permute-done.1
  24.4 0.7 collective-permute-start.3
  25.1 21.4 %collective-permute-done = f32[1,96,9216]{2,1,0:T(8,128)} collective-permute-done((f32[1,96,9216]{2,1,0:T(8,128)}, f32[1,96,9216]{2,1,0:T(8,128)}, u32[]{:S(2)}, u32[]{:S(2)}) %collective-permute-start) | collective-permute-done | bytes 3538976 | tf_op jit(solution)/shard_map/ppermute | solution.py:409
  46.5 0.0 collective-permute-done.3
  46.5 0.0 copy-start
  46.5 0.6 copy-done
  47.1 2.4 %collective-permute-start.4 = (f32[1,96,9216]{2,1,0:T(8,128)}, f32[1,96,9216]{2,1,0:T(8,128)}, u32[]{:S(2)}, u32[]{:S(2)}) collective-permute-start(f32[1,96,9216]{2,1,0:T(8,128)} %bitcast.28), channel_id=1, source_target_pairs={{13,14},{10,9},{2,1},{5,6},{29,30},{26,25},{18,17},{21,22}} | collective-permute-start | bytes 10616840 | tf_op jit(solution)/shard_map/ppermute | solution.py:409
  49.5 2.5 %collective-permute-start.7 = (f32[1,96,9216]{2,1,0:T(8,128)}, f32[1,96,9216]{2,1,0:T(8,128)}, u32[]{:S(2)}, u32[]{:S(2)}) collective-permute-start(f32[1,96,9216]{2,1,0:T(8,128)} %bitcast.29), channel_id=1, source_target_pairs={{5,10},{2,13},{10,5},{13,2},{21,26},{18,29},{26,21},{29,18}} | collective-permute-start | bytes 10616840 | tf_op jit(solution)/shard_map/ppermute | solution.py:409
  52.0 32.5 %collective-permute-done.2 = f32[1,96,9216]{2,1,0:T(8,128)} collective-permute-done((f32[1,96,9216]{2,1,0:T(8,128)}, f32[1,96,9216]{2,1,0:T(8,128)}, u32[]{:S(2)}, u32[]{:S(2)}) %collective-permute-start.2) | collective-permute-done | bytes 3538976 | tf_op jit(solution)/shard_map/ppermute | solution.py:409
  84.4 2.1 %pair_terms.5 = (f32[96,9216]{1,0:T(8,128)}, f32[96,9216]{1,0:T(8,128)}, f32[96,9216]{1,0:T(8,128)}) custom-call(s32[11]{0:T(128)} %dynamic-slice_bitcast_fusion.flags_ref.refs_0_, f32[96,9216]{1,0:T(8,128)} %bitcast.1.refs_2_.refs_1_.refs_0_, f32[96,9216]{1,0:T(8,128)} %bitcast.24, f32[96,9216]{1,0:T(8,128)} %bitcast.3.refs_1_.refs_3_, ...), custom_call_target="tpu_custom_call" | custom-call | flops 100000000 | bytes 1000000 | tf_op jit(solution)/shard_map/pair_terms/pallas_call | solution.py:254
  86.6 2.5 %collective-permute-start.10 = (f32[1,96,9216]{2,1,0:T(8,128)}, f32[1,96,9216]{2,1,0:T(8,128)}, u32[]{:S(2)}, u32[]{:S(2)}) collective-permute-start(f32[1,96,9216]{2,1,0:T(8,128)} %bitcast.32), channel_id=1, source_target_pairs={{9,4},{14,3},{6,11},{1,12},{25,20},{30,19},{22,27},{17,28}} | collective-permute-start | bytes 10616840 | tf_op jit(solution)/shard_map/ppermute | solution.py:409
  89.1 2.5 %collective-permute-start.9 = (f32[1,96,9216]{2,1,0:T(8,128)}, f32[1,96,9216]{2,1,0:T(8,128)}, u32[]{:S(2)}, u32[]{:S(2)}) collective-permute-start(f32[1,96,9216]{2,1,0:T(8,128)} %bitcast.17), channel_id=1, source_target_pairs={{11,14},{12,9},{4,1},{3,6},{27,30},{28,25},{20,17},{19,22}} | collective-permute-start | bytes 10616840 | tf_op jit(solution)/shard_map/ppermute | solution.py:409
  91.6 0.0 collective-permute-done.4
  91.6 1.5 pair_terms.6
  93.1 1.7 %collective-permute-start.6 = (f32[1,32,9216]{2,1,0:T(8,128)}, f32[1,32,9216]{2,1,0:T(8,128)}, u32[]{:S(2)}, u32[]{:S(2)}) collective-permute-start(f32[1,32,9216]{2,1,0:T(8,128)} %bitcast.35), channel_id=1, source_target_pairs={{9,11},{14,12},{6,4},{1,3},{25,27},{30,28},{22,20},{17,19}} | collective-permute-start | bytes 3538952 | tf_op jit(solution)/shard_map/ppermute | solution.py:409
  94.8 1.5 collective-permute-start.5
  96.3 1.6 pair_terms.7.refs_3_
  97.9 0.0 collective-permute-done.7
  97.9 1.6 pair_terms.8.refs_1_
  99.5 0.0 collective-permute-done.6
  99.5 1.6 collective-permute-start.8
  101.0 0.0 collective-permute-done.10
  101.1 0.8 settle.2.refs_3_
  101.9 0.0 collective-permute-done.9
  101.9 1.6 pair_terms.9.refs_2_
  103.4 50.4 %collective-permute-done.8 = f32[1,32,9216]{2,1,0:T(8,128)} collective-permute-done((f32[1,32,9216]{2,1,0:T(8,128)}, f32[1,32,9216]{2,1,0:T(8,128)}, u32[]{:S(2)}, u32[]{:S(2)}) %collective-permute-start.8) | collective-permute-done | bytes 1179680 | tf_op jit(solution)/shard_map/ppermute | solution.py:409
  153.8 0.0 collective-permute-done.5
  153.8 3.7 %settle.3 = f32[96,9216]{1,0:T(8,128)} custom-call(s32[11]{0:T(128)} %dynamic-slice_bitcast_fusion.flags_ref.refs_0_, f32[64,9216]{1,0:T(8,128)} %bitcast.11.refs_0_, f32[32,9216]{1,0:T(8,128)} %bitcast.16.refs_1_, f32[96,9216]{1,0:T(8,128)} %pair_terms.9.refs_2_), custom_call_target="tpu_custom_call", output_to_operand_aliasing={{}: (3, {})} | custom-call | tf_op jit(solution)/shard_map/settle/pallas_call | solution.py:370
  (8 shorter events, 0.0 us)
Async XLA Ops:
  0.0 24.4 %collective-permute-start.1 = (f32[1,96,9216]{2,1,0:T(8,128)}, f32[1,96,9216]{2,1,0:T(8,128)}, u32[]{:S(2)}, u32[]{:S(2)}) collective-permute-start(f32[1,96,9216]{2,1,0:T(8,128)} %param.4), channel_id=1, source_target_pairs={{3,14},{4,9},{12,1},{11,6},{19,30},{20,25},{28,17},{27,22}} | collective-permute-start | bytes 10616840 | tf_op jit(solution)/shard_map/ppermute | solution.py:409
  2.5 44.0 %collective-permute-start = (f32[1,96,9216]{2,1,0:T(8,128)}, f32[1,96,9216]{2,1,0:T(8,128)}, u32[]{:S(2)}, u32[]{:S(2)}) collective-permute-start(f32[1,96,9216]{2,1,0:T(8,128)} %param.4), channel_id=1, source_target_pairs={{8,14},{15,9},{9,11},{14,12},{7,1},{0,6},{6,4},{1,3},{24,30},{31,2... | collective-permute-start | bytes 10616840 | tf_op jit(solution)/shard_map/ppermute | solution.py:409
  20.0 64.4 %collective-permute-start.2 = (f32[1,96,9216]{2,1,0:T(8,128)}, f32[1,96,9216]{2,1,0:T(8,128)}, u32[]{:S(2)}, u32[]{:S(2)}) collective-permute-start(f32[1,96,9216]{2,1,0:T(8,128)} %bitcast.33), channel_id=1, source_target_pairs={{15,10},{8,13},{0,5},{7,2},{31,26},{24,29},{16,21},{23,18}} | collective-permute-start | bytes 10616840 | tf_op jit(solution)/shard_map/ppermute | solution.py:409
  24.4 22.1 %collective-permute-start.3 = (f32[1,8,128]{2,1,0:T(8,128)}, f32[1,8,128]{2,1,0:T(8,128)S(1)}, u32[]{:S(2)}, u32[]{:S(2)}) collective-permute-start(f32[1,8,128]{2,1,0:T(8,128)} %bitcast.30), channel_id=1, source_target_pairs={{14,2},{9,5},{1,13},{6,10},{30,18},{25,21},{17,29},{22,26}} | collective-permute-start | bytes 12296 | tf_op jit(solution)/shard_map/ppermute | solution.py:409
  46.5 0.6 copy-start
  47.1 44.5 %collective-permute-start.4 = (f32[1,96,9216]{2,1,0:T(8,128)}, f32[1,96,9216]{2,1,0:T(8,128)}, u32[]{:S(2)}, u32[]{:S(2)}) collective-permute-start(f32[1,96,9216]{2,1,0:T(8,128)} %bitcast.28), channel_id=1, source_target_pairs={{13,14},{10,9},{2,1},{5,6},{29,30},{26,25},{18,17},{21,22}} | collective-permute-start | bytes 10616840 | tf_op jit(solution)/shard_map/ppermute | solution.py:409
  49.5 48.4 %collective-permute-start.7 = (f32[1,96,9216]{2,1,0:T(8,128)}, f32[1,96,9216]{2,1,0:T(8,128)}, u32[]{:S(2)}, u32[]{:S(2)}) collective-permute-start(f32[1,96,9216]{2,1,0:T(8,128)} %bitcast.29), channel_id=1, source_target_pairs={{5,10},{2,13},{10,5},{13,2},{21,26},{18,29},{26,21},{29,18}} | collective-permute-start | bytes 10616840 | tf_op jit(solution)/shard_map/ppermute | solution.py:409
  86.6 14.4 %collective-permute-start.10 = (f32[1,96,9216]{2,1,0:T(8,128)}, f32[1,96,9216]{2,1,0:T(8,128)}, u32[]{:S(2)}, u32[]{:S(2)}) collective-permute-start(f32[1,96,9216]{2,1,0:T(8,128)} %bitcast.32), channel_id=1, source_target_pairs={{9,4},{14,3},{6,11},{1,12},{25,20},{30,19},{22,27},{17,28}} | collective-permute-start | bytes 10616840 | tf_op jit(solution)/shard_map/ppermute | solution.py:409
  89.1 12.8 %collective-permute-start.9 = (f32[1,96,9216]{2,1,0:T(8,128)}, f32[1,96,9216]{2,1,0:T(8,128)}, u32[]{:S(2)}, u32[]{:S(2)}) collective-permute-start(f32[1,96,9216]{2,1,0:T(8,128)} %bitcast.17), channel_id=1, source_target_pairs={{11,14},{12,9},{4,1},{3,6},{27,30},{28,25},{20,17},{19,22}} | collective-permute-start | bytes 10616840 | tf_op jit(solution)/shard_map/ppermute | solution.py:409
  93.1 6.4 %collective-permute-start.6 = (f32[1,32,9216]{2,1,0:T(8,128)}, f32[1,32,9216]{2,1,0:T(8,128)}, u32[]{:S(2)}, u32[]{:S(2)}) collective-permute-start(f32[1,32,9216]{2,1,0:T(8,128)} %bitcast.35), channel_id=1, source_target_pairs={{9,11},{14,12},{6,4},{1,3},{25,27},{30,28},{22,20},{17,19}} | collective-permute-start | bytes 3538952 | tf_op jit(solution)/shard_map/ppermute | solution.py:409
  94.8 59.0 %collective-permute-start.5 = (f32[1,64,9216]{2,1,0:T(8,128)}, f32[1,64,9216]{2,1,0:T(8,128)}, u32[]{:S(2)}, u32[]{:S(2)}) collective-permute-start(f32[1,64,9216]{2,1,0:T(8,128)} %bitcast.34), channel_id=1, source_target_pairs={{9,15},{14,8},{6,0},{1,7},{25,31},{30,24},{22,16},{17,23}} | collective-permute-start | bytes 7077896 | tf_op jit(solution)/shard_map/ppermute | solution.py:409
  99.5 54.3 %collective-permute-start.8 = (f32[1,32,9216]{2,1,0:T(8,128)}, f32[1,32,9216]{2,1,0:T(8,128)}, u32[]{:S(2)}, u32[]{:S(2)}) collective-permute-start(f32[1,32,9216]{2,1,0:T(8,128)} %bitcast.15), channel_id=1, source_target_pairs={{11,15},{12,8},{4,0},{3,7},{27,31},{28,24},{20,16},{19,23}} | collective-permute-start | bytes 3538952 | tf_op jit(solution)/shard_map/ppermute | solution.py:409

commit v13 on v12

--- a/solution.py
+++ b/solution.py
@@ -436,7 +436,7 @@
     (own_sum,) = pair(3, [own], single, constants, sum_a=own_sum, in_place=True)
     bottom = send(hold(bottom, own_sum), HOME_TURNED)
     own_sum = settle(flags, 1, [home], own_sum)
-    (own_sum,) = pair(4, [own], turned, constants, sum_a=own_sum, in_place=True)
+    (own_sum,) = pair(4, [own], turned, constants, sum_a=own_sum, in_place=True, plane_steps=1)
     return settle(flags, 2, [top, bottom], own_sum)[None]
 
 

time: 158 us -> 158 us (level)
  no operation moved by 1% of the time
where the time goes in v13:
time: 158 us
  waiting for transfers between devices  104 us (66%)
  starting transfers between devices  27.4 us (17%)
  Pallas kernels  18 us (11%)
  other arithmetic  4.59 us (3%)
  local copies, waits for them, and re-layouts  3.1 us (2%)
    ppermute x11, waiting for transfers between devices, send(): return lax.ppermute(value[None], 'band', pairs)[0]  104 us
    ppermute x11, starting transfers between devices, send(): return lax.ppermute(value[None], 'band', pairs)[0]  27.4 us
    pallas_call x5, Pallas kernels, pair_terms(): pl.pallas_call(functools.partial(pair_body, points, slot, jobs, plane_ste...  8.28 us
    pallas_call x1, Pallas kernels, copied(): pl.pallas_call(copy_body, grid=(X_STEPS,), in_specs=[pl.BlockSpec(memory_...  5.23 us
    pallas_call x2, Pallas kernels, settle(): pl.pallas_call(functools.partial(settle_body, wanted, count), in_specs=[p...  4.53 us
    select_n x1, other arithmetic, screened_kernel(): return jnp.where(inside, kernel / -float(points * points * points), 0.0)  4.49 us
  transfers between devices with their start and end apart: 11, of which 3 were waited for; matrix products, arithmetic and copies ran while one was open for 4% of the time, Pallas kernels for 9%

profile of v13, /device:TPU:0, one launch (start us, length us, event | category | flops | bytes accessed | tf_op | source)
XLA Modules:
  0.0 157.7 jit_solution(17984484885981607679)
XLA Ops:
  0.0 2.5 %collective-permute-start.1 = (f32[1,96,9216]{2,1,0:T(8,128)}, f32[1,96,9216]{2,1,0:T(8,128)}, u32[]{:S(2)}, u32[]{:S(2)}) collective-permute-start(f32[1,96,9216]{2,1,0:T(8,128)} %param.4), channel_id=1, source_target_pairs={{3,14},{4,9},{12,1},{11,6},{19,30},{20,25},{28,17},{27,22}} | collective-permute-start | bytes 10616840 | tf_op jit(solution)/shard_map/ppermute | solution.py:409
  2.5 6.5 %collective-permute-start = (f32[1,96,9216]{2,1,0:T(8,128)}, f32[1,96,9216]{2,1,0:T(8,128)}, u32[]{:S(2)}, u32[]{:S(2)}) collective-permute-start(f32[1,96,9216]{2,1,0:T(8,128)} %param.4), channel_id=1, source_target_pairs={{8,14},{15,9},{9,11},{14,12},{7,1},{0,6},{6,4},{1,3},{24,30},{31,2... | collective-permute-start | bytes 10616840 | tf_op jit(solution)/shard_map/ppermute | solution.py:409
  9.0 1.2 dynamic-slice_bitcast_fusion.flags_ref.refs_0_
  10.3 0.1 broadcast_add_fusion
  10.3 4.5 %fusion.5.kernel_ref.refs_1_ = f32[96,96,128]{2,1,0:T(8,128)} fusion(f32[128]{0:T(128)S(1)} %fusion.11, f32[96,96]{1,0:T(8,128)S(1)} %broadcast_add_fusion, pred[128]{0:T(512)(128)(4,1)S(1)} %iota_compare_fusion), kind=kLoop, calls=%fused_computation.7 | loop fusion | flops 12976128 | bytes 4756096 | tf_op jit(solution)/shard_map/jit(_where)/select_n | solution.py:39
  14.8 5.2 %copied.1 = (f32[96,9216]{1,0:T(8,128)}, f32[96,9216]{1,0:T(8,128)}) custom-call(s32[11]{0:T(128)} %dynamic-slice_bitcast_fusion.flags_ref.refs_0_, f32[96,96,128]{2,1,0:T(8,128)} %fusion.5.kernel_ref.refs_1_, bf16[192,192]{1,0:T(8,128)(2,1)} %constant.37.clone.left_ref.refs_6_.refs_5_, bf16[256,256]{1,0:T(8,128)(2,1)} %constant.38.clone.right_ref.refs_7_.refs_6_, ...), custom_call_target="tpu_custom_call" | custom-call | tf_op jit(solution)/shard_map/copied/pallas_call | solution.py:289
  20.0 3.1 %collective-permute-start.2 = (f32[1,96,9216]{2,1,0:T(8,128)}, f32[1,96,9216]{2,1,0:T(8,128)}, u32[]{:S(2)}, u32[]{:S(2)}) collective-permute-start(f32[1,96,9216]{2,1,0:T(8,128)} %bitcast.33), channel_id=1, source_target_pairs={{15,10},{8,13},{0,5},{7,2},{31,26},{24,29},{16,21},{23,18}} | collective-permute-start | bytes 10616840 | tf_op jit(solution)/shard_map/ppermute | solution.py:409
  23.1 1.3 slice.10.refs_0_
  24.4 0.0 collective-permute-done.1
  24.4 0.7 collective-permute-start.3
  25.1 21.4 %collective-permute-done = f32[1,96,9216]{2,1,0:T(8,128)} collective-permute-done((f32[1,96,9216]{2,1,0:T(8,128)}, f32[1,96,9216]{2,1,0:T(8,128)}, u32[]{:S(2)}, u32[]{:S(2)}) %collective-permute-start) | collective-permute-done | bytes 3538976 | tf_op jit(solution)/shard_map/ppermute | solution.py:409
  46.5 0.0 collective-permute-done.3
  46.5 0.0 copy-start
  46.5 0.6 copy-done
  47.1 2.4 %collective-permute-start.4 = (f32[1,96,9216]{2,1,0:T(8,128)}, f32[1,96,9216]{2,1,0:T(8,128)}, u32[]{:S(2)}, u32[]{:S(2)}) collective-permute-start(f32[1,96,9216]{2,1,0:T(8,128)} %bitcast.28), channel_id=1, source_target_pairs={{13,14},{10,9},{2,1},{5,6},{29,30},{26,25},{18,17},{21,22}} | collective-permute-start | bytes 10616840 | tf_op jit(solution)/shard_map/ppermute | solution.py:409
  49.5 2.5 %collective-permute-start.7 = (f32[1,96,9216]{2,1,0:T(8,128)}, f32[1,96,9216]{2,1,0:T(8,128)}, u32[]{:S(2)}, u32[]{:S(2)}) collective-permute-start(f32[1,96,9216]{2,1,0:T(8,128)} %bitcast.29), channel_id=1, source_target_pairs={{5,10},{2,13},{10,5},{13,2},{21,26},{18,29},{26,21},{29,18}} | collective-permute-start | bytes 10616840 | tf_op jit(solution)/shard_map/ppermute | solution.py:409
  52.0 32.5 %collective-permute-done.2 = f32[1,96,9216]{2,1,0:T(8,128)} collective-permute-done((f32[1,96,9216]{2,1,0:T(8,128)}, f32[1,96,9216]{2,1,0:T(8,128)}, u32[]{:S(2)}, u32[]{:S(2)}) %collective-permute-start.2) | collective-permute-done | bytes 3538976 | tf_op jit(solution)/shard_map/ppermute | solution.py:409
  84.4 2.1 %pair_terms.5 = (f32[96,9216]{1,0:T(8,128)}, f32[96,9216]{1,0:T(8,128)}, f32[96,9216]{1,0:T(8,128)}) custom-call(s32[11]{0:T(128)} %dynamic-slice_bitcast_fusion.flags_ref.refs_0_, f32[96,9216]{1,0:T(8,128)} %bitcast.1.refs_2_.refs_1_.refs_0_, f32[96,9216]{1,0:T(8,128)} %bitcast.24, f32[96,9216]{1,0:T(8,128)} %bitcast.3.refs_1_.refs_3_, ...), custom_call_target="tpu_custom_call" | custom-call | flops 100000000 | bytes 1000000 | tf_op jit(solution)/shard_map/pair_terms/pallas_call | solution.py:254
  86.6 2.5 %collective-permute-start.10 = (f32[1,96,9216]{2,1,0:T(8,128)}, f32[1,96,9216]{2,1,0:T(8,128)}, u32[]{:S(2)}, u32[]{:S(2)}) collective-permute-start(f32[1,96,9216]{2,1,0:T(8,128)} %bitcast.32), channel_id=1, source_target_pairs={{9,4},{14,3},{6,11},{1,12},{25,20},{30,19},{22,27},{17,28}} | collective-permute-start | bytes 10616840 | tf_op jit(solution)/shard_map/ppermute | solution.py:409
  89.1 2.5 %collective-permute-start.9 = (f32[1,96,9216]{2,1,0:T(8,128)}, f32[1,96,9216]{2,1,0:T(8,128)}, u32[]{:S(2)}, u32[]{:S(2)}) collective-permute-start(f32[1,96,9216]{2,1,0:T(8,128)} %bitcast.17), channel_id=1, source_target_pairs={{11,14},{12,9},{4,1},{3,6},{27,30},{28,25},{20,17},{19,22}} | collective-permute-start | bytes 10616840 | tf_op jit(solution)/shard_map/ppermute | solution.py:409
  91.6 0.0 collective-permute-done.4
  91.6 1.5 pair_terms.6
  93.1 1.7 %collective-permute-start.6 = (f32[1,32,9216]{2,1,0:T(8,128)}, f32[1,32,9216]{2,1,0:T(8,128)}, u32[]{:S(2)}, u32[]{:S(2)}) collective-permute-start(f32[1,32,9216]{2,1,0:T(8,128)} %bitcast.35), channel_id=1, source_target_pairs={{9,11},{14,12},{6,4},{1,3},{25,27},{30,28},{22,20},{17,19}} | collective-permute-start | bytes 3538952 | tf_op jit(solution)/shard_map/ppermute | solution.py:409
  94.8 1.5 collective-permute-start.5
  96.3 1.6 pair_terms.7.refs_3_
  97.9 0.0 collective-permute-done.7
  97.9 1.6 pair_terms.8.refs_1_
  99.5 0.0 collective-permute-done.6
  99.5 1.6 collective-permute-start.8
  101.0 0.0 collective-permute-done.10
  101.1 0.8 settle.2.refs_3_
  101.9 0.0 collective-permute-done.9
  101.9 1.5 pair_terms.9.refs_2_
  103.4 50.4 %collective-permute-done.8 = f32[1,32,9216]{2,1,0:T(8,128)} collective-permute-done((f32[1,32,9216]{2,1,0:T(8,128)}, f32[1,32,9216]{2,1,0:T(8,128)}, u32[]{:S(2)}, u32[]{:S(2)}) %collective-permute-start.8) | collective-permute-done | bytes 1179680 | tf_op jit(solution)/shard_map/ppermute | solution.py:409
  153.8 0.0 collective-permute-done.5
  153.8 3.7 %settle.3 = f32[96,9216]{1,0:T(8,128)} custom-call(s32[11]{0:T(128)} %dynamic-slice_bitcast_fusion.flags_ref.refs_0_, f32[64,9216]{1,0:T(8,128)} %bitcast.11.refs_0_, f32[32,9216]{1,0:T(8,128)} %bitcast.16.refs_1_, f32[96,9216]{1,0:T(8,128)} %pair_terms.9.refs_2_), custom_call_target="tpu_custom_call", output_to_operand_aliasing={{}: (3, {})} | custom-call | tf_op jit(solution)/shard_map/settle/pallas_call | solution.py:370
  (8 shorter events, 0.0 us)
Async XLA Ops:
  0.0 24.4 %collective-permute-start.1 = (f32[1,96,9216]{2,1,0:T(8,128)}, f32[1,96,9216]{2,1,0:T(8,128)}, u32[]{:S(2)}, u32[]{:S(2)}) collective-permute-start(f32[1,96,9216]{2,1,0:T(8,128)} %param.4), channel_id=1, source_target_pairs={{3,14},{4,9},{12,1},{11,6},{19,30},{20,25},{28,17},{27,22}} | collective-permute-start | bytes 10616840 | tf_op jit(solution)/shard_map/ppermute | solution.py:409
  2.5 44.0 %collective-permute-start = (f32[1,96,9216]{2,1,0:T(8,128)}, f32[1,96,9216]{2,1,0:T(8,128)}, u32[]{:S(2)}, u32[]{:S(2)}) collective-permute-start(f32[1,96,9216]{2,1,0:T(8,128)} %param.4), channel_id=1, source_target_pairs={{8,14},{15,9},{9,11},{14,12},{7,1},{0,6},{6,4},{1,3},{24,30},{31,2... | collective-permute-start | bytes 10616840 | tf_op jit(solution)/shard_map/ppermute | solution.py:409
  20.0 64.4 %collective-permute-start.2 = (f32[1,96,9216]{2,1,0:T(8,128)}, f32[1,96,9216]{2,1,0:T(8,128)}, u32[]{:S(2)}, u32[]{:S(2)}) collective-permute-start(f32[1,96,9216]{2,1,0:T(8,128)} %bitcast.33), channel_id=1, source_target_pairs={{15,10},{8,13},{0,5},{7,2},{31,26},{24,29},{16,21},{23,18}} | collective-permute-start | bytes 10616840 | tf_op jit(solution)/shard_map/ppermute | solution.py:409
  24.4 22.1 %collective-permute-start.3 = (f32[1,8,128]{2,1,0:T(8,128)}, f32[1,8,128]{2,1,0:T(8,128)S(1)}, u32[]{:S(2)}, u32[]{:S(2)}) collective-permute-start(f32[1,8,128]{2,1,0:T(8,128)} %bitcast.30), channel_id=1, source_target_pairs={{14,2},{9,5},{1,13},{6,10},{30,18},{25,21},{17,29},{22,26}} | collective-permute-start | bytes 12296 | tf_op jit(solution)/shard_map/ppermute | solution.py:409
  46.5 0.6 copy-start
  47.1 44.5 %collective-permute-start.4 = (f32[1,96,9216]{2,1,0:T(8,128)}, f32[1,96,9216]{2,1,0:T(8,128)}, u32[]{:S(2)}, u32[]{:S(2)}) collective-permute-start(f32[1,96,9216]{2,1,0:T(8,128)} %bitcast.28), channel_id=1, source_target_pairs={{13,14},{10,9},{2,1},{5,6},{29,30},{26,25},{18,17},{21,22}} | collective-permute-start | bytes 10616840 | tf_op jit(solution)/shard_map/ppermute | solution.py:409
  49.5 48.4 %collective-permute-start.7 = (f32[1,96,9216]{2,1,0:T(8,128)}, f32[1,96,9216]{2,1,0:T(8,128)}, u32[]{:S(2)}, u32[]{:S(2)}) collective-permute-start(f32[1,96,9216]{2,1,0:T(8,128)} %bitcast.29), channel_id=1, source_target_pairs={{5,10},{2,13},{10,5},{13,2},{21,26},{18,29},{26,21},{29,18}} | collective-permute-start | bytes 10616840 | tf_op jit(solution)/shard_map/ppermute | solution.py:409
  86.6 14.4 %collective-permute-start.10 = (f32[1,96,9216]{2,1,0:T(8,128)}, f32[1,96,9216]{2,1,0:T(8,128)}, u32[]{:S(2)}, u32[]{:S(2)}) collective-permute-start(f32[1,96,9216]{2,1,0:T(8,128)} %bitcast.32), channel_id=1, source_target_pairs={{9,4},{14,3},{6,11},{1,12},{25,20},{30,19},{22,27},{17,28}} | collective-permute-start | bytes 10616840 | tf_op jit(solution)/shard_map/ppermute | solution.py:409
  89.1 12.8 %collective-permute-start.9 = (f32[1,96,9216]{2,1,0:T(8,128)}, f32[1,96,9216]{2,1,0:T(8,128)}, u32[]{:S(2)}, u32[]{:S(2)}) collective-permute-start(f32[1,96,9216]{2,1,0:T(8,128)} %bitcast.17), channel_id=1, source_target_pairs={{11,14},{12,9},{4,1},{3,6},{27,30},{28,25},{20,17},{19,22}} | collective-permute-start | bytes 10616840 | tf_op jit(solution)/shard_map/ppermute | solution.py:409
  93.1 6.4 %collective-permute-start.6 = (f32[1,32,9216]{2,1,0:T(8,128)}, f32[1,32,9216]{2,1,0:T(8,128)}, u32[]{:S(2)}, u32[]{:S(2)}) collective-permute-start(f32[1,32,9216]{2,1,0:T(8,128)} %bitcast.35), channel_id=1, source_target_pairs={{9,11},{14,12},{6,4},{1,3},{25,27},{30,28},{22,20},{17,19}} | collective-permute-start | bytes 3538952 | tf_op jit(solution)/shard_map/ppermute | solution.py:409
  94.8 59.0 %collective-permute-start.5 = (f32[1,64,9216]{2,1,0:T(8,128)}, f32[1,64,9216]{2,1,0:T(8,128)}, u32[]{:S(2)}, u32[]{:S(2)}) collective-permute-start(f32[1,64,9216]{2,1,0:T(8,128)} %bitcast.34), channel_id=1, source_target_pairs={{9,15},{14,8},{6,0},{1,7},{25,31},{30,24},{22,16},{17,23}} | collective-permute-start | bytes 7077896 | tf_op jit(solution)/shard_map/ppermute | solution.py:409
  99.5 54.3 %collective-permute-start.8 = (f32[1,32,9216]{2,1,0:T(8,128)}, f32[1,32,9216]{2,1,0:T(8,128)}, u32[]{:S(2)}, u32[]{:S(2)}) collective-permute-start(f32[1,32,9216]{2,1,0:T(8,128)} %bitcast.15), channel_id=1, source_target_pairs={{11,15},{12,8},{4,0},{3,7},{27,31},{28,24},{20,16},{19,23}} | collective-permute-start | bytes 3538952 | tf_op jit(solution)/shard_map/ppermute | solution.py:409
